TPU v7x, 32 devices: a whole 2x2x4 slice. The times are simulated.
32 devices in a mesh: dp: 8 (over z, y), head: 4 (over x, core).
Axes of the slice: x: 2, y: 2, z: 4, core: 2. Of those that a mesh axis runs over, the one named last changes fastest.
Arguments:
- features: bfloat16 [32768, 768], P('dp'), may hold values from -6 to 6
- laplacian: float32 [8192, 16], P('dp'), may hold values from -4 to 4
- endpoints: int32 [32768, 2], P('dp'), may hold values from 0 to 31
- lengths: int32 [16, 16], P('dp'), may hold values from 1 to 128, 1536 in all within a row
- pairing: int32 [8, 16], P('dp'), may hold values from 0 to 15, each once within a row
- ident_weight: float32 [32, 768], P(None, ('dp', 'head')), may hold values from -1 to 1
- qkv_weight: float32 [768, 3, 768], P('dp', None, 'head'), may hold values from -0.21875 to 0.21875
- out_weight: float32 [768, 768], P('head', 'dp'), may hold values from -1.75 to 1.75
- ffn_weight: float32 [2, 768, 768], P(None, ('dp', 'head')), may hold values from -0.21875 to 0.21875
- norm_gains: float32 [3, 768], P(None, ('dp', 'head')), may hold values from 0.5 to 1.5
- ident_first: float32 [32, 768], P(None, ('dp', 'head')), may hold values from -0.015625 to 0.015625
- qkv_first: float32 [768, 3, 768], P('dp', None, 'head'), may hold values from -0.015625 to 0.015625
- out_first: float32 [768, 768], P('head', 'dp'), may hold values from -0.015625 to 0.015625
- ffn_first: float32 [2, 768, 768], P(None, ('dp', 'head')), may hold values from -0.015625 to 0.015625
- gains_first: float32 [3, 768], P(None, ('dp', 'head')), may hold values from -0.0625 to 0.0625
- ident_second: float32 [32, 768], P(None, ('dp', 'head')), may hold values from 7.0110023e-06 to 2.8044009e-05
- qkv_second: float32 [768, 3, 768], P('dp', None, 'head'), may hold values from 7.0110023e-06 to 2.8044009e-05
- out_second: float32 [768, 768], P('head', 'dp'), may hold values from 7.0110023e-06 to 2.8044009e-05
- ffn_second: float32 [2, 768, 768], P(None, ('dp', 'head')), may hold values from 7.0110023e-06 to 2.8044009e-05
- gains_second: float32 [3, 768], P(None, ('dp', 'head')), may hold values from 0.000112176036 to 0.00044870414
Outputs:
- grad_norm: float32 [], replicated
- total_loss: float32 [], replicated
- new_ident: float32 [32, 768], P(None, ('dp', 'head'))
- new_qkv: float32 [768, 3, 768], P('dp', None, 'head')
- new_out: float32 [768, 768], P('head', 'dp')
- new_ffn: float32 [2, 768, 768], P(None, ('dp', 'head'))
- new_gains: float32 [3, 768], P(None, ('dp', 'head'))
- first_ident: float32 [32, 768], P(None, ('dp', 'head'))
- first_qkv: float32 [768, 3, 768], P('dp', None, 'head')
- first_out: float32 [768, 768], P('head', 'dp')
- first_ffn: float32 [2, 768, 768], P(None, ('dp', 'head'))
- first_gains: float32 [3, 768], P(None, ('dp', 'head'))
- second_ident: float32 [32, 768], P(None, ('dp', 'head'))
- second_qkv: float32 [768, 3, 768], P('dp', None, 'head')
- second_out: float32 [768, 768], P('head', 'dp')
- second_ffn: float32 [2, 768, 768], P(None, ('dp', 'head'))
- second_gains: float32 [3, 768], P(None, ('dp', 'head'))
All inputs are finite; a program needn't handle non-finite values.
Results may differ from a plain program's by a relative error of at most 0.0099.
Values may be sent and summed in bfloat16 or wider, within the bound.
No kernel may reach another device: no remote copies, remote signals or barrier semaphores. Data moves between devices by JAX's collectives and lax.ppermute only.
A program may use at most 192 MiB of HBM per device.

v0:
```python
import jax
import jax.numpy as jnp
from jax import lax
from jax.sharding import PartitionSpec as P

D = 768
HEAD_DIM = 24
LAP = 16
LEN = 128
NODE = 32
STEPS = 3
GRAPHS_DEV = 16


HIGHEST = lax.Precision.HIGHEST
NORM_EPS = 1e-05
CLIP_AT = 5.0
STEP_RATES = (0.08, 0.02, 0.15, 0.02, 0.5)
BETA_ONE = 0.5
BETA_TWO = 0.5
DECAY = 0.01
ADAM_EPS = 1e-08
MASKED = -1e30


def layer_norm(values, gain):
    centred = values - jnp.mean(values, axis=-1, keepdims=True)
    spread = jnp.mean(centred * centred, axis=-1, keepdims=True)
    return centred * lax.rsqrt(spread + NORM_EPS) * gain


def gelu_exact(values):
    return jax.nn.gelu(values, approximate=False)


def log_total(values, axis):
    top = jnp.max(values, axis=axis, keepdims=True)
    return jnp.squeeze(top, axis) + jnp.log(jnp.sum(jnp.exp(values - top), axis=axis))


def identifiers(table, endpoints):
    graphs = endpoints.shape[0] // LEN
    nodes = table.reshape(graphs, NODE, LAP)
    picks = (
        endpoints.reshape(graphs, LEN, 2)[..., None] == jnp.arange(NODE, dtype=jnp.int32)
    ).astype(jnp.float32)
    found = jnp.einsum("glan,gnc->glac", picks, nodes, precision=HIGHEST)
    return found.reshape(graphs * LEN, 2 * LAP)


def split_parts(projected, live):
    graphs = live.shape[0]
    parts = projected.reshape(graphs, LEN, 3, -1, HEAD_DIM)
    return (parts[:, :, 0], parts[:, :, 1], parts[:, :, 2])


def masked_scores(query, keys, live):
    scores = jnp.einsum(
        "gqhe,gkhe->ghqk", query, keys, preferred_element_type=jnp.float32
    ) * HEAD_DIM ** (-0.5)
    return jnp.where(live[:, None, None, :], scores, MASKED)


def attend(projected, live):
    query, keys, values = split_parts(projected, live)
    scores = masked_scores(query, keys, live)
    top = jnp.max(scores, axis=-1, keepdims=True)
    expo = jnp.exp(scores - top)
    totals = jnp.sum(expo, axis=-1, keepdims=True)
    probs = (expo / totals).astype(jnp.bfloat16)
    heads_out = jnp.einsum(
        "ghqk,gkhe->gqhe", probs, values, preferred_element_type=jnp.float32
    ).astype(jnp.bfloat16)
    return (heads_out.reshape(projected.shape[0], -1), top + jnp.log(totals))


def attend_back(projected, live, log_totals, d_heads):
    query, keys, values = split_parts(projected, live)
    probs = jnp.exp(masked_scores(query, keys, live) - log_totals)
    d_out = d_heads.reshape(query.shape)
    d_probs = jnp.einsum("gqhe,gkhe->ghqk", d_out, values, preferred_element_type=jnp.float32)
    d_scores = (probs * (d_probs - jnp.sum(probs * d_probs, axis=-1, keepdims=True))).astype(
        jnp.bfloat16
    )
    scale = HEAD_DIM ** (-0.5)
    d_query = (
        jnp.einsum("ghqk,gkhe->gqhe", d_scores, keys, preferred_element_type=jnp.float32) * scale
    )
    d_keys = (
        jnp.einsum("ghqk,gqhe->gkhe", d_scores, query, preferred_element_type=jnp.float32) * scale
    )
    d_values = jnp.einsum(
        "ghqk,gqhe->gkhe", probs.astype(jnp.bfloat16), d_out, preferred_element_type=jnp.float32
    )
    stacked = jnp.stack([d_query, d_keys, d_values], axis=2)
    return stacked.reshape(projected.shape[0], 3, -1).astype(jnp.bfloat16)


def contract_rows(left, right):
    return lax.dot_general(
        left, right, (((0,), (0,)), ((), ())), preferred_element_type=jnp.float32
    )


def contract_last(left, right):
    return lax.dot_general(
        left, right, (((1,), (1,)), ((), ())), preferred_element_type=jnp.float32
    )


def adam_step(weight, gradient, first, second, factor, rate):
    clipped = gradient * factor
    first_new = BETA_ONE * first + (1.0 - BETA_ONE) * clipped
    second_new = BETA_TWO * second + (1.0 - BETA_TWO) * clipped * clipped
    first_hat = first_new / (1.0 - BETA_ONE**STEPS)
    second_hat = second_new / (1.0 - BETA_TWO**STEPS)
    weight_new = weight - rate * (first_hat / (jnp.sqrt(second_hat) + ADAM_EPS) + DECAY * weight)
    return (weight_new, first_new, second_new)


def per_device(
    features,
    laplacian,
    endpoints,
    lengths,
    pairing,
    ident_weight,
    qkv_weight,
    out_weight,
    ffn_weight,
    norm_gains,
    ident_first,
    qkv_first,
    out_first,
    ffn_first,
    gains_first,
    ident_second,
    qkv_second,
    out_second,
    ffn_second,
    gains_second,
):
    head_count = lax.axis_size("head")
    head_place = lax.axis_index("head")
    group_place = lax.axis_index("dp")
    token_count = features.shape[0]
    own_rows = token_count // head_count
    own_graphs = own_rows // LEN
    ident_full, gain_full = (
        lax.all_gather(ident_weight, ("dp", "head"), axis=1, tiled=True),
        lax.all_gather(norm_gains, ("dp", "head"), axis=1, tiled=True),
    )
    ffn_full = lax.all_gather(ffn_weight.astype(jnp.bfloat16), ("dp", "head"), axis=1, tiled=True)
    qkv_local, out_local = (
        lax.all_gather(qkv_weight.astype(jnp.bfloat16), "dp", axis=0, tiled=True),
        lax.all_gather(out_weight.astype(jnp.bfloat16), "dp", axis=1, tiled=True),
    )
    qkv_use, out_use = (
        lax.all_gather(qkv_local, "head", axis=2, tiled=True),
        lax.all_gather(out_local, "head", axis=0, tiled=True),
    )
    start_row = head_place * own_rows
    graph_start = start_row // LEN
    graph_count = own_rows // LEN
    lens_all = lengths.reshape(-1)
    live_all = jnp.arange(LEN, dtype=jnp.int32)[None, :] < lens_all[:, None]
    live_rows = lax.dynamic_slice_in_dim(live_all, graph_start, graph_count, 0)
    table_rows = lax.dynamic_slice_in_dim(laplacian, graph_start * NODE, graph_count * NODE, 0)
    end_rows = lax.dynamic_slice_in_dim(endpoints, start_row, own_rows, 0)
    ident_rows = identifiers(table_rows, end_rows).astype(jnp.bfloat16)
    embedded = lax.dynamic_slice_in_dim(features, start_row, own_rows, 0).astype(jnp.float32)
    embedded = embedded + jnp.dot(
        ident_rows, ident_full.astype(jnp.bfloat16), preferred_element_type=jnp.float32
    )
    normed_one = layer_norm(embedded, gain_full[0]).astype(jnp.bfloat16)
    projected = jnp.einsum(
        "td,dcf->tcf", normed_one, qkv_use, preferred_element_type=jnp.float32
    ).astype(jnp.bfloat16)
    heads_out, log_totals = attend(projected, live_rows)
    partial_value = jnp.dot(heads_out, out_use, preferred_element_type=jnp.float32)
    middle = embedded + partial_value
    normed_two, norm_two_back = jax.vjp(layer_norm, middle, gain_full[1])
    normed_two = normed_two.astype(jnp.bfloat16)
    up_pre = jnp.dot(normed_two, ffn_full[0], preferred_element_type=jnp.float32)
    hidden, gelu_back = jax.vjp(gelu_exact, up_pre)
    hidden = hidden.astype(jnp.bfloat16)
    output_rows = middle + contract_last(hidden, ffn_full[1])
    own_lens = lax.dynamic_slice_in_dim(lens_all, head_place * own_graphs, own_graphs, 0).astype(
        jnp.float32
    )
    own_live = lax.dynamic_slice_in_dim(live_all, head_place * own_graphs, own_graphs, 0).astype(
        jnp.float32
    )
    pooled = (
        jnp.sum(output_rows.reshape(own_graphs, LEN, -1) * own_live[:, :, None], axis=1)
        / own_lens[:, None]
    )
    summary, final_back = jax.vjp(layer_norm, pooled, gain_full[2])
    gathered = lax.all_gather(summary, ("dp", "head"), axis=0, tiled=True)
    by_view = gathered.reshape(-1, 2, GRAPHS_DEV, D)
    left_side = by_view[:, 0].reshape(-1, D)
    right_side = by_view[:, 1].reshape(-1, D)
    root_width = D**0.5
    logits = jnp.dot(left_side, right_side.T, precision=HIGHEST) / root_width
    row_totals = log_total(logits, 1)
    col_totals = log_total(logits, 0)
    weights_both = jnp.exp(logits - row_totals[:, None]) + jnp.exp(logits - col_totals[None, :])
    grad_left = jnp.dot(weights_both, right_side, precision=HIGHEST) / root_width
    grad_right = jnp.dot(weights_both.T, left_side, precision=HIGHEST) / root_width
    pair_row = pairing.reshape(-1)
    slots = jnp.arange(GRAPHS_DEV, dtype=jnp.int32)
    inverse = jnp.sum(
        slots[:, None] * (pair_row[:, None] == slots[None, :]).astype(jnp.int32), axis=0
    )
    own_index = head_place * own_graphs + jnp.arange(own_graphs, dtype=jnp.int32)
    first_view = own_index < GRAPHS_DEV
    graph_slot = own_index % GRAPHS_DEV
    global_id = group_place * GRAPHS_DEV + graph_slot
    partner_right = group_place * GRAPHS_DEV + pair_row[graph_slot]
    partner_left = group_place * GRAPHS_DEV + inverse[graph_slot]
    d_summary = jnp.where(
        first_view[:, None],
        grad_left[global_id] - 2.0 * right_side[partner_right] / root_width,
        grad_right[global_id] - 2.0 * left_side[partner_left] / root_width,
    )
    loss_terms = jnp.where(
        first_view,
        row_totals[global_id] - logits[global_id, partner_right],
        col_totals[global_id] - logits[partner_left, global_id],
    )
    d_pooled, gain_three = final_back(d_summary)
    d_output = ((d_pooled / own_lens[:, None])[:, None, :] * own_live[:, :, None]).reshape(
        own_rows, -1
    )
    d_ffn = d_output.astype(jnp.bfloat16)
    grad_down = contract_rows(d_ffn, hidden)
    d_hidden = jnp.dot(d_ffn, ffn_full[1], preferred_element_type=jnp.float32)
    d_up = gelu_back(d_hidden)[0].astype(jnp.bfloat16)
    grad_up = contract_rows(normed_two, d_up)
    d_normed_two = contract_last(d_up, ffn_full[0])
    d_middle_norm, gain_two = norm_two_back(d_normed_two)
    d_middle = d_output + d_middle_norm
    d_attn = d_middle.astype(jnp.bfloat16)
    grad_out = contract_rows(heads_out, d_attn)
    d_heads = contract_last(d_attn, out_use).astype(jnp.bfloat16)
    d_projected = attend_back(projected, live_rows, log_totals, d_heads)
    grad_qkv = jnp.einsum(
        "td,tcf->dcf", normed_one, d_projected, preferred_element_type=jnp.float32
    )
    d_normed_one = jnp.einsum(
        "tcf,dcf->td", d_projected, qkv_use, preferred_element_type=jnp.float32
    )
    grad_qkv, grad_out = (
        lax.psum_scatter(
            grad_qkv.astype(jnp.bfloat16), "head", scatter_dimension=2, tiled=True
        ).astype(jnp.float32),
        lax.psum_scatter(
            grad_out.astype(jnp.bfloat16), "head", scatter_dimension=0, tiled=True
        ).astype(jnp.float32),
    )
    grad_qkv, grad_out = (
        lax.psum_scatter(grad_qkv, "dp", scatter_dimension=0, tiled=True),
        lax.psum_scatter(grad_out, "dp", scatter_dimension=1, tiled=True),
    )
    normed_again, norm_one_back = jax.vjp(layer_norm, embedded, gain_full[0])
    d_embedded_norm, gain_one = norm_one_back(d_normed_one)
    d_embedded = d_middle + d_embedded_norm
    grad_ident = contract_rows(ident_rows, d_embedded.astype(jnp.bfloat16))
    grad_ffn, grad_ident, grad_gains = (
        lax.psum_scatter(
            jnp.stack([grad_up, grad_down]), ("dp", "head"), scatter_dimension=1, tiled=True
        ),
        lax.psum_scatter(grad_ident, ("dp", "head"), scatter_dimension=1, tiled=True),
        lax.psum_scatter(
            jnp.stack([gain_one, gain_two, gain_three]),
            ("dp", "head"),
            scatter_dimension=1,
            tiled=True,
        ),
    )
    grads = (grad_ident, grad_qkv, grad_out, grad_ffn, grad_gains)
    squares = sum((jnp.sum(gradient * gradient) for gradient in grads))
    total_loss, square_total = lax.psum((jnp.sum(loss_terms), squares), ("dp", "head"))
    grad_norm = jnp.sqrt(square_total)
    factor = CLIP_AT / jnp.maximum(grad_norm, CLIP_AT)
    ident_res = adam_step(
        ident_weight, grad_ident, ident_first, ident_second, factor, STEP_RATES[0]
    )
    qkv_res = adam_step(qkv_weight, grad_qkv, qkv_first, qkv_second, factor, STEP_RATES[1])
    out_res = adam_step(out_weight, grad_out, out_first, out_second, factor, STEP_RATES[2])
    ffn_res = adam_step(ffn_weight, grad_ffn, ffn_first, ffn_second, factor, STEP_RATES[3])
    gains_res = adam_step(norm_gains, grad_gains, gains_first, gains_second, factor, STEP_RATES[4])
    return (
        grad_norm,
        total_loss,
        ident_res[0],
        qkv_res[0],
        out_res[0],
        ffn_res[0],
        gains_res[0],
        ident_res[1],
        qkv_res[1],
        out_res[1],
        ffn_res[1],
        gains_res[1],
        ident_res[2],
        qkv_res[2],
        out_res[2],
        ffn_res[2],
        gains_res[2],
    )


def solution(mesh):
    in_specs = (
        P("dp", None),
        P("dp", None),
        P("dp", None),
        P("dp", None),
        P("dp", None),
        P(None, ("dp", "head")),
        P("dp", None, "head"),
        P("head", "dp"),
        P(None, ("dp", "head"), None),
        P(None, ("dp", "head")),
        P(None, ("dp", "head")),
        P("dp", None, "head"),
        P("head", "dp"),
        P(None, ("dp", "head"), None),
        P(None, ("dp", "head")),
        P(None, ("dp", "head")),
        P("dp", None, "head"),
        P("head", "dp"),
        P(None, ("dp", "head"), None),
        P(None, ("dp", "head")),
    )
    out_specs = (
        P(),
        P(),
        P(None, ("dp", "head")),
        P("dp", None, "head"),
        P("head", "dp"),
        P(None, ("dp", "head"), None),
        P(None, ("dp", "head")),
        P(None, ("dp", "head")),
        P("dp", None, "head"),
        P("head", "dp"),
        P(None, ("dp", "head"), None),
        P(None, ("dp", "head")),
        P(None, ("dp", "head")),
        P("dp", None, "head"),
        P("head", "dp"),
        P(None, ("dp", "head"), None),
        P(None, ("dp", "head")),
    )
    return jax.shard_map(
        per_device, mesh=mesh, in_specs=in_specs, out_specs=out_specs, check_vma=False
    )
```

profile of v0, /device:TPU:0, one launch (start us, length us, event | category | flops | bytes accessed | tf_op | source)
XLA Modules:
  0.0 850.2 jit_solution(6228935855538569955)
XLA Ops:
  8.4 38.7 %all_gather.26 = bf16[768,3,192]{2,1,0:T(4,128)(2,1)S(1)} all-gather(bf16[96,3,192]{2,1,0:T(4,128)(2,1)S(1)} %copy.206), channel_id=1, replica_groups=mesh['dp'=8,'head'=4] {'dp'}, dimensions={0}, use_global_device_ids=true | all-gather | bytes 995328 | tf_op jit(solution)/shard_map/all_gather | solution.py:155
  49.4 31.1 %all_gather.28 = bf16[192,768]{0,1:T(8,128)(2,1)S(1)} all-gather(bf16[192,96]{0,1:T(8,128)(2,1)S(1)} %copy.214), channel_id=1, replica_groups=mesh['dp'=8,'head'=4] {'dp'}, dimensions={1}, use_global_device_ids=true | all-gather | bytes 331776 | tf_op jit(solution)/shard_map/all_gather | solution.py:156
  88.4 40.1 %all-gather = f32[32,24,3]{1,2,0:T(4,128)S(1)} all-gather(f32[1,24,3]{1,2,0:T(4,128)S(1)} %bitcast.217), channel_id=1, replica_groups=mesh['dp'=8,'head'=4] {'dp','head'}, dimensions={0}, use_global_device_ids=true | all-gather | bytes 9504 | tf_op jit(solution)/shard_map/all_gather | solution.py:151
  128.7 37.5 %all_gather.24 = bf16[32,768]{0,1:T(8,128)(2,1)S(1)} all-gather(bf16[32,24]{0,1:T(8,128)(2,1)S(1)} %convert.37), channel_id=1, replica_groups=mesh['dp'=8,'head'=4] {'dp','head'}, dimensions={1}, use_global_device_ids=true | all-gather | bytes 50688 | tf_op jit(solution)/shard_map/all_gather | solution.py:150
  168.9 8.3 convolution_convert_fusion
  177.2 6.7 copy.208
  187.8 8.6 %fusion.86 = (f32[8,32,128]{2,1,0:T(8,128)S(1)}, f32[8,32,128,128]{2,3,1,0:T(8,128)}) fusion(bf16[8,128,1,32,24]{1,0,4,3,2:T(8,128)(2,1)S(1)} %get-tuple-element.160, bf16[8,128,1,32,24]{1,0,4,3,2:T(8,128)(2,1)S(1)} %get-tuple-element.159, pred[8,128]{1,0:T(8,128)(4,1)S(1)} %get-tuple-element.167), kind=kOutput, calls=%fused_computation.209 | convolution fusion | flops 213876736 | bytes 20055040 | tf_op jit(solution)/shard_map/gqhe,gkhe->ghqk/dot_general | solution.py:58
  196.4 10.5 %fusion = f32[8,32,128]{2,1,0:T(8,128)S(1)} fusion(f32[8,32,128,128]{2,3,1,0:T(8,128)} %get-tuple-element.175, f32[8,32,128]{2,1,0:T(8,128)S(1)} %get-tuple-element.174), kind=kLoop, calls=%fused_computation.16 | loop fusion | flops 8355840 | bytes 17039360 | tf_op jit(solution)/shard_map/reduce_sum | solution.py:69
  207.0 8.9 %fusion.28 = bf16[8,128,32,24]{1,3,2,0:T(8,128)(2,1)S(1)} fusion(f32[8,32,128,128]{2,3,1,0:T(8,128)} %get-tuple-element.175, f32[8,32,128]{2,1,0:T(8,128)S(1)} %fusion, f32[8,32,128]{2,1,0:T(8,128)S(1)} %get-tuple-element.174, bf16[8,128,1,32,24]{1,0,4,3,2:T(8,128)(2,1)S(1)} %get-tuple-element.158), kind=kOutput, calls=%fused_computation.80 | convolution fusion | flops 214695936 | bytes 20185088 | tf_op jit(solution)/shard_map/ghqk,gkhe->gqhe/dot_general | solution.py:71
  224.1 11.5 %multiply_convert_fusion.4 = (bf16[1024,768]{1,0:T(8,128)(2,1)S(1)}, f32[1024,768]{1,0:T(8,128)}, f32[1024,768]{1,0:T(8,128)}) fusion(bf16[2,768,768]{2,1,0:T(8,128)(2,1)} %all-gather.9.cloned.1.call-done, f32[1024,768]{1,0:T(8,128)S(1)} %get-tuple-element.177, f32[768]{0:T(1024)S(1)} %get-tuple-element.130, f32[1024]{0:T(1024)S(1)} %fusion.59, ...), kind=kOutput, calls=%fused_computation.42 | convolution fusion | flops 1262223360 | bytes 12200960 | tf_op jit(solution)/shard_map/dot_general | solution.py:184
  237.6 40.1 %all_gather.31 = f32[256,768]{1,0:T(8,128)S(1)} all-gather(f32[8,768]{1,0:T(8,128)S(1)} %multiply_multiply_fusion.8), channel_id=1, replica_groups=mesh['dp'=8,'head'=4] {'dp','head'}, dimensions={0}, use_global_device_ids=true | all-gather | bytes 811008 | tf_op jit(solution)/shard_map/all_gather | solution.py:199
  313.3 17.1 %multiply_reduce_fusion = (f32[8,32,128]{2,1,0:T(8,128)S(1)}, f32[8,32,128,128]{2,3,1,0:T(8,128)}) fusion(f32[8,32,128,128]{2,3,1,0:T(8,128)} %get-tuple-element.175, f32[8,32,128]{2,1,0:T(8,128)S(1)} %log_add_fusion, bf16[8,128,1,32,24]{1,0,4,3,2:T(8,128)(2,1)} %copy-done.10, bf16[8,128,32,24]{1,0,3,2:T(8,128)(2,1)} %bitcast.196), kind=kOutput, calls=%fused_computation.11 | convolution fusion | flops 213876736 | bytes 36962304 | tf_op jit(solution)/shard_map/gqhe,gkhe->ghqk/dot_general | solution.py:81
  330.4 15.2 %multiply_convert_fusion = bf16[8,32,128,128]{2,3,1,0:T(8,128)(2,1)} fusion(f32[8,32,128,128]{2,3,1,0:T(8,128)} %get-tuple-element.182, f32[8,32,128,128]{2,3,1,0:T(8,128)} %get-tuple-element.175, f32[8,32,128]{2,1,0:T(8,128)S(1)} %get-tuple-element.181, f32[8,32,128]{2,1,0:T(8,128)S(1)} %log_add_fusion), kind=kLoop, calls=%fused_computation.10 | loop fusion | flops 16777216 | bytes 42205184 | tf_op jit(solution)/shard_map/convert_element_type | solution.py:82
  345.6 10.2 %fusion.29 = bf16[8,128,32,24]{1,3,2,0:T(8,128)(2,1)S(1)} fusion(f32[8,32,128,128]{2,3,1,0:T(8,128)} %get-tuple-element.175, f32[8,32,128]{2,1,0:T(8,128)S(1)} %log_add_fusion, bf16[8,128,32,24]{1,0,3,2:T(8,128)(2,1)S(1)} %bitcast.197), kind=kOutput, calls=%fused_computation.81 | convolution fusion | flops 210501632 | bytes 20054016 | tf_op jit(solution)/shard_map/ghqk,gqhe->gkhe/dot_general | solution.py:92
  381.0 8.3 fusion.33
  398.8 9.2 %convolution_convert_fusion.1 = bf16[768,3,768]{0,2,1:T(8,128)(2,1)} fusion(bf16[1024,1,768]{2,0,1:T(8,128)(2,1)} %copy.228, bf16[1024,1,768]{2,0,1:T(8,128)(2,1)} %copy.227, bf16[1024,1,768]{2,0,1:T(8,128)(2,1)} %copy.226, f32[1024,768]{1,0:T(8,128)} %copy-done.3, f32[768]{0:T(1024)S(1)} %copy-done.50, f32[1024]{0:T(1024)S(1)} %copy-done.46, ...), kind=kOutput, calls=%fused_computation.63 | convolution fusion | flops 3642949632 | bytes 11414528 | tf_op jit(solution)/shard_map/td,tcf->dcf/dot_general | solution.py:247
  408.1 9.2 %fusion.7 = (f32[768]{0:T(1024)S(1)}, f32[1024]{0:T(1024)S(1)}, f32[1024,768,1]{1,0,2:T(8,128)S(1)}) fusion(f32[1024,768]{1,0:T(8,128)} %copy-done.3, f32[1024]{0:T(1024)S(1)} %copy-done.46, f32[1024]{0:T(1024)S(1)} %broadcast_multiply_fusion.1, f32[768]{0:T(1024)S(1)} %copy-done.50, bf16[768,3,768]{0,2,1:T(8,128)(2,1)} %all-gather.5.cloned.1.call-done, ...), kind=kOutput, calls=%fused_computation.29 | convolution fusion | flops 3634100480 | bytes 14567424 | tf_op jit(solution)/shard_map/tcf,dcf->td/dot_general | solution.py:250
  432.5 12.3 %reduce-scatter.14.cloned.1.call-done = bf16[768,3,192]{0,2,1:T(8,128)(2,1)} async-done(((bf16[768,3,768]{0,2,1:T(8,128)(2,1)}), bf16[768,3,192]{0,2,1:T(8,128)(2,1)}) %reduce-scatter.14.cloned.1.call-update) | async-done | bytes 884752 | tf_op jit(solution)/shard_map/reduce_scatter | solution.py:254
  451.1 39.5 %all-reduce.1 = f32[3,768]{1,0:T(4,128)S(1)} all-reduce(f32[3,768]{1,0:T(4,128)S(1)} %pad_maximum_fusion.4), channel_id=8, replica_groups=mesh['dp'=8,'head'=4] {'dp','head'}, use_global_device_ids=true, to_apply=%region_34.35.clone | all-reduce | flops 2304 | bytes 18432
  491.9 52.4 %reduce-scatter.24.cloned.1.call-done = f32[32,24]{0,1:T(8,128)} async-done(((f32[32,768]{0,1:T(8,128)}), f32[32,24]{0,1:T(8,128)}) %reduce-scatter.24.cloned.1.call-update) | async-done | bytes 3088
  545.6 63.9 %reduce-scatter.22.cloned.1.call-done = f32[96,192]{1,0:T(8,128)} async-done(((f32[768,192]{1,0:T(8,128)}), f32[96,192]{1,0:T(8,128)}) %reduce-scatter.22.cloned.1.call-update) | async-done | bytes 73744
  611.2 109.8 %reduce-scatter.18.cloned.1.call-done = f32[2,24,768]{2,1,0:T(8,128)} async-done(((f32[2,768,768]{2,1,0:T(8,128)}), f32[2,24,768]{2,1,0:T(8,128)}) %reduce-scatter.18.cloned.1.call-update) | async-done | bytes 147472 | tf_op jit(solution)/shard_map/reduce_scatter | solution.py:270
  722.6 68.3 %reduce-scatter.20.cloned.1.call-done = f32[96,576]{1,0:T(8,128)} async-done(((f32[768,576]{1,0:T(8,128)}), f32[96,576]{1,0:T(8,128)}) %reduce-scatter.20.cloned.1.call-update) | async-done | bytes 221200
  796.1 39.6 %all-reduce.2 = (f32[]{:T(128)}, f32[]{:T(128)}) all-reduce(f32[]{:T(128)S(6)} %add.358, f32[]{:T(128)} %select_reduce_fusion.1), channel_id=1, replica_groups=mesh['dp'=8,'head'=4] {'dp','head'}, use_global_device_ids=true, to_apply=%region_36.37 | all-reduce | flops 2 | bytes 16 | tf_op jit(solution)/shard_map/psum | solution.py:283
  (268 shorter events, 132.8 us)
Async XLA Ops:
  7.2 161.7 %all-gather.5.cloned.1.call-start = ((), (), s32[]{:S(2)}) async-start(), calls=%async_computation.6 | async-start | bytes 4423680 | tf_op jit(solution)/shard_map/all_gather | solution.py:159
  49.2 169.6 %all-gather.7.cloned.1.call-start = ((), (), s32[]{:S(2)}) async-start(), calls=%async_computation.7 | async-start | bytes 1474560 | tf_op jit(solution)/shard_map/all_gather | solution.py:160
  81.4 142.7 %all-gather.9.cloned.1.call-start = ((), (), s32[]{:S(2)}) async-start(), calls=%async_computation.8 | async-start | bytes 2433024 | tf_op jit(solution)/shard_map/all_gather | solution.py:153
  82.1 340.5 %reduce-scatter.16.cloned.1.call-start = ((), (), s32[]{:S(2)}) async-start(), calls=%async_computation.10 | async-start | bytes 1474560 | tf_op jit(solution)/shard_map/reduce_scatter | solution.py:257
  82.9 154.6 %copy-start.41 = (f32[8]{0:T(128)}, f32[8]{0:T(128)S(1)}, u32[]{:S(2)}) copy-start(f32[8]{0:T(128)S(1)} %dynamic-slice_convert_fusion.1) | copy-start | bytes 100
  313.3 131.5 %reduce-scatter.14.cloned.1.call-start = ((), (), s32[]{:S(2)}) async-start(), calls=%async_computation.9 | async-start | bytes 4423680 | tf_op jit(solution)/shard_map/reduce_scatter | solution.py:254
  408.0 136.3 %reduce-scatter.24.cloned.1.call-start = ((), (), s32[]{:S(2)}) async-start(), calls=%async_computation.14 | async-start | bytes 405504
  422.5 187.0 %reduce-scatter.22.cloned.1.call-start = ((), (), s32[]{:S(2)}) async-start(), calls=%async_computation.13 | async-start | bytes 884736
  424.7 296.3 %reduce-scatter.18.cloned.1.call-start = ((), (), s32[]{:S(2)}) async-start(), calls=%async_computation.11 | async-start | bytes 4866048 | tf_op jit(solution)/shard_map/reduce_scatter | solution.py:270
  432.4 358.5 %reduce-scatter.20.cloned.1.call-start = ((), (), s32[]{:S(2)}) async-start(), calls=%async_computation.12 | async-start | bytes 2211840
  448.0 347.9 %copy-start.29 = (f32[96,3,192]{2,0,1:T(8,128)S(1)}, f32[96,3,192]{2,0,1:T(8,128)}, u32[]{:S(2)}) copy-start(f32[96,3,192]{2,0,1:T(8,128)} %param.36) | copy-start | bytes 663556
  450.3 389.0 %copy-start.55 = (f32[3,24]{1,0:T(4,128)S(1)}, f32[3,24]{1,0:T(4,128)}, u32[]{:S(2)}) copy-start(f32[3,24]{1,0:T(4,128)} %param.29) | copy-start | bytes 868
  450.4 389.0 %copy-start.56 = (f32[3,24]{1,0:T(4,128)S(1)}, f32[3,24]{1,0:T(4,128)}, u32[]{:S(2)}) copy-start(f32[3,24]{1,0:T(4,128)} %param.34) | copy-start | bytes 868
  450.4 389.0 %copy-start.57 = (f32[3,24]{1,0:T(4,128)S(1)}, f32[3,24]{1,0:T(4,128)}, u32[]{:S(2)}) copy-start(f32[3,24]{1,0:T(4,128)} %param.39) | copy-start | bytes 868
  450.4 389.6 %copy-start.27 = (f32[192,96]{1,0:T(8,128)S(1)}, f32[192,96]{1,0:T(8,128)}, u32[]{:S(2)}) copy-start(f32[192,96]{1,0:T(8,128)} %param.27) | copy-start | bytes 221188
  450.4 389.6 %copy-start.32 = (f32[192,96]{1,0:T(8,128)S(1)}, f32[192,96]{1,0:T(8,128)}, u32[]{:S(2)}) copy-start(f32[192,96]{1,0:T(8,128)} %param.32) | copy-start | bytes 221188
  450.4 389.6 %copy-start.33 = (f32[192,96]{1,0:T(8,128)S(1)}, f32[192,96]{1,0:T(8,128)}, u32[]{:S(2)}) copy-start(f32[192,96]{1,0:T(8,128)} %param.37) | copy-start | bytes 221188
  610.5 230.3 %copy-start.35 = (f32[32,24]{0,1:T(8,128)S(1)}, f32[32,24]{0,1:T(8,128)}, u32[]{:S(2)}) copy-start(f32[32,24]{0,1:T(8,128)} %param.25) | copy-start | bytes 9220
  610.5 230.2 %copy-start.36 = (f32[32,24]{0,1:T(8,128)S(1)}, f32[32,24]{0,1:T(8,128)}, u32[]{:S(2)}) copy-start(f32[32,24]{0,1:T(8,128)} %reduce-scatter.24.cloned.1.call-done) | copy-start | bytes 9220
  610.5 230.2 %copy-start.51 = (f32[32,24]{0,1:T(8,128)S(1)}, f32[32,24]{0,1:T(8,128)}, u32[]{:S(2)}) copy-start(f32[32,24]{0,1:T(8,128)} %param.30) | copy-start | bytes 9220
  610.6 230.2 %copy-start.52 = (f32[32,24]{0,1:T(8,128)S(1)}, f32[32,24]{0,1:T(8,128)}, u32[]{:S(2)}) copy-start(f32[32,24]{0,1:T(8,128)} %param.35) | copy-start | bytes 9220
  610.6 230.9 %copy-start.20 = (f32[2,24,768]{2,1,0:T(8,128)S(1)}, f32[2,24,768]{2,1,0:T(8,128)}, u32[]{:S(2)}) copy-start(f32[2,24,768]{2,1,0:T(8,128)} %param.28) | copy-start | bytes 442372
  610.6 230.8 %copy-start.30 = (f32[2,24,768]{2,1,0:T(8,128)S(1)}, f32[2,24,768]{2,1,0:T(8,128)}, u32[]{:S(2)}) copy-start(f32[2,24,768]{2,1,0:T(8,128)} %param.33) | copy-start | bytes 442372
  610.6 230.8 %copy-start.31 = (f32[2,24,768]{2,1,0:T(8,128)S(1)}, f32[2,24,768]{2,1,0:T(8,128)}, u32[]{:S(2)}) copy-start(f32[2,24,768]{2,1,0:T(8,128)} %param.38) | copy-start | bytes 442372
  (47 other events, 1185.9 us)
Sparse Core Ops, SparseCore 0:
  49.4 30.0 all-gather.4
  81.6 17.6 all-gather.6
  102.8 57.7 all-gather.8
  313.4 21.8 reduce-scatter.15
  408.1 36.5 reduce-scatter.13
  449.5 94.7 reduce-scatter.23
  548.0 61.5 reduce-scatter.21
  615.0 105.9 reduce-scatter.17
  724.9 65.9 reduce-scatter.19
where the time goes:
time: 859 us; the launch traced here: 850 us
  waiting for transfers between devices  307 us (36%)
  blocking collectives  267 us (31%)
  matrix products  129 us (15%)
  local copies, waits for them, and re-layouts  75.6 us (9%)
  other arithmetic  51.1 us (6%)
  between operations  20.4 us (2%)
    unnamed x12, waiting for transfers between devices  185 us
    reduce_scatter x1, waiting for transfers between devices, per_device(): lax.psum_scatter(jnp.stack([grad_up, grad_down]), ('dp', 'head'), scatter...  110 us
    all_gather x1, blocking collectives, per_device(): lax.all_gather(norm_gains, ('dp', 'head'), axis=1, tiled=True)  40.1 us
    all_gather x1, blocking collectives, per_device(): gathered = lax.all_gather(summary, ('dp', 'head'), axis=0, tiled=True)  40.1 us
    psum x1, blocking collectives, per_device(): lax.psum((jnp.sum(loss_terms), squares), ('dp', 'head'))  39.6 us
    unnamed x1, blocking collectives  39.5 us
    all_gather x1, blocking collectives, per_device(): lax.all_gather(qkv_weight.astype(jnp.bfloat16), 'dp', axis=0, tiled=True)  38.7 us
    all_gather x1, blocking collectives, per_device(): lax.all_gather(ident_weight, ('dp', 'head'), axis=1, tiled=True)  37.5 us
  transfers between devices with their start and end apart: 9, of which 5 were waited for; matrix products, arithmetic and copies ran while one was open for 23% of the time, Pallas kernels for 0%

commit v1 on v0

v1 whole, which is shorter than its diff:
```python
import functools

import jax
import jax.numpy as jnp
from jax import lax
from jax.experimental import pallas as pl
from jax.experimental.pallas import tpu as pltpu
from jax.sharding import PartitionSpec as P

D = 768
HEAD_DIM = 24
LAP = 16
LEN = 128
NODE = 32
STEPS = 3
GRAPHS_DEV = 16

HIGHEST = lax.Precision.HIGHEST
NORM_EPS = 1e-05
CLIP_AT = 5.0
STEP_RATES = (0.08, 0.02, 0.15, 0.02, 0.5)
BETA_ONE = 0.5
BETA_TWO = 0.5
DECAY = 0.01
ADAM_EPS = 1e-08
MASKED = -1e30

BF = jnp.bfloat16
F32 = jnp.float32
SUB = 4
SW = SUB * HEAD_DIM
PACK = 4 * SW
V_AT = 128 - SW
SCALE = HEAD_DIM ** (-0.5)
VMEM_LIMIT = 56 * 2**20


def nn(a, b):
    return lax.dot_general(a, b, (((1,), (0,)), ((), ())), preferred_element_type=F32)


def nt(a, b):
    return lax.dot_general(a, b, (((1,), (1,)), ((), ())), preferred_element_type=F32)


def tn(a, b):
    return lax.dot_general(a, b, (((0,), (0,)), ((), ())), preferred_element_type=F32)


def lanes():
    return lax.broadcasted_iota(jnp.int32, (1, 128), 1)


def head_lanes(h, at):
    lane = lanes()
    return (lane >= at + h * HEAD_DIM) & (lane < at + (h + 1) * HEAD_DIM)


def by_head(v, at):
    zero = jnp.zeros_like(v)
    return jnp.concatenate([jnp.where(head_lanes(h, at), v, zero) for h in range(SUB)], axis=0)


def stack_heads(v):
    return jnp.concatenate([v[:, h * LEN : (h + 1) * LEN] for h in range(SUB)], axis=0)


def attend_kernel(lens_ref, x_ref, w_ref, qkv_ref, p_ref, o_ref, rinv_ref, *, graphs):
    y = nn(x_ref[...], w_ref[0])
    qkv_ref[0, 0] = y[:, :128].astype(BF)
    qkv_ref[0, 1] = pltpu.roll(y, PACK - SW, 1)[:, :128].astype(BF)
    qkv_ref[0, 2] = pltpu.roll(y, SW, 1)[:, 256:].astype(BF)
    col = lanes()
    ones = by_head(jnp.ones((LEN, 128), BF), V_AT)
    for g in range(graphs):
        rows = slice(g * LEN, (g + 1) * LEN)
        query, keys, values = qkv_ref[0, 0, rows, :], qkv_ref[0, 1, rows, :], qkv_ref[0, 2, rows, :]
        live = col < lens_ref[g]
        scores = nt(query, by_head(keys, 0))
        parts = []
        for h in range(SUB):
            own = jnp.where(live, scores[:, h * LEN : (h + 1) * LEN] * SCALE, MASKED)
            parts.append(jnp.exp(own - jnp.max(own, axis=1, keepdims=True)).astype(BF))
        expo = jnp.concatenate(parts, axis=1)
        both = nn(expo, jnp.concatenate([by_head(values, V_AT), ones], axis=1))
        rinv = jnp.where(col >= V_AT, 1.0 / both[:, 128:], 0.0)
        p_ref[0, rows, :] = expo
        rinv_ref[0, rows, :] = rinv
        o_ref[0, rows, :] = jnp.where(col >= V_AT, both[:, :128] * rinv, 0.0).astype(BF)


def attend(lens, x, w):
    tokens, groups = x.shape[0], w.shape[0]
    block = lambda *tail: pl.BlockSpec((1,) + tail, lambda i: (i,) + (0,) * len(tail))
    return pl.pallas_call(
        functools.partial(attend_kernel, graphs=tokens // LEN),
        grid=(groups,),
        in_specs=[
            pl.BlockSpec(memory_space=pltpu.SMEM),
            pl.BlockSpec((tokens, D), lambda i: (0, 0)),
            block(D, PACK),
        ],
        out_specs=[block(3, tokens, 128), block(tokens, 512), block(tokens, 128), block(tokens, 128)],
        out_shape=[
            jax.ShapeDtypeStruct((groups, 3, tokens, 128), BF),
            jax.ShapeDtypeStruct((groups, tokens, 512), BF),
            jax.ShapeDtypeStruct((groups, tokens, 128), BF),
            jax.ShapeDtypeStruct((groups, tokens, 128), F32),
        ],
        compiler_params=pltpu.CompilerParams(vmem_limit_bytes=VMEM_LIMIT),
        cost_estimate=pl.CostEstimate(
            flops=groups * 2_500_000_000, bytes_accessed=groups * 3_000_000, transcendentals=0
        ),
        name="attend",
    )(lens, x, w)


def attend_back_kernel(
    x_ref, da_ref, w_ref, qkv_ref, p_ref, o_ref, rinv_ref, g_ref, dn_ref, xt, dt, dqkv, aug, *, graphs
):
    step = pl.program_id(0)

    @pl.when(step == 0)
    def _():
        xt[...] = x_ref[...].T
        dt[...] = da_ref[...].T

    w = w_ref[0]
    lane = lanes()
    d_out = jnp.where(lane >= V_AT, nn(da_ref[...], w[:, 256:]) * rinv_ref[0], 0.0)
    heads_out = o_ref[0]
    terms = d_out * heads_out.astype(F32)
    high = terms.astype(BF)
    low = (terms - high.astype(F32)).astype(BF)
    row = lax.broadcasted_iota(jnp.int32, (128, 128), 0)
    column = lax.broadcasted_iota(jnp.int32, (128, 128), 1)
    pick = jnp.zeros((128, 128), BF)
    for h in range(SUB):
        inside = (row >= V_AT + h * HEAD_DIM) & (row < V_AT + (h + 1) * HEAD_DIM)
        pick = jnp.where(inside & ((column == h) | (column == SUB + h)), jnp.ones_like(pick), pick)
    delta = nn(high, pick) + nn(low, pick)
    rounded = delta.astype(BF).astype(F32)
    aug[...] = jnp.where(
        lane >= V_AT, d_out, jnp.where(lane < SUB, -rounded, rounded - delta)
    ).astype(BF)
    for g in range(graphs):
        rows = slice(g * LEN, (g + 1) * LEN)
        query, keys, values = qkv_ref[0, 0, rows, :], qkv_ref[0, 1, rows, :], qkv_ref[0, 2, rows, :]
        d_rows, expo = aug[rows, :], p_ref[0, rows, :]
        one, zero = jnp.ones_like(values), jnp.zeros_like(values)
        spread = jnp.concatenate(
            [
                jnp.where(
                    head_lanes(h, V_AT), values, jnp.where((lane == h) | (lane == SUB + h), one, zero)
                )
                for h in range(SUB)
            ],
            axis=0,
        )
        d_scores = (expo.astype(F32) * nt(d_rows, spread)).astype(BF)
        d_query = nn(d_scores, by_head(keys, 0)) * SCALE
        d_keys = tn(stack_heads(d_scores), by_head(query, 0)) * SCALE
        d_values = tn(stack_heads(expo), by_head(d_rows, V_AT))
        rolled_keys, rolled_values = pltpu.roll(d_keys, SW, 1), pltpu.roll(d_values, V_AT, 1)
        dqkv[rows, 0:128] = jnp.where(lane < SW, d_query, rolled_keys).astype(BF)
        dqkv[rows, 128:256] = jnp.where(lane < 64, rolled_keys, rolled_values).astype(BF)
        dqkv[rows, 256:384] = jnp.where(lane < V_AT, rolled_values, 0.0).astype(BF)
    d_packed = dqkv[...]
    grad = nn(xt[...], d_packed)
    grad_out = nn(dt[...], heads_out)
    g_ref[0, :, 0:256] = grad[:, 0:256].astype(BF)
    g_ref[0, :, 256:384] = (grad[:, 256:384] + grad_out).astype(BF)
    d_normed = nt(d_packed, w)

    @pl.when(step == 0)
    def _():
        dn_ref[...] = d_normed

    @pl.when(step > 0)
    def _():
        dn_ref[...] += d_normed


def attend_back(x, d_attn, w, saved):
    qkv, expo, heads_out, rinv = saved
    tokens, groups = x.shape[0], w.shape[0]
    block = lambda *tail: pl.BlockSpec((1,) + tail, lambda i: (i,) + (0,) * len(tail))
    whole = pl.BlockSpec((tokens, D), lambda i: (0, 0))
    return pl.pallas_call(
        functools.partial(attend_back_kernel, graphs=tokens // LEN),
        grid=(groups,),
        in_specs=[
            whole,
            whole,
            block(D, PACK),
            block(3, tokens, 128),
            block(tokens, 512),
            block(tokens, 128),
            block(tokens, 128),
        ],
        out_specs=[block(D, PACK), whole],
        out_shape=[
            jax.ShapeDtypeStruct((groups, D, PACK), BF),
            jax.ShapeDtypeStruct((tokens, D), F32),
        ],
        scratch_shapes=[
            pltpu.VMEM((D, tokens), BF),
            pltpu.VMEM((D, tokens), BF),
            pltpu.VMEM((tokens, PACK), BF),
            pltpu.VMEM((tokens, 128), BF),
        ],
        compiler_params=pltpu.CompilerParams(vmem_limit_bytes=VMEM_LIMIT),
        cost_estimate=pl.CostEstimate(
            flops=groups * 7_000_000_000, bytes_accessed=groups * 3_000_000, transcendentals=0
        ),
        name="attend_back",
    )(x, d_attn, w, qkv, expo, heads_out, rinv)


def erf(x):
    x = jnp.clip(x, -3.832506856900711, 3.832506856900711)
    x2 = x * x
    top = 0.00022905065861350646
    for c in (
        0.0034082910107109506,
        0.050955695062380861,
        0.18520832239976145,
        1.128379143519084,
    ):
        top = top * x2 + c
    bottom = -1.1791602954361697e-7
    for c in (
        0.000023547966471313185,
        0.0010179625278914885,
        0.014070470171167667,
        0.11098505178285362,
        0.49746925110067538,
        1.0,
    ):
        bottom = bottom * x2 + c
    return x * top / bottom


def normalize(values):
    centred = values - jnp.mean(values, axis=-1, keepdims=True)
    spread = jnp.mean(centred * centred, axis=-1, keepdims=True)
    rstd = lax.rsqrt(spread + NORM_EPS)
    return centred * rstd, rstd


def two_parts(v):
    high = v.astype(BF)
    return high, (v - high.astype(F32)).astype(BF)


def forward_kernel(
    lens_ref, e_ref, gain_ref, up_ref, down_ref, *refs, tile_graphs, waves, groups
):
    o_refs, w_refs = refs[:waves], refs[waves : 2 * waves]
    mid_ref, slope_ref, hsum_ref, pay_ref, hsum, msum = refs[2 * waves :]
    step, steps = pl.program_id(0), pl.num_programs(0)
    middle = e_ref[...]
    for wave in range(waves):
        left = jnp.concatenate([o_refs[wave][j] for j in range(groups)], axis=1)
        right = jnp.concatenate([w_refs[wave][j][:, 256:] for j in range(groups)], axis=1)
        middle = middle + nt(left, right)
    mid_ref[...] = middle
    xhat, _ = normalize(middle)
    up = nn((xhat * gain_ref[1:2, :]).astype(BF), up_ref[...])
    cdf = 0.5 + 0.5 * erf(up * (0.5**0.5))
    hidden = (up * cdf).astype(BF).astype(F32)
    slope_ref[...] = (cdf + up * (0.3989422804014327 * jnp.exp(-0.5 * up * up))).astype(BF)
    place = lax.broadcasted_iota(jnp.int32, (LEN, 1), 0)
    for j in range(tile_graphs):
        g = step * tile_graphs + j
        live = place < lens_ref[g]
        rows = slice(j * LEN, (j + 1) * LEN)
        hsum[pl.ds(g, 1), :] = jnp.sum(jnp.where(live, hidden[rows], 0.0), axis=0, keepdims=True)
        msum[pl.ds(g, 1), :] = jnp.sum(jnp.where(live, middle[rows], 0.0), axis=0, keepdims=True)

    @pl.when(step == steps - 1)
    def _():
        graphs = hsum.shape[0]
        high, low = two_parts(hsum[...])
        which = lax.broadcasted_iota(jnp.int32, (graphs, 1), 0)
        length = jnp.ones((graphs, 1), F32)
        for g in range(graphs):
            length = jnp.where(which == g, lens_ref[g].astype(F32), length)
        pooled = (msum[...] + (nt(high, down_ref[...]) + nt(low, down_ref[...]))) / length
        xhat_pool, rstd = normalize(pooled)
        hsum_ref[...] = hsum[...].astype(BF)
        pay_ref[:, :D] = xhat_pool
        lane = lanes()
        pay_ref[:, D:] = jnp.where(lane == 0, rstd, jnp.where(lane == 1, 1.0 / length, 0.0))


def forward_rest(lens, embedded, gains, w_up, w_down, outs, weights):
    tokens = embedded.shape[0]
    graphs = tokens // LEN
    tile_graphs = min(2, graphs)
    rows = tile_graphs * LEN
    waves, groups = len(outs), outs[0].shape[0]
    full = lambda a: pl.BlockSpec(a.shape, lambda i: (0,) * a.ndim)
    tile = pl.BlockSpec((rows, D), lambda i: (i, 0))
    return pl.pallas_call(
        functools.partial(forward_kernel, tile_graphs=tile_graphs, waves=waves, groups=groups),
        grid=(tokens // rows,),
        in_specs=[pl.BlockSpec(memory_space=pltpu.SMEM), tile, full(gains), full(w_up), full(w_down)]
        + [pl.BlockSpec((groups, rows, 128), lambda i: (0, i, 0)) for _ in outs]
        + [full(w) for w in weights],
        out_specs=[
            tile,
            tile,
            pl.BlockSpec((graphs, D), lambda i: (0, 0)),
            pl.BlockSpec((graphs, D + 128), lambda i: (0, 0)),
        ],
        out_shape=[
            jax.ShapeDtypeStruct((tokens, D), F32),
            jax.ShapeDtypeStruct((tokens, D), BF),
            jax.ShapeDtypeStruct((graphs, D), BF),
            jax.ShapeDtypeStruct((graphs, D + 128), F32),
        ],
        scratch_shapes=[pltpu.VMEM((graphs, D), F32), pltpu.VMEM((graphs, D), F32)],
        compiler_params=pltpu.CompilerParams(vmem_limit_bytes=VMEM_LIMIT),
        cost_estimate=pl.CostEstimate(
            flops=10_000_000_000, bytes_accessed=20_000_000, transcendentals=0
        ),
        name="forward_rest",
    )(lens, embedded, gains, w_up, w_down, *outs, *weights)


def norm_back(d_normed, xhat, rstd, gain):
    d_hat = d_normed * gain
    return rstd * (
        d_hat
        - jnp.mean(d_hat, axis=-1, keepdims=True)
        - xhat * jnp.mean(d_hat * xhat, axis=-1, keepdims=True)
    )


def ffn_back_kernel(
    lens_ref, mid_ref, slope_ref, dout_ref, dhid_ref, gain_ref, up_ref,
    dmid_ref, dattn_ref, grad_ref, dgain_ref, grad, dgain, *, tile_graphs
):
    step, steps = pl.program_id(0), pl.num_programs(0)
    xhat, rstd = normalize(mid_ref[...])
    gain = gain_ref[1:2, :]
    place = lax.broadcasted_iota(jnp.int32, (LEN, 1), 0)
    d_up, d_out = [], []
    for j in range(tile_graphs):
        g = step * tile_graphs + j
        live = place < lens_ref[g]
        rows = slice(j * LEN, (j + 1) * LEN)
        d_hidden = jnp.where(live, dhid_ref[pl.ds(g, 1), :], 0.0)
        d_up.append((slope_ref[rows, :].astype(F32) * d_hidden).astype(BF))
        d_out.append(jnp.where(live, dout_ref[pl.ds(g, 1), :], 0.0))
    d_up, d_out = jnp.concatenate(d_up, axis=0), jnp.concatenate(d_out, axis=0)
    d_normed = nt(d_up, up_ref[...])
    d_mid = d_out + norm_back(d_normed, xhat, rstd, gain)
    dmid_ref[...] = d_mid
    dattn_ref[...] = d_mid.astype(BF)
    part = tn((xhat * gain).astype(BF), d_up)
    part_gain = jnp.sum((d_normed * xhat).reshape(-1, 8, D), axis=0)

    @pl.when(step == 0)
    def _():
        grad[...] = part
        dgain[...] = part_gain

    @pl.when(step > 0)
    def _():
        grad[...] += part
        dgain[...] += part_gain

    @pl.when(step == steps - 1)
    def _():
        grad_ref[...] = grad[...].astype(BF)
        dgain_ref[...] = dgain[...]


def ffn_back(lens, middle, slope, d_out, d_hidden, gains, w_up):
    tokens = middle.shape[0]
    tile_graphs = min(2, tokens // LEN)
    rows = tile_graphs * LEN
    full = lambda a: pl.BlockSpec(a.shape, lambda i: (0,) * a.ndim)
    tile = pl.BlockSpec((rows, D), lambda i: (i, 0))
    return pl.pallas_call(
        functools.partial(ffn_back_kernel, tile_graphs=tile_graphs),
        grid=(tokens // rows,),
        in_specs=[pl.BlockSpec(memory_space=pltpu.SMEM), tile, tile]
        + [full(a) for a in (d_out, d_hidden, gains, w_up)],
        out_specs=[
            tile,
            tile,
            pl.BlockSpec((D, D), lambda i: (0, 0)),
            pl.BlockSpec((8, D), lambda i: (0, 0)),
        ],
        out_shape=[
            jax.ShapeDtypeStruct((tokens, D), F32),
            jax.ShapeDtypeStruct((tokens, D), BF),
            jax.ShapeDtypeStruct((D, D), BF),
            jax.ShapeDtypeStruct((8, D), F32),
        ],
        scratch_shapes=[pltpu.VMEM((D, D), F32), pltpu.VMEM((8, D), F32)],
        compiler_params=pltpu.CompilerParams(vmem_limit_bytes=VMEM_LIMIT),
        cost_estimate=pl.CostEstimate(
            flops=10_000_000_000, bytes_accessed=15_000_000, transcendentals=0
        ),
        name="ffn_back",
    )(lens, middle, slope, d_out, d_hidden, gains, w_up)


class Place:
    def __init__(self):
        self.n, self.heads = lax.axis_size("dp"), lax.axis_size("head")
        self.inner = 1 << ((self.n.bit_length() - 1) // 2)
        self.outer = self.n // self.inner
        self.dp, self.head = lax.axis_index("dp"), lax.axis_index("head")
        self.bits = [1 << b for b in range(self.heads.bit_length() - 1)]

    def swap(self, v, bit):
        return lax.ppermute(v, "head", [(i, i ^ bit) for i in range(self.heads)])

    def digit(self, which):
        size, stride = (self.outer, self.inner) if which == "outer" else (self.inner, 1)
        return size, stride, (self.dp // stride) % size

    def shift(self, v, which, by):
        size, stride, _ = self.digit(which)
        pairs = []
        for i in range(self.n):
            own = (i // stride) % size
            pairs.append((i, i + ((own + by) % size - own) * stride))
        return lax.ppermute(v, "dp", pairs)

    def gather_digit(self, v, which, axis=0):
        size, _, own = self.digit(which)
        out = jnp.zeros(v.shape[:axis] + (size,) + v.shape[axis:], v.dtype)
        out = lax.dynamic_update_index_in_dim(out, v, own, axis)
        for by in range(1, size):
            out = lax.dynamic_update_index_in_dim(
                out, self.shift(v, which, by), (own - by) % size, axis
            )
        return out

    def gather_bit(self, v, bit, axis=0):
        own = (self.head // bit) % 2
        other = self.swap(v, bit)
        first, second = jnp.where(own == 0, v, other), jnp.where(own == 0, other, v)
        return jnp.stack([first, second], axis=axis)

    def gather_all(self, v):
        v = self.gather_digit(v, "outer")
        v = self.gather_digit(v, "inner", 1)
        for bit in self.bits[::-1]:
            v = self.gather_bit(v, bit, 2 + self.bits[::-1].index(bit))
        return v.reshape((self.n, self.heads) + v.shape[2 + len(self.bits) :])

    def reduce_digit(self, v, which, axis=0):
        size, _, own = self.digit(which)
        pick = lambda by: lax.dynamic_index_in_dim(v, (own + by) % size, axis, keepdims=False)
        total = pick(0).astype(F32)
        for by in range(1, size):
            total = total + self.shift(pick(by), which, by).astype(F32)
        return total

    def reduce_bit(self, v, bit, axis):
        own = (self.head // bit) % 2
        pick = lambda at: lax.dynamic_index_in_dim(v, at, axis, keepdims=False)
        return pick(own).astype(F32) + self.swap(pick(1 - own), bit).astype(F32)

    def reduce_all(self, v, dtype):
        rows = v.shape[0] // (self.n * self.heads)
        v = v.reshape((self.outer, self.inner) + (2,) * len(self.bits) + (rows,) + v.shape[1:])
        for bit in self.bits:
            v = self.reduce_bit(v.astype(dtype), bit, 1 + len(self.bits) - self.bits.index(bit))
        v = self.reduce_digit(v.astype(dtype), "inner", 1)
        return self.reduce_digit(v.astype(dtype), "outer", 0)

    def total(self, v):
        for bit in self.bits:
            v = v + self.swap(v, bit)
        for which in ("inner", "outer"):
            size, stride, own = self.digit(which)
            by = 1
            while by < size:
                pairs = []
                for i in range(self.n):
                    at = (i // stride) % size
                    pairs.append((i, i + ((at ^ by) - at) * stride))
                v = v + lax.ppermute(v, "dp", pairs)
                by *= 2
        return v


def gather_attention(place, shards):
    low, high = place.bits[:-1], place.bits[-1:]
    result = []
    for s, shard in enumerate(shards):
        part = place.gather_digit(shard, "outer")
        found = {0: part}

        def exchange(bits, found):
            for bit in bits:
                found = {**found, **{r ^ bit: place.swap(v, bit) for r, v in found.items()}}
            return found

        if s % 2:
            found = exchange(high, found)
        found = {r: place.gather_digit(v, "inner", 1) for r, v in found.items()}
        if s % 2 == 0:
            found = exchange(high, found)
        found = exchange(low[::-1], found)
        result.append({r: v.reshape(-1, v.shape[-1]) for r, v in found.items()})
    return result


def reduce_attention(place, s, grads):
    found = {
        r: v.reshape(place.outer, place.inner, -1, v.shape[-1]) for r, v in grads.items()
    }

    def fold(bits, found):
        for bit in bits:
            found = {
                r: v.astype(F32) + place.swap(found[r ^ bit].astype(BF), bit).astype(F32)
                for r, v in found.items()
                if not r & bit
            }
        return found

    low, high = place.bits[:-1], place.bits[-1:]
    found = fold(low, found)
    if s % 2 == 0:
        found = fold(high, found)
    found = {r: place.reduce_digit(v.astype(BF), "inner", 1) for r, v in found.items()}
    if s % 2:
        found = fold(high, found)
    return place.reduce_digit(found[0].astype(BF), "outer", 0)


def log_total(values, axis):
    top = jnp.max(values, axis=axis, keepdims=True)
    return jnp.squeeze(top, axis) + jnp.log(jnp.sum(jnp.exp(values - top), axis=axis))


def identifiers(table, endpoints):
    graphs = endpoints.shape[0] // LEN
    nodes = table.reshape(graphs, NODE, LAP).astype(BF)
    picks = (
        endpoints.reshape(graphs, LEN, 2)[..., None] == jnp.arange(NODE, dtype=jnp.int32)
    ).astype(BF)
    found = jnp.einsum("glan,gnc->glac", picks, nodes, preferred_element_type=F32)
    return found.reshape(graphs * LEN, 2 * LAP).astype(BF)


def adam_step(weight, gradient, first, second, factor, rate):
    clipped = gradient * factor
    first_new = BETA_ONE * first + (1.0 - BETA_ONE) * clipped
    second_new = BETA_TWO * second + (1.0 - BETA_TWO) * clipped * clipped
    first_hat = first_new / (1.0 - BETA_ONE**STEPS)
    second_hat = second_new / (1.0 - BETA_TWO**STEPS)
    weight_new = weight - rate * (first_hat / (jnp.sqrt(second_hat) + ADAM_EPS) + DECAY * weight)
    return (weight_new, first_new, second_new)


def per_device(
    features,
    laplacian,
    endpoints,
    lengths,
    pairing,
    ident_weight,
    qkv_weight,
    out_weight,
    ffn_weight,
    norm_gains,
    ident_first,
    qkv_first,
    out_first,
    ffn_first,
    gains_first,
    ident_second,
    qkv_second,
    out_second,
    ffn_second,
    gains_second,
):
    place = Place()
    heads, head, dp = place.heads, place.head, place.dp
    tokens = features.shape[0] // heads
    graphs = tokens // LEN
    width = qkv_weight.shape[2]
    subs = width // SW
    own_columns = norm_gains.shape[1]

    small = jnp.concatenate([ident_weight, norm_gains], axis=0)
    small_rows = small.shape[0]
    small = place.gather_all(small.reshape(1, -1)).reshape(-1, small_rows, own_columns)
    small = small.transpose(1, 0, 2).reshape(small_rows, D)
    ident_full, gains = small[: 2 * LAP].astype(BF), small[2 * LAP :]

    packed = [qkv_weight[:, 0], qkv_weight[:, 1], qkv_weight[:, 2], out_weight.T]
    shards = [
        jnp.concatenate([m[:, s * SW : (s + 1) * SW] for m in packed], axis=1).astype(BF)
        for s in range(subs)
    ]
    packs = gather_attention(place, shards)
    ffn = ffn_weight.astype(BF)
    for bit in place.bits[1:][::-1]:
        ffn = place.gather_bit(ffn, bit, 0)
    ffn = place.gather_digit(ffn, "inner", 0)
    ffn = place.gather_digit(ffn, "outer", 0)
    ffn = place.gather_bit(ffn, place.bits[0], 1 + len(place.bits))
    lead = ffn.ndim - 3
    w_up = lax.index_in_dim(ffn, 0, lead, keepdims=False).reshape(D, -1)
    w_down = lax.index_in_dim(ffn, 1, lead, keepdims=False).reshape(D, -1)

    start_row = head * tokens
    lens = lax.dynamic_slice_in_dim(lengths.reshape(-1), head * graphs, graphs, 0)
    table_rows = lax.dynamic_slice_in_dim(laplacian, head * graphs * NODE, graphs * NODE, 0)
    end_rows = lax.dynamic_slice_in_dim(endpoints, start_row, tokens, 0)
    ident_rows = identifiers(table_rows, end_rows)
    embedded = lax.dynamic_slice_in_dim(features, start_row, tokens, 0).astype(F32)
    embedded = embedded + nn(ident_rows, ident_full)
    xhat_one, rstd_one = normalize(embedded)
    normed_one = (xhat_one * gains[0]).astype(BF)

    waves = [[(s, r), (s, r + 1)] for s in range(subs) for r in range(0, heads, 2)]
    stacks = [jnp.stack([packs[s][r] for s, r in wave]) for wave in waves]
    saved = [attend(lens, normed_one, w) for w in stacks]

    middle, slope, hsum, payload = forward_rest(
        lens, embedded, gains, w_up, w_down, [v[2] for v in saved], stacks
    )

    partner_slot = lax.dynamic_slice_in_dim(
        jnp.concatenate([pairing.reshape(-1)] * 2), head * graphs, graphs, 0
    ).astype(F32)
    payload = lax.dynamic_update_slice(payload, partner_slot[:, None], (0, D + 2))
    everyone = place.gather_all(payload).reshape(place.n, 2, GRAPHS_DEV, -1)
    hidden_sums = place.gather_all(hsum).reshape(-1, hsum.shape[-1])
    xhat = everyone[..., :D]
    summaries = xhat * gains[2]
    left, right = summaries[:, 0].reshape(-1, D), summaries[:, 1].reshape(-1, D)
    root_width = D**0.5
    logits = jnp.dot(left, right.T, precision=HIGHEST) / root_width
    row_totals, col_totals = log_total(logits, 1), log_total(logits, 0)
    count = logits.shape[0]
    group = jnp.arange(count, dtype=jnp.int32) // GRAPHS_DEV
    partner = group * GRAPHS_DEV + everyone[:, 0, :, D + 2].reshape(-1).astype(jnp.int32)
    positive = (partner[:, None] == jnp.arange(count, dtype=jnp.int32)[None, :]).astype(F32)
    total_loss = (
        jnp.sum(row_totals) + jnp.sum(col_totals) - 2.0 * jnp.sum(positive * logits)
    )
    d_logits = (
        jnp.exp(logits - row_totals[:, None])
        + jnp.exp(logits - col_totals[None, :])
        - 2.0 * positive
    )
    d_left = jnp.dot(d_logits, right, precision=HIGHEST) / root_width
    d_right = jnp.dot(d_logits.T, left, precision=HIGHEST) / root_width
    d_summary = jnp.stack(
        [d_left.reshape(place.n, GRAPHS_DEV, D), d_right.reshape(place.n, GRAPHS_DEV, D)], axis=1
    ).reshape(-1, D)
    xhat = xhat.reshape(-1, D)
    stats = everyone.reshape(-1, everyone.shape[-1])
    gain_three = jnp.sum(d_summary * xhat, axis=0)
    d_rows = norm_back(d_summary, xhat, stats[:, D : D + 1], gains[2]) * stats[:, D + 1 : D + 2]
    d_rows_low = d_rows.astype(BF)
    own_row = (dp * heads + head) * graphs
    d_out = lax.dynamic_slice_in_dim(d_rows, own_row, graphs, 0)
    d_hidden = nn(d_out.astype(BF), w_down)

    own_column = (dp * heads + head) * own_columns
    d_columns = lax.dynamic_slice_in_dim(d_rows_low, own_column, own_columns, 1)
    grad_down = tn(d_columns, hidden_sums)
    d_middle, d_attn, grad_up, gain_two = ffn_back(
        lens, middle, slope, d_out, d_hidden, gains, w_up
    )
    grad_up = place.reduce_all(grad_up, BF)
    order = sorted(range(len(waves)), key=lambda i: -waves[i][0][1])
    d_normed = 0.0
    by_sub = [dict() for _ in range(subs)]
    half = len(order) // 2
    for chosen in (order[:half], order[half:]):
        cat = lambda k: jnp.concatenate([saved[i][k] for i in chosen], axis=0)
        grads, d_part = attend_back(
            normed_one,
            d_attn,
            jnp.concatenate([stacks[i] for i in chosen], axis=0),
            [cat(k) for k in range(4)],
        )
        d_normed = d_normed + d_part
        for at, (s, r) in enumerate([pair for i in chosen for pair in waves[i]]):
            by_sub[s][r] = grads[at]
    grad_packs = [reduce_attention(place, s, by_sub[s]) for s in range(subs)]
    d_embedded = d_middle + norm_back(d_normed, xhat_one, rstd_one, gains[0])
    gain_one = jnp.sum(d_normed * xhat_one, axis=0)
    grad_ident = tn(ident_rows, d_embedded.astype(BF))
    rows = jnp.concatenate([grad_ident, gain_one[None], jnp.sum(gain_two, axis=0)[None]], axis=0)
    row_count = rows.shape[0]
    rows = rows.T.reshape(-1, own_columns * row_count)
    rows = place.reduce_all(rows, F32).reshape(own_columns, row_count).T
    grad_ident = rows[: 2 * LAP]
    grad_gains = jnp.concatenate(
        [rows[2 * LAP :], lax.dynamic_slice_in_dim(gain_three, own_column, own_columns, 0)[None]],
        axis=0,
    )
    columns = lambda j: jnp.concatenate([v[:, j * SW : (j + 1) * SW] for v in grad_packs], axis=1)
    grad_qkv = jnp.stack([columns(0), columns(1), columns(2)], axis=1)
    grad_out = columns(3).T
    grad_ffn = jnp.stack([grad_up.reshape(own_columns, -1), grad_down])

    grads = (grad_ident, grad_qkv, grad_out, grad_ffn, grad_gains)
    squares = sum((jnp.sum(gradient * gradient) for gradient in grads))
    grad_norm = jnp.sqrt(place.total(squares))
    factor = CLIP_AT / jnp.maximum(grad_norm, CLIP_AT)
    results = [
        adam_step(weight, gradient, first, second, factor, rate)
        for weight, gradient, first, second, rate in zip(
            (ident_weight, qkv_weight, out_weight, ffn_weight, norm_gains),
            grads,
            (ident_first, qkv_first, out_first, ffn_first, gains_first),
            (ident_second, qkv_second, out_second, ffn_second, gains_second),
            STEP_RATES,
        )
    ]
    return (grad_norm, total_loss) + tuple(r[k] for k in range(3) for r in results)


def solution(mesh):
    both = P(None, ("dp", "head"))
    weights = (both, P("dp", None, "head"), P("head", "dp"), P(None, ("dp", "head"), None), both)
    in_specs = (P("dp", None),) * 5 + weights * 3
    out_specs = (P(), P()) + weights * 3
    return jax.shard_map(
        per_device, mesh=mesh, in_specs=in_specs, out_specs=out_specs, check_vma=False
    )
```

time: 859 us -> 379 us (0.44)
  blocking collectives: 267 us -> 0 us
  waiting for transfers between devices: 307 us -> 75.1 us
  matrix products: 129 us -> 7.43 us
  Pallas kernels: 0 us -> 113 us
  starting transfers between devices: 0.37 us -> 77.4 us
  local copies, waits for them, and re-layouts: 75.6 us -> 29 us
    all_gather x5 -> x0, blocking collectives: 188 us -> none  [the longest x1 40.1 us: per_device(): lax.all_gather(norm_gains, ('dp', 'head'), axis=1, tiled=True)]
    unnamed x12 -> x0, waiting for transfers between devices: 185 us -> none
    reduce_scatter x3 -> x0, waiting for transfers between devices: 122 us -> none  [the longest x1 110 us: per_device(): lax.psum_scatter(jnp.stack([grad_up, grad_down]), ('dp', 'head'), scatter...]
    dot_general x24 -> x8, matrix products: 129 us -> 7.43 us  [the longest x2 2.98 us: nn(): lax.dot_general(a, b, (((1,), (0,)), ((), ())), preferred_element_type=F32)]
    pallas_call x0 -> x8, Pallas kernels: none -> 113 us  [the longest x2 60.7 us: attend_back(): pl.pallas_call(functools.partial(attend_back_kernel, graphs=tokens // LEN...]
    ppermute x0 -> x71, starting transfers between devices: none -> 77.4 us  [the longest x42 53.8 us: shift(): return lax.ppermute(v, 'dp', pairs)]
    ppermute x0 -> x71, waiting for transfers between devices: none -> 75.1 us  [the longest x42 50.8 us: shift(): return lax.ppermute(v, 'dp', pairs)]
    psum x1 -> x0, blocking collectives: 39.6 us -> none  [per_device(): lax.psum((jnp.sum(loss_terms), squares), ('dp', 'head'))]
  transfers between devices with their start and end apart: 9 -> 71, of which waited for: 5 -> 31; matrix products, arithmetic and copies ran while one was open for 23% -> 18% of each run, Pallas kernels for 0% -> 8%
where the time goes in v1:
time: 379 us; the launch traced here: 372 us
  Pallas kernels  113 us (30%)
  starting transfers between devices  77.4 us (20%)
  waiting for transfers between devices  75.1 us (20%)
  other arithmetic  57.2 us (15%)
  local copies, waits for them, and re-layouts  29 us (8%)
  between operations  13.5 us (4%)
  matrix products  7.43 us (2%)
    pallas_call x2, Pallas kernels, attend_back(): pl.pallas_call(functools.partial(attend_back_kernel, graphs=tokens // LEN...  60.7 us
    ppermute x42, starting transfers between devices, shift(): return lax.ppermute(v, 'dp', pairs)  53.8 us
    ppermute x42, waiting for transfers between devices, shift(): return lax.ppermute(v, 'dp', pairs)  50.8 us
    pallas_call x4, Pallas kernels, attend(): pl.pallas_call(functools.partial(attend_kernel, graphs=tokens // LEN), gr...  28.1 us
    ppermute x26, waiting for transfers between devices, swap(): return lax.ppermute(v, 'head', [(i, i ^ bit) for i in range(self.heads)])  19.1 us
    concatenate x8, other arithmetic, per_device(): cat = lambda k: jnp.concatenate([saved[i][k] for i in chosen], axis=0)  17.8 us
    ppermute x26, starting transfers between devices, swap(): return lax.ppermute(v, 'head', [(i, i ^ bit) for i in range(self.heads)])  17.2 us
    pallas_call x1, Pallas kernels, forward_rest(): pl.pallas_call(functools.partial(forward_kernel, tile_graphs=tile_graphs,...  15.4 us
  transfers between devices with their start and end apart: 71, of which 31 were waited for; matrix products, arithmetic and copies ran while one was open for 18% of the time, Pallas kernels for 8%

profile of v1, /device:TPU:0, one launch (start us, length us, event | category | flops | bytes accessed | tf_op | source)
XLA Modules:
  0.0 372.5 jit_solution(12371252967978308136)
XLA Ops:
  2.5 3.1 collective-permute-start
  14.7 3.4 collective-permute-start.19
  55.9 4.9 %collective-permute-done.8 = bf16[2,2,2,24,768]{4,3,1,0,2:T(8,128)(2,1)S(1)} collective-permute-done((bf16[2,2,2,24,768]{4,3,1,0,2:T(8,128)(2,1)S(1)}, bf16[2,2,2,24,768]{4,3,1,0,2:T(8,128)(2,1)S(1)}, u32[]{:S(2)}, u32[]{:S(2)}) %collective-permute-start.8) | collective-permute-done | bytes 294944 | tf_op jit(solution)/shard_map/ppermute | solution.py:434
  60.8 9.9 %collective-permute-done.9 = bf16[2,2,2,24,768]{4,3,1,0,2:T(8,128)(2,1)S(1)} collective-permute-done((bf16[2,2,2,24,768]{4,3,1,0,2:T(8,128)(2,1)S(1)}, bf16[2,2,2,24,768]{4,3,1,0,2:T(8,128)(2,1)S(1)}, u32[]{:S(2)}, u32[]{:S(2)}) %collective-permute-start.9) | collective-permute-done | bytes 294944 | tf_op jit(solution)/shard_map/ppermute | solution.py:434
  71.4 6.3 %collective-permute-done.25 = bf16[4,96,384]{2,1,0:T(8,128)(2,1)S(1)} collective-permute-done((bf16[4,96,384]{2,1,0:T(8,128)(2,1)S(1)}, bf16[4,96,384]{2,1,0:T(8,128)(2,1)S(1)}, u32[]{:S(2)}, u32[]{:S(2)}) %collective-permute-start.25) | collective-permute-done | bytes 294944 | tf_op jit(solution)/shard_map/ppermute | solution.py:434
  82.3 7.0 %attend.4 = (bf16[2,3,1024,128]{3,2,1,0:T(8,128)(2,1)}, bf16[2,1024,512]{2,1,0:T(8,128)(2,1)}, bf16[2,1024,128]{2,1,0:T(8,128)(2,1)}, f32[2,1024,128]{2,1,0:T(8,128)}) custom-call(s32[8]{0:T(128)} %dynamic_slice.138.lens_ref, bf16[1024,768]{1,0:T(8,128)(2,1)} %multiply_convert_fusion.x_ref, bf16[2,768,384]{2,1,0:T(8,128)(2,1)} %pad_maximum_fusion.9.w_ref.refs_4_), custom_call_target="tpu_custom_call" | custom-call | flops 5000000000 | bytes 6000000 | tf_op jit(solution)/shard_map/attend/pallas_call | solution.py:95
  89.3 7.1 %attend.6 = (bf16[2,3,1024,128]{3,2,1,0:T(8,128)(2,1)}, bf16[2,1024,512]{2,1,0:T(8,128)(2,1)}, bf16[2,1024,128]{2,1,0:T(8,128)(2,1)}, f32[2,1024,128]{2,1,0:T(8,128)}) custom-call(s32[8]{0:T(128)} %dynamic_slice.138.lens_ref, bf16[1024,768]{1,0:T(8,128)(2,1)} %multiply_convert_fusion.x_ref, bf16[2,768,384]{2,1,0:T(8,128)(2,1)} %pad_maximum_fusion.11.w_ref.refs_6_), custom_call_target="tpu_custom_call" | custom-call | flops 5000000000 | bytes 6000000 | tf_op jit(solution)/shard_map/attend/pallas_call | solution.py:95
  98.7 3.5 pad_maximum_fusion.3.qkv_ref
  104.2 3.1 pad_maximum_fusion.5.w_ref
  110.8 7.0 %attend.7 = (bf16[2,3,1024,128]{3,2,1,0:T(8,128)(2,1)}, bf16[2,1024,512]{2,1,0:T(8,128)(2,1)}, bf16[2,1024,128]{2,1,0:T(8,128)(2,1)}, f32[2,1024,128]{2,1,0:T(8,128)}) custom-call(s32[8]{0:T(128)} %dynamic_slice.138.lens_ref, bf16[1024,768]{1,0:T(8,128)(2,1)} %multiply_convert_fusion.x_ref, bf16[2,768,384]{2,1,0:T(8,128)(2,1)} %pad_maximum_fusion.12.w_ref.refs_7_), custom_call_target="tpu_custom_call" | custom-call | flops 5000000000 | bytes 6000000 | tf_op jit(solution)/shard_map/attend/pallas_call | solution.py:95
  118.9 7.1 %attend.5 = (bf16[2,3,1024,128]{3,2,1,0:T(8,128)(2,1)}, bf16[2,1024,512]{2,1,0:T(8,128)(2,1)}, bf16[2,1024,128]{2,1,0:T(8,128)(2,1)}, f32[2,1024,128]{2,1,0:T(8,128)}) custom-call(s32[8]{0:T(128)} %dynamic_slice.138.lens_ref, bf16[1024,768]{1,0:T(8,128)(2,1)} %multiply_convert_fusion.x_ref, bf16[2,768,384]{2,1,0:T(8,128)(2,1)} %pad_maximum_fusion.10.w_ref.refs_5_), custom_call_target="tpu_custom_call" | custom-call | flops 5000000000 | bytes 6000000 | tf_op jit(solution)/shard_map/attend/pallas_call | solution.py:95
  138.1 15.4 %forward_rest.1 = (f32[1024,768]{1,0:T(8,128)}, bf16[1024,768]{1,0:T(8,128)(2,1)}, bf16[8,768]{1,0:T(8,128)(2,1)}, f32[8,896]{1,0:T(8,128)}) custom-call(s32[8]{0:T(128)} %dynamic_slice.138.lens_ref, f32[1024,768]{1,0:T(8,128)} %copy-done.2, f32[3,768]{1,0:T(4,128)} %slice.136.gain_ref, bf16[768,768]{1,0:T(8,128)(2,1)} %bitcast.367, ...), custom_call_target="tpu_custom_call" | custom-call | flops 10000000000 | bytes 20000000 | tf_op jit(solution)/shard_map/forward_rest/pallas_call | solution.py:305
  156.9 3.4 collective-permute-start.28
  167.1 3.4 collective-permute-done.62
  179.3 3.0 collective-permute-done.31
  192.0 8.7 %ffn_back.1 = (f32[1024,768]{1,0:T(8,128)}, bf16[1024,768]{1,0:T(8,128)(2,1)}, bf16[768,768]{1,0:T(8,128)(2,1)}, f32[8,768]{1,0:T(8,128)}) custom-call(s32[8]{0:T(128)} %dynamic_slice.138.lens_ref, f32[1024,768]{1,0:T(8,128)} %get-tuple-element.49.mid_ref, bf16[1024,768]{1,0:T(8,128)(2,1)} %get-tuple-element.50.slope_ref, f32[8,768]{1,0:T(8,128)} %copy-done.36, ...), custom_call_target="tpu_custom_call" | custom-call | flops 10000000000 | bytes 15000000 | tf_op jit(solution)/shard_map/ffn_back/pallas_call | solution.py:387
  201.4 30.2 %attend_back.2 = (bf16[4,768,384]{2,1,0:T(8,128)(2,1)}, f32[1024,768]{1,0:T(8,128)}) custom-call(bf16[1024,768]{1,0:T(8,128)(2,1)} %multiply_convert_fusion.x_ref, bf16[1024,768]{1,0:T(8,128)(2,1)} %get-tuple-element.53.da_ref, bf16[4,768,384]{2,1,0:T(8,128)(2,1)} %pad_maximum_fusion.4.w_ref, bf16[4,3,1024,128]{3,2,1,0:T(8,128)(2,1)} %pad_maximum_fusion.2.qkv_ref, ...), custom_call_target="tpu_custom_call" | custom-call | flops 28000000000 | bytes 12000000 | tf_op jit(solution)/shard_map/attend_back/pallas_call | solution.py:189
  231.6 30.5 %attend_back.3 = (bf16[4,768,384]{2,1,0:T(8,128)(2,1)}, f32[1024,768]{1,0:T(8,128)}) custom-call(bf16[1024,768]{1,0:T(8,128)(2,1)} %multiply_convert_fusion.x_ref, bf16[1024,768]{1,0:T(8,128)(2,1)} %get-tuple-element.53.da_ref, bf16[4,768,384]{2,1,0:T(8,128)(2,1)} %pad_maximum_fusion.5.w_ref, bf16[4,3,1024,128]{3,2,1,0:T(8,128)(2,1)} %pad_maximum_fusion.3.qkv_ref, ...), custom_call_target="tpu_custom_call" | custom-call | flops 28000000000 | bytes 12000000 | tf_op jit(solution)/shard_map/attend_back/pallas_call | solution.py:189
  262.1 3.3 multiply_reduce_fusion.1
  298.4 4.5 %collective-permute-done.55 = bf16[4,2,24,768]{3,2,0,1:T(8,128)(2,1)S(1)} collective-permute-done((bf16[4,2,24,768]{3,2,0,1:T(8,128)(2,1)S(1)}, bf16[4,2,24,768]{3,2,0,1:T(8,128)(2,1)S(1)}, u32[]{:S(2)}, u32[]{:S(2)}) %collective-permute-start.55) | collective-permute-done | bytes 294944 | tf_op jit(solution)/shard_map/ppermute | solution.py:422
  305.4 3.9 %collective-permute-done.56 = bf16[4,24,768]{2,1,0:T(8,128)(2,1)S(1)} collective-permute-done((bf16[4,24,768]{2,1,0:T(8,128)(2,1)S(1)}, bf16[4,24,768]{2,1,0:T(8,128)(2,1)S(1)}, u32[]{:S(2)}, u32[]{:S(2)}) %collective-permute-start.56) | collective-permute-done | bytes 147488 | tf_op jit(solution)/shard_map/ppermute | solution.py:434
  312.5 3.0 collective-permute-done.41
  325.9 5.2 %collective-permute-done.52 = bf16[96,384]{1,0:T(8,128)(2,1)S(1)} collective-permute-done((bf16[96,384]{1,0:T(8,128)(2,1)S(1)}, bf16[96,384]{1,0:T(8,128)(2,1)S(1)}, u32[]{:S(2)}, u32[]{:S(2)}) %collective-permute-start.52) | collective-permute-done | bytes 73760 | tf_op jit(solution)/shard_map/ppermute | solution.py:434
  335.7 3.7 collective-permute-done.44
  (437 shorter events, 178.6 us)
Async XLA Ops:
  11.8 17.3 %collective-permute-start.12 = (bf16[96,384]{0,1:T(8,128)(2,1)S(1)}, bf16[96,384]{0,1:T(8,128)(2,1)S(1)}, u32[]{:S(2)}, u32[]{:S(2)}) collective-permute-start(bf16[96,384]{0,1:T(8,128)(2,1)S(1)} %pad_maximum_fusion.25), channel_id=1, source_target_pairs={{0,8},{4,12},{8,16},{12,20},{16,24},{20,28},{24,0},{28,4},{1,9},{5... | collective-permute-start | bytes 221192 | tf_op jit(solution)/shard_map/ppermute | solution.py:434
  12.6 24.2 %collective-permute-start.13 = (bf16[96,384]{0,1:T(8,128)(2,1)S(1)}, bf16[96,384]{0,1:T(8,128)(2,1)S(1)}, u32[]{:S(2)}, u32[]{:S(2)}) collective-permute-start(bf16[96,384]{0,1:T(8,128)(2,1)S(1)} %pad_maximum_fusion.25), channel_id=1, source_target_pairs={{0,16},{4,20},{8,24},{12,28},{16,0},{20,4},{24,8},{28,12},{1,17},{... | collective-permute-start | bytes 221192 | tf_op jit(solution)/shard_map/ppermute | solution.py:434
  14.7 16.6 %collective-permute-start.19 = (bf16[96,384]{0,1:T(8,128)(2,1)S(1)}, bf16[96,384]{0,1:T(8,128)(2,1)S(1)}, u32[]{:S(2)}, u32[]{:S(2)}) collective-permute-start(bf16[96,384]{0,1:T(8,128)(2,1)S(1)} %pad_maximum_fusion.27), channel_id=1, source_target_pairs={{0,8},{4,12},{8,16},{12,20},{16,24},{20,28},{24,0},{28,4},{1,9},{5... | collective-permute-start | bytes 221192 | tf_op jit(solution)/shard_map/ppermute | solution.py:434
  18.1 14.3 %collective-permute-start.20 = (bf16[96,384]{0,1:T(8,128)(2,1)S(1)}, bf16[96,384]{0,1:T(8,128)(2,1)S(1)}, u32[]{:S(2)}, u32[]{:S(2)}) collective-permute-start(bf16[96,384]{0,1:T(8,128)(2,1)S(1)} %pad_maximum_fusion.27), channel_id=1, source_target_pairs={{0,16},{4,20},{8,24},{12,28},{16,0},{20,4},{24,8},{28,12},{1,17},{... | collective-permute-start | bytes 221192 | tf_op jit(solution)/shard_map/ppermute | solution.py:434
  32.8 21.1 %collective-permute-start.22 = (bf16[4,96,384]{2,1,0:T(8,128)(2,1)S(1)}, bf16[4,96,384]{2,1,0:T(8,128)(2,1)S(1)}, u32[]{:S(2)}, u32[]{:S(2)}) collective-permute-start(bf16[4,96,384]{2,1,0:T(8,128)(2,1)S(1)} %constant_dynamic-update-slice_fusion.4), channel_id=1, source_target_pairs={{0,4},{4,0},{8,12},{12,8},{16,20},{20,16},{24,28},{28,24},{1,5},{5... | collective-permute-start | bytes 884744 | tf_op jit(solution)/shard_map/ppermute | solution.py:434
  35.7 19.0 %collective-permute-start.24 = (bf16[4,96,384]{2,1,0:T(8,128)(2,1)S(1)}, bf16[4,96,384]{2,1,0:T(8,128)(2,1)S(1)}, u32[]{:S(2)}, u32[]{:S(2)}) collective-permute-start(bf16[4,96,384]{2,1,0:T(8,128)(2,1)S(1)} %constant_dynamic-update-slice_fusion.4), channel_id=1, source_target_pairs={{0,2},{1,3},{2,0},{3,1},{4,6},{5,7},{6,4},{7,5},{8,10},{9,11},{10,... | collective-permute-start | bytes 884744 | tf_op jit(solution)/shard_map/ppermute | solution.py:422
  49.0 21.7 %collective-permute-start.9 = (bf16[2,2,2,24,768]{4,3,1,0,2:T(8,128)(2,1)S(1)}, bf16[2,2,2,24,768]{4,3,1,0,2:T(8,128)(2,1)S(1)}, u32[]{:S(2)}, u32[]{:S(2)}) collective-permute-start(bf16[2,2,2,24,768]{4,3,1,0,2:T(8,128)(2,1)S(1)} %copy_dynamic-update-slice_fusion), channel_id=1, source_target_pairs={{0,16},{4,20},{8,24},{12,28},{16,0},{20,4},{24,8},{28,12},{1,17},{... | collective-permute-start | bytes 884744 | tf_op jit(solution)/shard_map/ppermute | solution.py:434
  51.8 19.5 %collective-permute-start.10 = (bf16[2,2,2,24,768]{4,3,1,0,2:T(8,128)(2,1)S(1)}, bf16[2,2,2,24,768]{4,3,1,0,2:T(8,128)(2,1)S(1)}, u32[]{:S(2)}, u32[]{:S(2)}) collective-permute-start(bf16[2,2,2,24,768]{4,3,1,0,2:T(8,128)(2,1)S(1)} %copy_dynamic-update-slice_fusion), channel_id=1, source_target_pairs={{0,24},{4,28},{8,0},{12,4},{16,8},{20,12},{24,16},{28,20},{1,25},{... | collective-permute-start | bytes 884744 | tf_op jit(solution)/shard_map/ppermute | solution.py:434
  53.9 23.9 %collective-permute-start.16 = (bf16[4,2,96,384]{3,2,1,0:T(8,128)(2,1)}, bf16[4,2,96,384]{3,2,1,0:T(8,128)(2,1)S(1)}, u32[]{:S(2)}, u32[]{:S(2)}) collective-permute-start(bf16[4,2,96,384]{3,2,1,0:T(8,128)(2,1)} %bitcast_dynamic-update-slice_fusion.3), channel_id=1, source_target_pairs={{0,1},{1,0},{2,3},{3,2},{4,5},{5,4},{6,7},{7,6},{8,9},{9,8},{10,11... | collective-permute-start | bytes 1769480 | tf_op jit(solution)/shard_map/ppermute | solution.py:422
  54.7 47.5 %collective-permute-start.17 = (bf16[4,2,96,384]{3,2,1,0:T(8,128)(2,1)}, bf16[4,2,96,384]{3,2,1,0:T(8,128)(2,1)S(1)}, u32[]{:S(2)}, u32[]{:S(2)}) collective-permute-start(bf16[4,2,96,384]{3,2,1,0:T(8,128)(2,1)} %bitcast_dynamic-update-slice_fusion.3), channel_id=1, source_target_pairs={{0,2},{1,3},{2,0},{3,1},{4,6},{5,7},{6,4},{7,5},{8,10},{9,11},{10,... | collective-permute-start | bytes 1769480 | tf_op jit(solution)/shard_map/ppermute | solution.py:422
  60.7 19.3 %collective-permute-start.23 = (bf16[4,2,96,384]{3,2,1,0:T(8,128)(2,1)}, bf16[4,2,96,384]{3,2,1,0:T(8,128)(2,1)S(1)}, u32[]{:S(2)}, u32[]{:S(2)}) collective-permute-start(bf16[4,2,96,384]{3,2,1,0:T(8,128)(2,1)} %bitcast_dynamic-update-slice_fusion.8), channel_id=1, source_target_pairs={{0,1},{1,0},{2,3},{3,2},{4,5},{5,4},{6,7},{7,6},{8,9},{9,8},{10,11... | collective-permute-start | bytes 1769480 | tf_op jit(solution)/shard_map/ppermute | solution.py:422
  71.3 65.0 %collective-permute-start.11 = (bf16[4,2,2,2,24,768]{5,4,2,1,0,3:T(8,128)(2,1)S(1)}, bf16[4,2,2,2,24,768]{5,4,2,1,0,3:T(8,128)(2,1)S(1)}, u32[]{:S(2)}, u32[]{:S(2)}) collective-permute-start(bf16[4,2,2,2,24,768]{5,4,2,1,0,3:T(8,128)(2,1)S(1)} %bitcast_dynamic-update-slice_fusion.9), channel_id=1, source_target_pairs={{0,1},{1,0},{2,3},{3,2},{4,5},{5,4},{6,7},{7,6},{8,9},{9,8},{10,11... | collective-permute-start | bytes 3538952 | tf_op jit(solution)/shard_map/ppermute | solution.py:422
  77.8 31.9 %collective-permute-start.26 = (bf16[4,2,96,384]{3,2,1,0:T(8,128)(2,1)S(1)}, bf16[4,2,96,384]{3,2,1,0:T(8,128)(2,1)S(1)}, u32[]{:S(2)}, u32[]{:S(2)}) collective-permute-start(bf16[4,2,96,384]{3,2,1,0:T(8,128)(2,1)S(1)} %bitcast_dynamic-update-slice_fusion), channel_id=1, source_target_pairs={{0,1},{1,0},{2,3},{3,2},{4,5},{5,4},{6,7},{7,6},{8,9},{9,8},{10,11... | collective-permute-start | bytes 1769480 | tf_op jit(solution)/shard_map/ppermute | solution.py:422
  102.2 15.6 %collective-permute-start.18 = (bf16[4,2,96,384]{3,2,1,0:T(8,128)(2,1)S(1)}, bf16[4,2,96,384]{3,2,1,0:T(8,128)(2,1)S(1)}, u32[]{:S(2)}, u32[]{:S(2)}) collective-permute-start(bf16[4,2,96,384]{3,2,1,0:T(8,128)(2,1)S(1)} %collective-permute-done.17), channel_id=1, source_target_pairs={{0,1},{1,0},{2,3},{3,2},{4,5},{5,4},{6,7},{7,6},{8,9},{9,8},{10,11... | collective-permute-start | bytes 1769480 | tf_op jit(solution)/shard_map/ppermute | solution.py:422
  154.9 16.4 %collective-permute-start.27 = (f32[8,896]{1,0:T(8,128)}, f32[8,896]{1,0:T(8,128)S(1)}, u32[]{:S(2)}, u32[]{:S(2)}) collective-permute-start(f32[8,896]{1,0:T(8,128)} %dynamic_update_slice.153), channel_id=1, source_target_pairs={{0,8},{4,12},{8,16},{12,20},{16,24},{20,28},{24,0},{28,4},{1,9},{5... | collective-permute-start | bytes 86024 | tf_op jit(solution)/shard_map/ppermute | solution.py:434
  156.9 14.4 %collective-permute-start.28 = (f32[8,896]{1,0:T(8,128)}, f32[8,896]{1,0:T(8,128)S(1)}, u32[]{:S(2)}, u32[]{:S(2)}) collective-permute-start(f32[8,896]{1,0:T(8,128)} %dynamic_update_slice.153), channel_id=1, source_target_pairs={{0,16},{4,20},{8,24},{12,28},{16,0},{20,4},{24,8},{28,12},{1,17},{... | collective-permute-start | bytes 86024 | tf_op jit(solution)/shard_map/ppermute | solution.py:434
  270.6 18.5 %collective-permute-start.48 = (bf16[4,2,96,384]{3,2,1,0:T(8,128)(2,1)}, bf16[4,2,96,384]{3,2,1,0:T(8,128)(2,1)}, u32[]{:S(2)}, u32[]{:S(2)}) collective-permute-start(bf16[4,2,96,384]{3,2,1,0:T(8,128)(2,1)} %bitcast.121), channel_id=1, source_target_pairs={{0,1},{1,0},{2,3},{3,2},{4,5},{5,4},{6,7},{7,6},{8,9},{9,8},{10,11... | collective-permute-start | bytes 1769480 | tf_op jit(solution)/shard_map/ppermute | solution.py:422
  272.3 21.9 %collective-permute-start.46 = (bf16[4,2,96,384]{3,2,1,0:T(8,128)(2,1)}, bf16[4,2,96,384]{3,2,1,0:T(8,128)(2,1)}, u32[]{:S(2)}, u32[]{:S(2)}) collective-permute-start(bf16[4,2,96,384]{3,2,1,0:T(8,128)(2,1)} %bitcast.117), channel_id=1, source_target_pairs={{0,1},{1,0},{2,3},{3,2},{4,5},{5,4},{6,7},{7,6},{8,9},{9,8},{10,11... | collective-permute-start | bytes 1769480 | tf_op jit(solution)/shard_map/ppermute | solution.py:422
  286.7 24.7 %collective-permute-start.39 = (bf16[4,2,96,384]{3,2,1,0:T(8,128)(2,1)}, bf16[4,2,96,384]{3,2,1,0:T(8,128)(2,1)}, u32[]{:S(2)}, u32[]{:S(2)}) collective-permute-start(bf16[4,2,96,384]{3,2,1,0:T(8,128)(2,1)} %bitcast.371), channel_id=1, source_target_pairs={{0,1},{1,0},{2,3},{3,2},{4,5},{5,4},{6,7},{7,6},{8,9},{9,8},{10,11... | collective-permute-start | bytes 1769480 | tf_op jit(solution)/shard_map/ppermute | solution.py:422
  290.4 13.4 %collective-permute-start.49 = (bf16[4,96,384]{2,1,0:T(8,128)(2,1)S(1)}, bf16[4,96,384]{2,1,0:T(8,128)(2,1)S(1)}, u32[]{:S(2)}, u32[]{:S(2)}) collective-permute-start(bf16[4,96,384]{2,1,0:T(8,128)(2,1)S(1)} %dynamic-slice_bitcast_fusion.1), channel_id=1, source_target_pairs={{0,4},{4,0},{8,12},{12,8},{16,20},{20,16},{24,28},{28,24},{1,5},{5... | collective-permute-start | bytes 884744 | tf_op jit(solution)/shard_map/ppermute | solution.py:434
  295.4 23.3 %collective-permute-start.47 = (bf16[4,96,384]{2,1,0:T(8,128)(2,1)S(1)}, bf16[4,96,384]{2,1,0:T(8,128)(2,1)S(1)}, u32[]{:S(2)}, u32[]{:S(2)}) collective-permute-start(bf16[4,96,384]{2,1,0:T(8,128)(2,1)S(1)} %dynamic-slice_bitcast_fusion.2), channel_id=1, source_target_pairs={{0,4},{4,0},{8,12},{12,8},{16,20},{20,16},{24,28},{28,24},{1,5},{5... | collective-permute-start | bytes 884744 | tf_op jit(solution)/shard_map/ppermute | solution.py:434
  297.8 17.7 %collective-permute-start.41 = (bf16[4,2,96,384]{3,2,1,0:T(8,128)(2,1)S(1)}, bf16[4,2,96,384]{3,2,1,0:T(8,128)(2,1)S(1)}, u32[]{:S(2)}, u32[]{:S(2)}) collective-permute-start(bf16[4,2,96,384]{3,2,1,0:T(8,128)(2,1)S(1)} %fusion.3), channel_id=1, source_target_pairs={{0,2},{1,3},{2,0},{3,1},{4,6},{5,7},{6,4},{7,5},{8,10},{9,11},{10,... | collective-permute-start | bytes 1769480 | tf_op jit(solution)/shard_map/ppermute | solution.py:422
  303.9 17.2 %collective-permute-start.50 = (bf16[4,96,384]{2,1,0:T(8,128)(2,1)S(1)}, bf16[4,96,384]{2,1,0:T(8,128)(2,1)S(1)}, u32[]{:S(2)}, u32[]{:S(2)}) collective-permute-start(bf16[4,96,384]{2,1,0:T(8,128)(2,1)S(1)} %fusion.13), channel_id=1, source_target_pairs={{0,2},{1,3},{2,0},{3,1},{4,6},{5,7},{6,4},{7,5},{8,10},{9,11},{10,... | collective-permute-start | bytes 884744 | tf_op jit(solution)/shard_map/ppermute | solution.py:422
  309.4 13.9 %collective-permute-start.59 = (bf16[24,768]{1,0:T(8,128)(2,1)S(1)}, bf16[24,768]{1,0:T(8,128)(2,1)S(1)}, u32[]{:S(2)}, u32[]{:S(2)}) collective-permute-start(bf16[24,768]{1,0:T(8,128)(2,1)S(1)} %get-tuple-element.212), channel_id=1, source_target_pairs={{0,24},{4,28},{8,0},{12,4},{16,8},{20,12},{24,16},{28,20},{1,25},{... | collective-permute-start | bytes 110600 | tf_op jit(solution)/shard_map/ppermute | solution.py:434
  (92 other events, 1049.2 us)

commit v2 on v1

v2 whole, which is shorter than its diff:
```python
import functools

import jax
import jax.numpy as jnp
from jax import lax
from jax.experimental import pallas as pl
from jax.experimental.pallas import tpu as pltpu
from jax.sharding import PartitionSpec as P

D = 768
HEAD_DIM = 24
LAP = 16
LEN = 128
NODE = 32
STEPS = 3
GRAPHS_DEV = 16

HIGHEST = lax.Precision.HIGHEST
NORM_EPS = 1e-05
CLIP_AT = 5.0
STEP_RATES = (0.08, 0.02, 0.15, 0.02, 0.5)
BETA_ONE = 0.5
BETA_TWO = 0.5
DECAY = 0.01
ADAM_EPS = 1e-08
MASKED = -1e30

BF = jnp.bfloat16
F32 = jnp.float32
SUB = 4
SW = SUB * HEAD_DIM
PACK = 4 * SW
V_AT = 128 - SW
SCALE = HEAD_DIM ** (-0.5)
VMEM_LIMIT = 44 * 2**20


def nn(a, b):
    return lax.dot_general(a, b, (((1,), (0,)), ((), ())), preferred_element_type=F32)


def nt(a, b):
    return lax.dot_general(a, b, (((1,), (1,)), ((), ())), preferred_element_type=F32)


def tn(a, b):
    return lax.dot_general(a, b, (((0,), (0,)), ((), ())), preferred_element_type=F32)


def lanes():
    return lax.broadcasted_iota(jnp.int32, (1, 128), 1)


def head_lanes(h, at):
    lane = lanes()
    return (lane >= at + h * HEAD_DIM) & (lane < at + (h + 1) * HEAD_DIM)


def by_head(v, at):
    zero = jnp.zeros_like(v)
    return jnp.concatenate([jnp.where(head_lanes(h, at), v, zero) for h in range(SUB)], axis=0)


def stack_heads(v):
    return jnp.concatenate([v[:, h * LEN : (h + 1) * LEN] for h in range(SUB)], axis=0)


def attend_kernel(lens_ref, x_ref, w_ref, qkv_ref, p_ref, o_ref, rinv_ref, *, graphs):
    y = nn(x_ref[...], w_ref[0])
    qkv_ref[0, 0] = y[:, :128].astype(BF)
    qkv_ref[0, 1] = pltpu.roll(y, PACK - SW, 1)[:, :128].astype(BF)
    qkv_ref[0, 2] = pltpu.roll(y, SW, 1)[:, 256:].astype(BF)
    col = lanes()
    ones = by_head(jnp.ones((LEN, 128), BF), V_AT)
    for g in range(graphs):
        rows = slice(g * LEN, (g + 1) * LEN)
        query, keys, values = qkv_ref[0, 0, rows, :], qkv_ref[0, 1, rows, :], qkv_ref[0, 2, rows, :]
        live = col < lens_ref[g]
        scores = nt(query, by_head(keys, 0))
        parts = []
        for h in range(SUB):
            own = jnp.where(live, scores[:, h * LEN : (h + 1) * LEN] * SCALE, MASKED)
            parts.append(jnp.exp(own - jnp.max(own, axis=1, keepdims=True)).astype(BF))
        expo = jnp.concatenate(parts, axis=1)
        both = nn(expo, jnp.concatenate([by_head(values, V_AT), ones], axis=1))
        rinv = jnp.where(col >= V_AT, 1.0 / both[:, 128:], 0.0)
        p_ref[0, rows, :] = expo
        rinv_ref[0, rows, :] = rinv
        o_ref[0, rows, :] = jnp.where(col >= V_AT, both[:, :128] * rinv, 0.0).astype(BF)


def attend(lens, x, w):
    tokens, groups = x.shape[0], w.shape[0]
    block = lambda *tail: pl.BlockSpec((1,) + tail, lambda i: (i,) + (0,) * len(tail))
    return pl.pallas_call(
        functools.partial(attend_kernel, graphs=tokens // LEN),
        grid=(groups,),
        in_specs=[
            pl.BlockSpec(memory_space=pltpu.SMEM),
            pl.BlockSpec((tokens, D), lambda i: (0, 0)),
            block(D, PACK),
        ],
        out_specs=[block(3, tokens, 128), block(tokens, 512), block(tokens, 128), block(tokens, 128)],
        out_shape=[
            jax.ShapeDtypeStruct((groups, 3, tokens, 128), BF),
            jax.ShapeDtypeStruct((groups, tokens, 512), BF),
            jax.ShapeDtypeStruct((groups, tokens, 128), BF),
            jax.ShapeDtypeStruct((groups, tokens, 128), F32),
        ],
        compiler_params=pltpu.CompilerParams(vmem_limit_bytes=VMEM_LIMIT),
        cost_estimate=pl.CostEstimate(
            flops=groups * 2_500_000_000, bytes_accessed=groups * 3_000_000, transcendentals=0
        ),
        name="attend",
    )(lens, x, w)


def attend_back_kernel(
    xt_ref, dt_ref, da_ref, w_ref, qkv_ref, p_ref, o_ref, rinv_ref, g_ref, d_ref, aug, *, graphs
):
    w = w_ref[0]
    lane = lanes()
    d_out = jnp.where(lane >= V_AT, nn(da_ref[...], w[:, 256:]) * rinv_ref[0], 0.0)
    heads_out = o_ref[0]
    terms = d_out * heads_out.astype(F32)
    high, low = two_parts(terms)
    row = lax.broadcasted_iota(jnp.int32, (128, 128), 0)
    column = lax.broadcasted_iota(jnp.int32, (128, 128), 1)
    pick = jnp.zeros((128, 128), BF)
    for h in range(SUB):
        inside = (row >= V_AT + h * HEAD_DIM) & (row < V_AT + (h + 1) * HEAD_DIM)
        pick = jnp.where(inside & ((column == h) | (column == SUB + h)), jnp.ones_like(pick), pick)
    delta = nn(high, pick) + nn(low, pick)
    rounded = delta.astype(BF).astype(F32)
    aug[...] = jnp.where(
        lane >= V_AT, d_out, jnp.where(lane < SUB, -rounded, rounded - delta)
    ).astype(BF)
    for g in range(graphs):
        rows = slice(g * LEN, (g + 1) * LEN)
        query, keys, values = qkv_ref[0, 0, rows, :], qkv_ref[0, 1, rows, :], qkv_ref[0, 2, rows, :]
        d_rows, expo = aug[rows, :], p_ref[0, rows, :]
        one, zero = jnp.ones_like(values), jnp.zeros_like(values)
        spread = jnp.concatenate(
            [
                jnp.where(
                    head_lanes(h, V_AT), values, jnp.where((lane == h) | (lane == SUB + h), one, zero)
                )
                for h in range(SUB)
            ],
            axis=0,
        )
        d_scores = (expo.astype(F32) * nt(d_rows, spread)).astype(BF)
        d_query = nn(d_scores, by_head(keys, 0)) * SCALE
        d_keys = tn(stack_heads(d_scores), by_head(query, 0)) * SCALE
        d_values = tn(stack_heads(expo), by_head(d_rows, V_AT))
        rolled_keys, rolled_values = pltpu.roll(d_keys, SW, 1), pltpu.roll(d_values, V_AT, 1)
        d_ref[0, rows, 0:128] = jnp.where(lane < SW, d_query, rolled_keys).astype(BF)
        d_ref[0, rows, 128:256] = jnp.where(lane < 64, rolled_keys, rolled_values).astype(BF)
        d_ref[0, rows, 256:384] = jnp.where(lane < V_AT, rolled_values, 0.0).astype(BF)
    grad = nn(xt_ref[...], d_ref[0])
    grad_out = nn(dt_ref[...], heads_out)
    g_ref[0, :, 0:256] = grad[:, 0:256].astype(BF)
    g_ref[0, :, 256:384] = (grad[:, 256:384] + grad_out).astype(BF)


def attend_back(xt, dt, d_attn, w, saved, first, stride, groups):
    qkv, expo, heads_out, rinv = saved
    tokens = d_attn.shape[0]
    block = lambda *tail: pl.BlockSpec(
        (1,) + tail, lambda i: (first + i * stride,) + (0,) * len(tail)
    )
    out = lambda *tail: pl.BlockSpec((1,) + tail, lambda i: (i,) + (0,) * len(tail))
    full = lambda a: pl.BlockSpec(a.shape, lambda i: (0,) * a.ndim)
    return pl.pallas_call(
        functools.partial(attend_back_kernel, graphs=tokens // LEN),
        grid=(groups,),
        in_specs=[
            full(xt),
            full(dt),
            full(d_attn),
            block(D, PACK),
            block(3, tokens, 128),
            block(tokens, 512),
            block(tokens, 128),
            block(tokens, 128),
        ],
        out_specs=[out(D, PACK), out(tokens, PACK)],
        out_shape=[
            jax.ShapeDtypeStruct((groups, D, PACK), BF),
            jax.ShapeDtypeStruct((groups, tokens, PACK), BF),
        ],
        scratch_shapes=[pltpu.VMEM((tokens, 128), BF)],
        compiler_params=pltpu.CompilerParams(vmem_limit_bytes=VMEM_LIMIT),
        cost_estimate=pl.CostEstimate(
            flops=groups * 6_000_000_000, bytes_accessed=groups * 3_000_000, transcendentals=0
        ),
        name="attend_back",
    )(xt, dt, d_attn, w, qkv, expo, heads_out, rinv)


def first_back_kernel(e_ref, dmid_ref, ident_ref, gain_ref, *refs, parts):
    d_refs, w_refs = refs[: len(parts)], refs[len(parts) : -2]
    out_ref, acc = refs[-2:]
    step, steps = pl.program_id(0), pl.num_programs(0)
    d_normed = jnp.zeros(e_ref.shape, F32)
    for d_ref, (which, picks) in zip(d_refs, parts):
        for j, at in enumerate(picks):
            d_normed = d_normed + nt(d_ref[j], w_refs[which][at])
    xhat, rstd = normalize(e_ref[...])
    d_emb = dmid_ref[...] + norm_back(d_normed, xhat, rstd, gain_ref[0:1, :])
    part = tn(ident_ref[...], d_emb.astype(BF))
    part_gain = jnp.sum((d_normed * xhat).reshape(-1, 8, D), axis=0)

    @pl.when(step == 0)
    def _():
        acc[0 : 2 * LAP, :] = part
        acc[2 * LAP :, :] = part_gain

    @pl.when(step > 0)
    def _():
        acc[0 : 2 * LAP, :] += part
        acc[2 * LAP :, :] += part_gain

    @pl.when(step == steps - 1)
    def _():
        out_ref[...] = acc[...]


def first_back(embedded, d_middle, ident_rows, gains, ds, parts, weights):
    tokens = embedded.shape[0]
    rows = LEN * min(2, tokens // LEN)
    full = lambda a: pl.BlockSpec(a.shape, lambda i: (0,) * a.ndim)
    tile = pl.BlockSpec((rows, D), lambda i: (i, 0))
    return pl.pallas_call(
        functools.partial(first_back_kernel, parts=parts),
        grid=(tokens // rows,),
        in_specs=[tile, tile, pl.BlockSpec((rows, 2 * LAP), lambda i: (i, 0)), full(gains)]
        + [pl.BlockSpec((d.shape[0], rows, PACK), lambda i: (0, i, 0)) for d in ds]
        + [full(w) for w in weights],
        out_specs=pl.BlockSpec((2 * LAP + 8, D), lambda i: (0, 0)),
        out_shape=jax.ShapeDtypeStruct((2 * LAP + 8, D), F32),
        scratch_shapes=[pltpu.VMEM((2 * LAP + 8, D), F32)],
        compiler_params=pltpu.CompilerParams(vmem_limit_bytes=VMEM_LIMIT),
        cost_estimate=pl.CostEstimate(
            flops=8_000_000_000, bytes_accessed=15_000_000, transcendentals=0
        ),
        name="first_back",
    )(embedded, d_middle, ident_rows, gains, *ds, *weights)


def erf(x):
    x = jnp.clip(x, -3.832506856900711, 3.832506856900711)
    x2 = x * x
    top = 0.00022905065861350646
    for c in (
        0.0034082910107109506,
        0.050955695062380861,
        0.18520832239976145,
        1.128379143519084,
    ):
        top = top * x2 + c
    bottom = -1.1791602954361697e-7
    for c in (
        0.000023547966471313185,
        0.0010179625278914885,
        0.014070470171167667,
        0.11098505178285362,
        0.49746925110067538,
        1.0,
    ):
        bottom = bottom * x2 + c
    return x * top / bottom


def normalize(values):
    centred = values - jnp.mean(values, axis=-1, keepdims=True)
    spread = jnp.mean(centred * centred, axis=-1, keepdims=True)
    rstd = lax.rsqrt(spread + NORM_EPS)
    return centred * rstd, rstd


def two_parts(v):
    high = v.astype(BF)
    return high, (v - high.astype(F32)).astype(BF)


def forward_kernel(
    lens_ref, partner_ref, e_ref, gain_ref, up_ref, down_ref, *refs, tile_graphs, waves, groups
):
    o_refs, w_refs = refs[:waves], refs[waves : 2 * waves]
    mid_ref, slope_ref, pay_ref, hsum, msum = refs[2 * waves :]
    step, steps = pl.program_id(0), pl.num_programs(0)
    middle = e_ref[...]
    for wave in range(waves):
        left = jnp.concatenate([o_refs[wave][j] for j in range(groups)], axis=1)
        right = jnp.concatenate([w_refs[wave][j][:, 256:] for j in range(groups)], axis=1)
        middle = middle + nt(left, right)
    mid_ref[...] = middle
    xhat, _ = normalize(middle)
    up = nn((xhat * gain_ref[1:2, :]).astype(BF), up_ref[...])
    cdf = 0.5 + 0.5 * erf(up * (0.5**0.5))
    hidden = (up * cdf).astype(BF).astype(F32)
    slope_ref[...] = (cdf + up * (0.3989422804014327 * jnp.exp(-0.5 * up * up))).astype(BF)
    place = lax.broadcasted_iota(jnp.int32, (LEN, 1), 0)
    for j in range(tile_graphs):
        g = step * tile_graphs + j
        live = place < lens_ref[g]
        rows = slice(j * LEN, (j + 1) * LEN)
        hsum[pl.ds(g, 1), :] = jnp.sum(jnp.where(live, hidden[rows], 0.0), axis=0, keepdims=True)
        msum[pl.ds(g, 1), :] = jnp.sum(jnp.where(live, middle[rows], 0.0), axis=0, keepdims=True)

    @pl.when(step == steps - 1)
    def _():
        graphs = hsum.shape[0]
        high, low = two_parts(hsum[...])
        which = lax.broadcasted_iota(jnp.int32, (graphs, 1), 0)
        length, partner = jnp.ones((graphs, 1), F32), jnp.zeros((graphs, 1), F32)
        for g in range(graphs):
            length = jnp.where(which == g, lens_ref[g].astype(F32), length)
            partner = jnp.where(which == g, partner_ref[g].astype(F32), partner)
        pooled = (msum[...] + (nt(high, down_ref[...]) + nt(low, down_ref[...]))) / length
        xhat_pool, rstd = normalize(pooled)
        high, low = two_parts(xhat_pool)
        pay_ref[:, 0:D] = high
        pay_ref[:, D : 2 * D] = low
        pay_ref[:, 2 * D : 3 * D] = hsum[...].astype(BF)
        lane = lanes()
        stats = jnp.zeros((graphs, 128), F32)
        for at, value in enumerate(two_parts(rstd) + two_parts(1.0 / length) + (partner,)):
            stats = jnp.where(lane == at, value.astype(F32), stats)
        pay_ref[:, 3 * D :] = stats.astype(BF)


def forward_rest(lens, partner, embedded, gains, w_up, w_down, outs, weights):
    tokens = embedded.shape[0]
    graphs = tokens // LEN
    tile_graphs = min(2, graphs)
    rows = tile_graphs * LEN
    waves, groups = len(outs), outs[0].shape[0]
    full = lambda a: pl.BlockSpec(a.shape, lambda i: (0,) * a.ndim)
    tile = pl.BlockSpec((rows, D), lambda i: (i, 0))
    return pl.pallas_call(
        functools.partial(forward_kernel, tile_graphs=tile_graphs, waves=waves, groups=groups),
        grid=(tokens // rows,),
        in_specs=[pl.BlockSpec(memory_space=pltpu.SMEM)] * 2
        + [tile, full(gains), full(w_up), full(w_down)]
        + [pl.BlockSpec((groups, rows, 128), lambda i: (0, i, 0)) for _ in outs]
        + [full(w) for w in weights],
        out_specs=[
            tile,
            tile,
            pl.BlockSpec((graphs, 3 * D + 128), lambda i: (0, 0)),
        ],
        out_shape=[
            jax.ShapeDtypeStruct((tokens, D), F32),
            jax.ShapeDtypeStruct((tokens, D), BF),
            jax.ShapeDtypeStruct((graphs, 3 * D + 128), BF),
        ],
        scratch_shapes=[pltpu.VMEM((graphs, D), F32), pltpu.VMEM((graphs, D), F32)],
        compiler_params=pltpu.CompilerParams(vmem_limit_bytes=VMEM_LIMIT),
        cost_estimate=pl.CostEstimate(
            flops=10_000_000_000, bytes_accessed=20_000_000, transcendentals=0
        ),
        name="forward_rest",
    )(lens, partner, embedded, gains, w_up, w_down, *outs, *weights)


def norm_back(d_normed, xhat, rstd, gain):
    d_hat = d_normed * gain
    return rstd * (
        d_hat
        - jnp.mean(d_hat, axis=-1, keepdims=True)
        - xhat * jnp.mean(d_hat * xhat, axis=-1, keepdims=True)
    )


def ffn_back_kernel(
    lens_ref, mid_ref, slope_ref, dout_ref, dhid_ref, gain_ref, up_ref,
    dmid_ref, dattn_ref, dt_ref, grad_ref, dgain_ref, grad, dgain, *, tile_graphs
):
    step, steps = pl.program_id(0), pl.num_programs(0)
    xhat, rstd = normalize(mid_ref[...])
    gain = gain_ref[1:2, :]
    place = lax.broadcasted_iota(jnp.int32, (LEN, 1), 0)
    d_up, d_out = [], []
    for j in range(tile_graphs):
        g = step * tile_graphs + j
        live = place < lens_ref[g]
        rows = slice(j * LEN, (j + 1) * LEN)
        d_hidden = jnp.where(live, dhid_ref[pl.ds(g, 1), :], 0.0)
        d_up.append((slope_ref[rows, :].astype(F32) * d_hidden).astype(BF))
        d_out.append(jnp.where(live, dout_ref[pl.ds(g, 1), :], 0.0))
    d_up, d_out = jnp.concatenate(d_up, axis=0), jnp.concatenate(d_out, axis=0)
    d_normed = nt(d_up, up_ref[...])
    d_mid = d_out + norm_back(d_normed, xhat, rstd, gain)
    dmid_ref[...] = d_mid
    d_attn = d_mid.astype(BF)
    dattn_ref[...] = d_attn
    dt_ref[...] = d_attn.T
    part = tn((xhat * gain).astype(BF), d_up)
    part_gain = jnp.sum((d_normed * xhat).reshape(-1, 8, D), axis=0)

    @pl.when(step == 0)
    def _():
        grad[...] = part
        dgain[...] = part_gain

    @pl.when(step > 0)
    def _():
        grad[...] += part
        dgain[...] += part_gain

    @pl.when(step == steps - 1)
    def _():
        for half in range(2):
            grad_ref[half] = grad[:, half * PACK : (half + 1) * PACK].astype(BF)
        dgain_ref[...] = dgain[...]


def ffn_back(lens, middle, slope, d_out, d_hidden, gains, w_up):
    tokens = middle.shape[0]
    tile_graphs = min(2, tokens // LEN)
    rows = tile_graphs * LEN
    full = lambda a: pl.BlockSpec(a.shape, lambda i: (0,) * a.ndim)
    tile = pl.BlockSpec((rows, D), lambda i: (i, 0))
    return pl.pallas_call(
        functools.partial(ffn_back_kernel, tile_graphs=tile_graphs),
        grid=(tokens // rows,),
        in_specs=[pl.BlockSpec(memory_space=pltpu.SMEM), tile, tile]
        + [full(a) for a in (d_out, d_hidden, gains, w_up)],
        out_specs=[
            tile,
            tile,
            pl.BlockSpec((D, rows), lambda i: (0, i)),
            pl.BlockSpec((2, D, PACK), lambda i: (0, 0, 0)),
            pl.BlockSpec((8, D), lambda i: (0, 0)),
        ],
        out_shape=[
            jax.ShapeDtypeStruct((tokens, D), F32),
            jax.ShapeDtypeStruct((tokens, D), BF),
            jax.ShapeDtypeStruct((D, tokens), BF),
            jax.ShapeDtypeStruct((2, D, PACK), BF),
            jax.ShapeDtypeStruct((8, D), F32),
        ],
        scratch_shapes=[pltpu.VMEM((D, D), F32), pltpu.VMEM((8, D), F32)],
        compiler_params=pltpu.CompilerParams(vmem_limit_bytes=VMEM_LIMIT),
        cost_estimate=pl.CostEstimate(
            flops=10_000_000_000, bytes_accessed=15_000_000, transcendentals=0
        ),
        name="ffn_back",
    )(lens, middle, slope, d_out, d_hidden, gains, w_up)


class Place:
    def __init__(self):
        self.n, self.heads = lax.axis_size("dp"), lax.axis_size("head")
        self.outs = self.n // 2
        dp, head = lax.axis_index("dp"), lax.axis_index("head")
        self.dp, self.head = dp, head
        self.outer, self.inner, self.far, self.core = dp // 2, dp % 2, head // 2, head % 2

    def move(self, v, to):
        pairs = []
        for i in range(self.n * self.heads):
            outer, inner, far, core = i // 8, (i // 4) % 2, (i // 2) % 2, i % 2
            outer, inner, far, core = to(outer, inner, far, core)
            pairs.append((i, ((outer % self.outs * 2 + inner) * 2 + far) * 2 + core))
        return lax.ppermute(v, ("dp", "head"), pairs)

    def to_core(self, v):
        return self.move(v, lambda o, i, f, c: (o, i, f, 1 - c))

    def to_outer(self, v, by):
        return self.move(v, lambda o, i, f, c: (o + by, i, f, c))

    def mixed(self, v, turn):
        return self.move(
            v, lambda o, i, f, c: (o, 1 - i, f, c) if c == turn else (o, i, 1 - f, c)
        )

    def by_core(self, a, b):
        return jnp.where(self.core == 0, a, b)

    def gather_outer(self, v):
        out = jnp.zeros((self.outs,) + v.shape, v.dtype)
        out = lax.dynamic_update_index_in_dim(out, v, self.outer, 0)
        for by in range(1, self.outs):
            out = lax.dynamic_update_index_in_dim(
                out, self.to_outer(v, by), (self.outer - by) % self.outs, 0
            )
        return out

    def gather_pieces(self, v):
        return self.gather_near(self.gather_outer(v))

    def gather_near(self, own):
        second = self.mixed(own, 0)
        third = self.mixed(jnp.stack([own, second]), 1)
        return [
            [own, self.by_core(second, third[0])],
            [self.by_core(third[0], second), third[1]],
        ]

    def whole(self, pieces):
        rows = [
            [jnp.where(self.far == 0, pieces[f][i], pieces[1 - f][i]) for f in range(2)]
            for i in range(2)
        ]
        ordered = [
            [jnp.where(self.inner == 0, rows[i][f], rows[1 - i][f]) for f in range(2)]
            for i in range(2)
        ]
        return jnp.stack([jnp.stack(pair, axis=1) for pair in ordered], axis=1)

    def both_cores(self, v, axis):
        other = self.to_core(v)
        return jnp.stack([self.by_core(v, other), self.by_core(other, v)], axis=axis)

    def both_cores_of(self, own, sent):
        other = self.to_core(sent)
        return jnp.stack([self.by_core(own, other), self.by_core(other, own)])

    def gather_all(self, v):
        v = self.both_cores(self.whole(self.gather_pieces(v)), 3)
        return v.reshape((self.n, self.heads) + v.shape[4:])

    def fold_far(self, pieces):
        sent = jnp.stack([self.by_core(pieces[1][0], pieces[0][1]), pieces[1][1]])
        kept = jnp.stack([pieces[0][0], self.by_core(pieces[0][1], pieces[1][0])])
        return kept, sent

    def fold_near(self, kept, came, dtype):
        total = kept.astype(F32) + came.astype(F32)
        return total[0], total[1].astype(dtype)

    def fold_outer(self, kept, came, dtype):
        total = (kept.astype(F32) + came.astype(F32)).astype(dtype)
        pick = lambda by: lax.dynamic_index_in_dim(
            total, (self.outer + by) % self.outs, 0, keepdims=False
        )
        result = pick(0).astype(F32)
        for by in range(1, self.outs):
            result = result + self.to_outer(pick(by), by).astype(F32)
        return result

    def total(self, v):
        v = v + self.to_core(v)
        v = v + self.move(v, lambda o, i, f, c: (o, i, 1 - f, c))
        v = v + self.move(v, lambda o, i, f, c: (o, 1 - i, f, c))
        by = 1
        while by < self.outs:
            v = v + self.move(v, lambda o, i, f, c, by=by: (o ^ by, i, f, c))
            by *= 2
        return v

    def split_rows(self, v):
        v = v.reshape((self.outs, 2, -1) + v.shape[1:])
        return [
            lax.dynamic_index_in_dim(v, (self.inner + i) % 2, 1, keepdims=False) for i in range(2)
        ]


def tie(*values):
    return lax.optimization_barrier(values)


def log_total(values, axis):
    top = jnp.max(values, axis=axis, keepdims=True)
    return jnp.squeeze(top, axis) + jnp.log(jnp.sum(jnp.exp(values - top), axis=axis))


def identifiers(table, endpoints):
    graphs = endpoints.shape[0] // LEN
    nodes = table.reshape(graphs, NODE, LAP).astype(BF)
    picks = (
        endpoints.reshape(graphs, LEN, 2)[..., None] == jnp.arange(NODE, dtype=jnp.int32)
    ).astype(BF)
    found = jnp.einsum("glan,gnc->glac", picks, nodes, preferred_element_type=F32)
    return found.reshape(graphs * LEN, 2 * LAP).astype(BF)


def split_core(place, grad_up):
    v = grad_up.reshape((2, place.outs, 2, 2, 2, -1, PACK))
    pick = lambda at: lax.dynamic_index_in_dim(v, at, 4, keepdims=False)
    return pick(1 - place.core), pick(place.core)


def fold_pieces(place, own, came, up):
    pieces = []
    for f in range(2):
        total = own[f].astype(F32) + came[f].astype(F32)
        pieces.append([v.astype(BF) for v in place.split_rows(total)])
    if up is None:
        return pieces
    total = (up[0].astype(F32) + up[1].astype(F32)).astype(BF)
    for f in range(2):
        part = lax.dynamic_index_in_dim(total, (place.far + f) % 2, 3, keepdims=False)
        for i in range(2):
            rows = lax.dynamic_index_in_dim(part, (place.inner + i) % 2, 2, keepdims=False)
            pieces[f][i] = jnp.concatenate([pieces[f][i], rows[0], rows[1]], axis=1)
    return pieces


def adam_step(weight, gradient, first, second, factor, rate):
    clipped = gradient * factor
    first_new = BETA_ONE * first + (1.0 - BETA_ONE) * clipped
    second_new = BETA_TWO * second + (1.0 - BETA_TWO) * clipped * clipped
    first_hat = first_new / (1.0 - BETA_ONE**STEPS)
    second_hat = second_new / (1.0 - BETA_TWO**STEPS)
    weight_new = weight - rate * (first_hat / (jnp.sqrt(second_hat) + ADAM_EPS) + DECAY * weight)
    return (weight_new, first_new, second_new)


def per_device(
    features,
    laplacian,
    endpoints,
    lengths,
    pairing,
    ident_weight,
    qkv_weight,
    out_weight,
    ffn_weight,
    norm_gains,
    ident_first,
    qkv_first,
    out_first,
    ffn_first,
    gains_first,
    ident_second,
    qkv_second,
    out_second,
    ffn_second,
    gains_second,
):
    place = Place()
    heads, head, dp, core = place.heads, place.head, place.dp, place.core
    tokens = features.shape[0] // heads
    graphs = tokens // LEN
    own_columns = norm_gains.shape[1]

    small = jnp.concatenate([ident_weight, norm_gains], axis=0)
    small_rows = small.shape[0]

    packed = [qkv_weight[:, 0], qkv_weight[:, 1], qkv_weight[:, 2], out_weight.T]
    shards = jnp.stack(
        [
            jnp.concatenate([m[:, s * SW : (s + 1) * SW] for m in packed], axis=1).astype(BF)
            for s in range(2)
        ]
    )
    pick = lambda v, at: lax.dynamic_index_in_dim(v, at, 0, keepdims=False)
    near = jnp.stack([pick(shards, core), place.to_core(pick(shards, 1 - core))])
    near, small = tie(near, small.reshape(1, -1))
    near, small = tie(place.gather_outer(near), place.gather_outer(small))
    pieces = place.gather_near(near)
    small = place.both_cores(place.whole(place.gather_near(small)), 3)
    small = small.reshape(-1, small_rows, own_columns).transpose(1, 0, 2).reshape(small_rows, D)
    ident_full, gains = small[: 2 * LAP].astype(BF), small[2 * LAP :]
    mine = jnp.stack(
        [
            jnp.stack(
                [
                    jnp.where(place.inner == i, pieces[f][0][:, c], pieces[f][1][:, c])
                    for i in range(2)
                ],
                axis=1,
            ).reshape(D, PACK)
            for f in range(2)
            for c in range(2)
        ]
    )
    others = place.to_core(mine)
    ffn, near = tie(ffn_weight.astype(BF), near)
    ffn_near = place.both_cores_of(pick(ffn, core), pick(ffn, 1 - core))
    ffn_mine = place.whole(place.gather_pieces(ffn_near)).reshape(D, -1)
    ffn_other = place.to_core(ffn_mine)
    w_up, w_down = place.by_core(ffn_mine, ffn_other), place.by_core(ffn_other, ffn_mine)

    start_row = head * tokens
    lens = lax.dynamic_slice_in_dim(lengths.reshape(-1), head * graphs, graphs, 0)
    partner = lax.dynamic_slice_in_dim(
        jnp.concatenate([pairing.reshape(-1)] * 2), head * graphs, graphs, 0
    )
    table_rows = lax.dynamic_slice_in_dim(laplacian, head * graphs * NODE, graphs * NODE, 0)
    end_rows = lax.dynamic_slice_in_dim(endpoints, start_row, tokens, 0)
    ident_rows = identifiers(table_rows, end_rows)
    embedded = lax.dynamic_slice_in_dim(features, start_row, tokens, 0).astype(F32)
    embedded = embedded + nn(ident_rows, ident_full)
    normed_one = (normalize(embedded)[0] * gains[0]).astype(BF)

    saved_mine = attend(lens, normed_one, mine)
    saved_others = attend(lens, normed_one, others)
    normed_turned = normed_one.T
    middle, slope, payload = forward_rest(
        lens, partner, embedded, gains, w_up, w_down, [saved_mine[2], saved_others[2]], [mine, others]
    )

    everyone = place.gather_all(payload).reshape(place.n, 2, GRAPHS_DEV, -1)
    stats = everyone[..., 3 * D :].astype(F32)
    xhat = everyone[..., :D].astype(F32) + everyone[..., D : 2 * D].astype(F32)
    hidden_sums = everyone[..., 2 * D : 3 * D].reshape(-1, D)
    rstd_pool = (stats[..., 0:1] + stats[..., 1:2]).reshape(-1, 1)
    share = (stats[..., 2:3] + stats[..., 3:4]).reshape(-1, 1)
    summaries = xhat * gains[2]
    left, right = summaries[:, 0].reshape(-1, D), summaries[:, 1].reshape(-1, D)
    root_width = D**0.5
    logits = jnp.dot(left, right.T, precision=HIGHEST) / root_width
    row_totals, col_totals = log_total(logits, 1), log_total(logits, 0)
    count = logits.shape[0]
    group = jnp.arange(count, dtype=jnp.int32) // GRAPHS_DEV
    partners = group * GRAPHS_DEV + stats[:, 0, :, 4].reshape(-1).astype(jnp.int32)
    positive = (partners[:, None] == jnp.arange(count, dtype=jnp.int32)[None, :]).astype(F32)
    total_loss = jnp.sum(row_totals) + jnp.sum(col_totals) - 2.0 * jnp.sum(positive * logits)
    d_logits = (
        jnp.exp(logits - row_totals[:, None])
        + jnp.exp(logits - col_totals[None, :])
        - 2.0 * positive
    )
    d_left = jnp.dot(d_logits, right, precision=HIGHEST) / root_width
    d_right = jnp.dot(d_logits.T, left, precision=HIGHEST) / root_width
    d_summary = jnp.stack(
        [d_left.reshape(place.n, GRAPHS_DEV, D), d_right.reshape(place.n, GRAPHS_DEV, D)], axis=1
    ).reshape(-1, D)
    xhat = xhat.reshape(-1, D)
    gain_three = jnp.sum(d_summary * xhat, axis=0)
    d_rows = norm_back(d_summary, xhat, rstd_pool, gains[2]) * share
    d_rows_low = d_rows.astype(BF)
    own_row = (dp * heads + head) * graphs
    d_out = lax.dynamic_slice_in_dim(d_rows, own_row, graphs, 0)
    d_hidden = nn(d_out.astype(BF), w_down)

    own_column = (dp * heads + head) * own_columns
    d_columns = lax.dynamic_slice_in_dim(d_rows_low, own_column, own_columns, 1)
    grad_down = tn(d_columns, hidden_sums)
    d_middle, d_attn, d_turned, grad_up, gain_two = ffn_back(
        lens, middle, slope, d_out, d_hidden, gains, w_up
    )
    back = functools.partial(attend_back, normed_turned)
    up_sent, up_kept = split_core(place, grad_up)
    up_came = place.to_core(up_sent)
    grad_others, d_others = back(d_turned, d_attn, others, saved_others, 0, 1, heads)
    came = place.to_core(grad_others)
    d_attn, grad_others = tie(d_attn, grad_others)
    grad_even, d_even = back(d_turned, d_attn, mine, saved_mine, 0, 2, heads // 2)
    even = fold_pieces(place, [grad_even[0], grad_even[1]], [came[0], came[2]], (up_kept, up_came))
    even_kept, even_sent = place.fold_far(even)
    even_sent, d_attn = tie(even_sent, d_attn)
    even_came = place.mixed(even_sent, 1)
    grad_odd, d_odd = back(d_turned, d_attn, mine, saved_mine, 1, 2, 1)
    d_attn, even_came, grad_odd = tie(d_attn, even_came, grad_odd)
    even_kept, even_sent = place.fold_near(even_kept, even_came, BF)
    even_came = place.mixed(even_sent, 0)
    grad_last, d_last = back(d_turned, d_attn, mine, saved_mine, 3, 2, 1)
    grad_last, even_came = tie(grad_last, even_came)
    odd = fold_pieces(place, [grad_odd[0], grad_last[0]], [came[1], came[3]], None)
    odd_kept, odd_sent = place.fold_far(odd)
    odd_sent, d_last = tie(odd_sent, d_last)
    odd_came = place.mixed(odd_sent, 1)
    even = place.fold_outer(even_kept, even_came, BF)
    rows = first_back(
        embedded,
        d_middle,
        ident_rows,
        gains,
        [d_others, d_even, d_odd, d_last],
        ((1, (0, 1, 2, 3)), (0, (0, 2)), (0, (1,)), (0, (3,))),
        [mine, others],
    )
    odd_came, rows, even = tie(odd_came, rows, even)
    odd_kept, odd_sent = place.fold_near(odd_kept, odd_came, BF)
    odd_came = place.mixed(odd_sent, 0)
    odd = place.fold_outer(odd_kept, odd_came, BF)
    gain_rows = jnp.stack([jnp.sum(rows[2 * LAP :], axis=0), jnp.sum(gain_two, axis=0)])
    rows = jnp.concatenate([rows[: 2 * LAP], gain_rows], axis=0)
    row_count = rows.shape[0]
    rows = rows.T.reshape(place.outs, 2, 2, 2, own_columns * row_count)
    rows_kept = lax.dynamic_index_in_dim(rows, core, 3, keepdims=False)
    rows = rows_kept + place.to_core(lax.dynamic_index_in_dim(rows, 1 - core, 3, keepdims=False))
    turn = lambda v, axis, own, at: lax.dynamic_index_in_dim(v, (own + at) % 2, axis, keepdims=False)
    rows = [[turn(turn(rows, 2, place.far, f), 1, place.inner, i) for i in range(2)] for f in range(2)]
    rows_kept, rows_sent = place.fold_far(rows)
    rows_kept, rows_sent = place.fold_near(rows_kept, place.mixed(rows_sent, 1), F32)
    rows = place.fold_outer(rows_kept, place.mixed(rows_sent, 0), F32).reshape(own_columns, row_count).T
    grad_ident = rows[: 2 * LAP]
    grad_gains = jnp.concatenate(
        [rows[2 * LAP :], lax.dynamic_slice_in_dim(gain_three, own_column, own_columns, 0)[None]],
        axis=0,
    )
    shard_rows = D // place.n
    own_half, other_half = even[:shard_rows], place.to_core(odd)
    halves = [place.by_core(own_half, other_half), place.by_core(other_half, own_half)]
    columns = lambda j: jnp.concatenate([v[:, j * SW : (j + 1) * SW] for v in halves], axis=1)
    grad_qkv = jnp.stack([columns(0), columns(1), columns(2)], axis=1)
    grad_out = columns(3).T
    grad_up = even[shard_rows:].reshape(2, own_columns, PACK)
    grad_ffn = jnp.stack([jnp.concatenate([grad_up[0], grad_up[1]], axis=1), grad_down])

    grads = (grad_ident, grad_qkv, grad_out, grad_ffn, grad_gains)
    squares = sum((jnp.sum(gradient * gradient) for gradient in grads))
    grad_norm = jnp.sqrt(place.total(squares))
    factor = CLIP_AT / jnp.maximum(grad_norm, CLIP_AT)
    results = [
        adam_step(weight, gradient, first, second, factor, rate)
        for weight, gradient, first, second, rate in zip(
            (ident_weight, qkv_weight, out_weight, ffn_weight, norm_gains),
            grads,
            (ident_first, qkv_first, out_first, ffn_first, gains_first),
            (ident_second, qkv_second, out_second, ffn_second, gains_second),
            STEP_RATES,
        )
    ]
    return (grad_norm, total_loss) + tuple(r[k] for k in range(3) for r in results)


def solution(mesh):
    both = P(None, ("dp", "head"))
    weights = (both, P("dp", None, "head"), P("head", "dp"), P(None, ("dp", "head"), None), both)
    in_specs = (P("dp", None),) * 5 + weights * 3
    out_specs = (P(), P()) + weights * 3
    return jax.shard_map(
        per_device, mesh=mesh, in_specs=in_specs, out_specs=out_specs, check_vma=False
    )
```

time: 379 us -> 321 us (0.85)
  other arithmetic: 57.2 us -> 34.4 us
  starting transfers between devices: 77.4 us -> 61.5 us
  Pallas kernels: 113 us -> 97.6 us
    concatenate x14 -> x0, other arithmetic: 22.9 us -> none  [the longest x8 17.8 us: per_device(): cat = lambda k: jnp.concatenate([saved[i][k] for i in chosen], axis=0)]
    ppermute x71 -> x50, starting transfers between devices: 77.4 us -> 61.5 us  [move(): return lax.ppermute(v, ('dp', 'head'), pairs)]
    pallas_call x2 -> x4, Pallas kernels: 60.7 us -> 45.3 us  [attend_back(): pl.pallas_call(functools.partial(attend_back_kernel, graphs=tokens // LEN...]
    pallas_call x0 -> x1, Pallas kernels: none -> 10.9 us  [first_back(): pl.pallas_call(functools.partial(first_back_kernel, parts=parts), grid=(t...]
    unnamed x100 -> x117, local copies, waits for them, and re-layouts: 7.05 us -> 17.3 us
    pallas_call x4 -> x2, Pallas kernels: 28.1 us -> 19.2 us  [attend(): pl.pallas_call(functools.partial(attend_kernel, graphs=tokens // LEN), gr...]
    convert_element_type x13 -> x7, other arithmetic: 8.48 us -> 2.13 us  [the longest x1 1.21 us: fold_pieces(): total = (up[0].astype(F32) + up[1].astype(F32)).astype(BF)]
    slice x7 -> x4, local copies, waits for them, and re-layouts: 5.34 us -> 1.06 us  [the longest x1 1.02 us: per_device(): hidden_sums = everyone[..., 2 * D:3 * D].reshape(-1, D)]
  transfers between devices with their start and end apart: 71 -> 50, of which waited for: 31 -> 20; matrix products, arithmetic and copies ran while one was open for 18% -> 10% of each run, Pallas kernels for 8% -> 14%
where the time goes in v2:
time: 321 us; the launch traced here: 317 us
  Pallas kernels  97.6 us (30%)
  waiting for transfers between devices  72.4 us (23%)
  starting transfers between devices  61.5 us (19%)
  other arithmetic  34.4 us (11%)
  local copies, waits for them, and re-layouts  32 us (10%)
  between operations  13.5 us (4%)
  matrix products  6.16 us (2%)
    ppermute x50, waiting for transfers between devices, move(): return lax.ppermute(v, ('dp', 'head'), pairs)  72.4 us
    ppermute x50, starting transfers between devices, move(): return lax.ppermute(v, ('dp', 'head'), pairs)  61.5 us
    pallas_call x4, Pallas kernels, attend_back(): pl.pallas_call(functools.partial(attend_back_kernel, graphs=tokens // LEN...  45.3 us
    pallas_call x2, Pallas kernels, attend(): pl.pallas_call(functools.partial(attend_kernel, graphs=tokens // LEN), gr...  19.2 us
    unnamed x117, local copies, waits for them, and re-layouts  17.3 us
    pallas_call x1, Pallas kernels, forward_rest(): pl.pallas_call(functools.partial(forward_kernel, tile_graphs=tile_graphs,...  15.3 us
    pallas_call x1, Pallas kernels, first_back(): pl.pallas_call(functools.partial(first_back_kernel, parts=parts), grid=(t...  10.9 us
    pallas_call x1, Pallas kernels, ffn_back(): pl.pallas_call(functools.partial(ffn_back_kernel, tile_graphs=tile_graphs...  6.82 us
  transfers between devices with their start and end apart: 50, of which 20 were waited for; matrix products, arithmetic and copies ran while one was open for 10% of the time, Pallas kernels for 14%

profile of v2, /device:TPU:0, one launch (start us, length us, event | category | flops | bytes accessed | tf_op | source)
XLA Modules:
  0.0 317.4 jit_solution(1236798327357876138)
XLA Ops:
  6.1 4.8 %collective-permute-start.6 = (f32[1,840]{1,0:T(1,128)S(1)}, f32[1,840]{1,0:T(1,128)S(1)}, u32[]{:S(2)}, u32[]{:S(2)}) collective-permute-start(f32[1,840]{1,0:T(1,128)S(1)} %reshape.623), channel_id=1, source_target_pairs={{0,24},{1,25},{2,26},{3,27},{4,28},{5,29},{6,30},{7,31},{8,0},{9,1... | collective-permute-start | bytes 10088 | tf_op jit(solution)/shard_map/ppermute | solution.py:468
  16.4 3.6 %collective-permute-done.3 = bf16[2,96,384]{1,2,0:T(8,128)(2,1)S(1)} collective-permute-done((bf16[2,96,384]{1,2,0:T(8,128)(2,1)S(1)}, bf16[2,96,384]{1,2,0:T(8,128)(2,1)S(1)}, u32[]{:S(2)}, u32[]{:S(2)}) %collective-permute-start.3) | collective-permute-done | bytes 147488 | tf_op jit(solution)/shard_map/ppermute | solution.py:468
  20.2 12.6 %collective-permute-done.2 = bf16[2,96,384]{1,2,0:T(8,128)(2,1)S(1)} collective-permute-done((bf16[2,96,384]{1,2,0:T(8,128)(2,1)S(1)}, bf16[2,96,384]{1,2,0:T(8,128)(2,1)S(1)}, u32[]{:S(2)}, u32[]{:S(2)}) %collective-permute-start.2) | collective-permute-done | bytes 147488 | tf_op jit(solution)/shard_map/ppermute | solution.py:468
  35.3 8.0 %collective-permute-done.7 = f32[4,1,840]{2,1,0:T(1,128)S(1)} collective-permute-done((f32[4,1,840]{2,1,0:T(1,128)S(1)}, f32[4,1,840]{2,1,0:T(1,128)S(1)}, u32[]{:S(2)}, u32[]{:S(2)}) %collective-permute-start.7) | collective-permute-done | bytes 13472 | tf_op jit(solution)/shard_map/ppermute | solution.py:468
  46.9 4.0 %collective-permute-start.13 = (bf16[2,24,768]{2,1,0:T(8,128)(2,1)}, bf16[2,24,768]{2,1,0:T(8,128)(2,1)}, u32[]{:S(2)}, u32[]{:S(2)}) collective-permute-start(bf16[2,24,768]{2,1,0:T(8,128)(2,1)} %pad_maximum_fusion.21), channel_id=1, source_target_pairs={{0,24},{1,25},{2,26},{3,27},{4,28},{5,29},{6,30},{7,31},{8,0},{9,1... | collective-permute-start | bytes 221192 | tf_op jit(solution)/shard_map/ppermute | solution.py:468
  62.5 8.2 %collective-permute-done.14 = bf16[4,2,24,768]{3,2,1,0:T(8,128)(2,1)} collective-permute-done((bf16[4,2,24,768]{3,2,1,0:T(8,128)(2,1)S(1)}, bf16[4,2,24,768]{3,2,1,0:T(8,128)(2,1)}, u32[]{:S(2)}, u32[]{:S(2)}) %collective-permute-start.14) | collective-permute-done | bytes 294944 | tf_op jit(solution)/shard_map/ppermute | solution.py:468
  77.7 5.1 %collective-permute-done.15 = bf16[2,4,2,24,768]{4,3,2,1,0:T(8,128)(2,1)S(1)} collective-permute-done((bf16[2,4,2,24,768]{4,3,2,1,0:T(8,128)(2,1)S(1)}, bf16[2,4,2,24,768]{4,3,2,1,0:T(8,128)(2,1)S(1)}, u32[]{:S(2)}, u32[]{:S(2)}) %collective-permute-start.15) | collective-permute-done | bytes 589856 | tf_op jit(solution)/shard_map/ppermute | solution.py:468
  86.3 9.6 %attend.2 = (bf16[4,3,1024,128]{3,2,1,0:T(8,128)(2,1)S(1)}, bf16[4,1024,512]{2,1,0:T(8,128)(2,1)}, bf16[4,1024,128]{2,1,0:T(8,128)(2,1)S(1)}, f32[4,1024,128]{2,1,0:T(8,128)S(1)}) custom-call(s32[8]{0:T(128)S(1)} %dynamic_slice.155.lens_ref, bf16[1024,768]{1,0:T(8,128)(2,1)S(1)} %multiply_convert_fusion.x_ref, ...), custom_call_target="tpu_custom_call" | custom-call | flops 10000000000 | bytes 12000000 | tf_op jit(solution)/shard_map/attend/pallas_call | solution.py:95
  99.0 9.6 %attend.3 = (bf16[4,3,1024,128]{3,2,1,0:T(8,128)(2,1)S(1)}, bf16[4,1024,512]{2,1,0:T(8,128)(2,1)}, bf16[4,1024,128]{2,1,0:T(8,128)(2,1)S(1)}, f32[4,1024,128]{2,1,0:T(8,128)S(1)}) custom-call(s32[8]{0:T(128)S(1)} %dynamic_slice.155.lens_ref, bf16[1024,768]{1,0:T(8,128)(2,1)S(1)} %multiply_convert_fusion.x_ref, ...), custom_call_target="tpu_custom_call" | custom-call | flops 10000000000 | bytes 12000000 | tf_op jit(solution)/shard_map/attend/pallas_call | solution.py:95
  108.7 15.3 %forward_rest.1 = (f32[1024,768]{1,0:T(8,128)}, bf16[1024,768]{1,0:T(8,128)(2,1)S(1)}, bf16[8,2432]{1,0:T(8,128)(2,1)S(1)}) custom-call(s32[8]{0:T(128)S(1)} %dynamic_slice.155.lens_ref, s32[8]{0:T(128)S(1)} %copy-done.8, f32[1024,768]{1,0:T(8,128)} %copy-done.26, f32[3,768]{1,0:T(4,128)S(1)} %slice.292.gain_ref, ...), custom_call_target="tpu_custom_call" | custom-call | flops 10000000000 | bytes 20000000 | tf_op jit(solution)/shard_map/forward_rest/pallas_call | solution.py:342
  126.6 4.3 %collective-permute-done.20 = bf16[8,2432]{1,0:T(8,128)(2,1)S(1)} collective-permute-done((bf16[8,2432]{1,0:T(8,128)(2,1)S(1)}, bf16[8,2432]{1,0:T(8,128)(2,1)S(1)}, u32[]{:S(2)}, u32[]{:S(2)}) %collective-permute-start.20) | collective-permute-done | bytes 38944 | tf_op jit(solution)/shard_map/ppermute | solution.py:468
  132.5 4.2 %collective-permute-done.23 = bf16[4,8,2432]{2,1,0:T(8,128)(2,1)S(1)} collective-permute-done((bf16[4,8,2432]{2,1,0:T(8,128)(2,1)S(1)}, bf16[4,8,2432]{2,1,0:T(8,128)(2,1)S(1)}, u32[]{:S(2)}, u32[]{:S(2)}) %collective-permute-start.23) | collective-permute-done | bytes 155680 | tf_op jit(solution)/shard_map/ppermute | solution.py:468
  137.4 6.4 %collective-permute-done.24 = bf16[2,4,8,2432]{3,2,1,0:T(8,128)(2,1)S(1)} collective-permute-done((bf16[2,4,8,2432]{3,2,1,0:T(8,128)(2,1)S(1)}, bf16[2,4,8,2432]{3,2,1,0:T(8,128)(2,1)S(1)}, u32[]{:S(2)}, u32[]{:S(2)}) %collective-permute-start.24) | collective-permute-done | bytes 311328 | tf_op jit(solution)/shard_map/ppermute | solution.py:468
  145.0 3.5 %fusion.90 = bf16[768,1024]{0,1:T(8,128)(2,1)} fusion(f32[768]{0:T(1024)S(1)} %mul.296, f32[1024]{0:T(1024)S(1)} %add_rsqrt_fusion, f32[1024,768]{1,0:T(8,128)} %copy-done.26, f32[1024]{0:T(1024)S(1)} %broadcast_multiply_fusion.3), kind=kLoop, calls=%fused_computation.336 | loop fusion | flops 3145728 | bytes 4729856 | tf_op jit(solution)/shard_map/transpose | solution.py:694
  164.5 6.8 %ffn_back.1 = (f32[1024,768]{1,0:T(8,128)S(1)}, bf16[1024,768]{1,0:T(8,128)(2,1)S(1)}, bf16[768,1024]{1,0:T(8,128)(2,1)S(1)}, bf16[2,768,384]{2,1,0:T(8,128)(2,1)S(1)}, f32[8,768]{1,0:T(8,128)S(1)}) custom-call(s32[8]{0:T(128)S(1)} %dynamic_slice.155.lens_ref, f32[1024,768]{1,0:T(8,128)} %get-tuple-element.66.mid_ref, bf16[1024,768]{1,0:T(8,128)(2,1)S(1)} %copy-done.21, ...), custom_call_target="tpu_custom_call" | custom-call | flops 10000000000 | bytes 15000000 | tf_op jit(solution)/shard_map/ffn_back/pallas_call | solution.py:426
  173.1 21.9 %attend_back.4 = (bf16[4,768,384]{2,1,0:T(8,128)(2,1)}, bf16[4,1024,384]{2,1,0:T(8,128)(2,1)}) custom-call(bf16[768,1024]{1,0:T(8,128)(2,1)S(1)} %copy.248.xt_ref, bf16[768,1024]{1,0:T(8,128)(2,1)S(1)} %get-tuple-element.69.dt_ref, bf16[1024,768]{1,0:T(8,128)(2,1)S(1)} %get-tuple-element.84.da_ref, bf16[4,768,384]{2,1,0:T(8,128)(2,1)} %copy-done.6, ...), custom_call_target="tpu_custom_call" | custom-call | flops 24000000000 | bytes 12000000 | tf_op jit(solution)/shard_map/attend_back/pallas_call | solution.py:174
  207.1 11.1 %attend_back.5 = (bf16[2,768,384]{2,1,0:T(8,128)(2,1)S(1)}, bf16[2,1024,384]{2,1,0:T(8,128)(2,1)S(1)}) custom-call(bf16[768,1024]{1,0:T(8,128)(2,1)S(1)} %copy.248.xt_ref, bf16[768,1024]{1,0:T(8,128)(2,1)S(1)} %copy-done.15, bf16[1024,768]{1,0:T(8,128)(2,1)S(1)} %copy-done.13, bf16[4,768,384]{2,1,0:T(8,128)(2,1)} %copy-done.2, ...), custom_call_target="tpu_custom_call" | custom-call | flops 12000000000 | bytes 6000000 | tf_op jit(solution)/shard_map/attend_back/pallas_call | solution.py:174
  223.5 6.2 %attend_back.6 = (bf16[1,768,384]{2,1,0:T(8,128)(2,1)S(1)}, bf16[1,1024,384]{2,1,0:T(8,128)(2,1)S(1)}) custom-call(bf16[768,1024]{1,0:T(8,128)(2,1)S(1)} %copy.248.xt_ref, bf16[768,1024]{1,0:T(8,128)(2,1)S(1)} %copy-done.15, bf16[1024,768]{1,0:T(8,128)(2,1)S(1)} %copy-done.13, bf16[4,768,384]{2,1,0:T(8,128)(2,1)} %copy-done.2, ...), custom_call_target="tpu_custom_call" | custom-call | flops 6000000000 | bytes 3000000 | tf_op jit(solution)/shard_map/attend_back/pallas_call | solution.py:174
  229.7 5.0 %collective-permute-done.28 = bf16[2,4,144,384]{3,2,1,0:T(8,128)(2,1)S(1)} collective-permute-done((bf16[2,4,144,384]{3,2,1,0:T(8,128)(2,1)S(1)}, bf16[2,4,144,384]{3,2,1,0:T(8,128)(2,1)S(1)}, u32[]{:S(2)}, u32[]{:S(2)}) %collective-permute-start.28) | collective-permute-done | bytes 884768 | tf_op jit(solution)/shard_map/ppermute | solution.py:468
  236.5 6.2 %attend_back.7 = (bf16[1,768,384]{2,1,0:T(8,128)(2,1)S(1)}, bf16[1,1024,384]{2,1,0:T(8,128)(2,1)S(1)}) custom-call(bf16[768,1024]{1,0:T(8,128)(2,1)S(1)} %copy.248.xt_ref, bf16[768,1024]{1,0:T(8,128)(2,1)S(1)} %copy-done.15, bf16[1024,768]{1,0:T(8,128)(2,1)S(1)} %copy-done.13, bf16[4,768,384]{2,1,0:T(8,128)(2,1)} %copy-done.2, ...), custom_call_target="tpu_custom_call" | custom-call | flops 6000000000 | bytes 3000000 | tf_op jit(solution)/shard_map/attend_back/pallas_call | solution.py:174
  245.5 3.7 %collective-permute-start.33 = (bf16[144,384]{1,0:T(8,128)(2,1)S(1)}, bf16[144,384]{1,0:T(8,128)(2,1)S(1)}, u32[]{:S(2)}, u32[]{:S(2)}) collective-permute-start(bf16[144,384]{1,0:T(8,128)(2,1)S(1)} %get-tuple-element.260), channel_id=1, source_target_pairs={{0,24},{1,25},{2,26},{3,27},{4,28},{5,29},{6,30},{7,31},{8,0},{9,1... | collective-permute-start | bytes 331784 | tf_op jit(solution)/shard_map/ppermute | solution.py:468
  249.7 10.9 %first_back.1 = f32[40,768]{1,0:T(8,128)S(1)} custom-call(f32[1024,768]{1,0:T(8,128)} %copy-done.26, f32[1024,768]{1,0:T(8,128)} %copy-done.18, bf16[1024,32]{1,0:T(8,128)(2,1)S(1)} %copy.253.ident_ref, f32[3,768]{1,0:T(4,128)S(1)} %slice.292.gain_ref, bf16[4,1024,384]{2,1,0:T(8,128)(2,1)} %get-tuple-element.92.refs_0_, ...), custom_call_target="tpu_custom_call" | custom-call | flops 8000000000 | bytes 15000000 | tf_op jit(solution)/shard_map/first_back/pallas_call | solution.py:234
  274.5 3.8 %collective-permute-start.39 = (f32[816]{0:T(1024)S(1)}, f32[816]{0:T(1024)S(1)}, u32[]{:S(2)}, u32[]{:S(2)}) collective-permute-start(f32[816]{0:T(1024)S(1)} %get-tuple-element.182), channel_id=1, source_target_pairs={{0,24},{1,25},{2,26},{3,27},{4,28},{5,29},{6,30},{7,31},{8,0},{9,1... | collective-permute-start | bytes 9800 | tf_op jit(solution)/shard_map/ppermute | solution.py:468
  304.1 3.4 %collective-permute-start.49 = (f32[]{:T(128)}, f32[]{:T(128)}, u32[]{:S(2)}, u32[]{:S(2)}) collective-permute-start(f32[]{:T(128)} %add.591), channel_id=1, source_target_pairs={{0,16},{1,17},{2,18},{3,19},{4,20},{5,21},{6,22},{7,23},{8,24},{9,... | collective-permute-start | bytes 20 | tf_op jit(solution)/shard_map/ppermute | solution.py:468
  (392 shorter events, 125.8 us)
Async XLA Ops:
  6.1 10.3 %collective-permute-start.6 = (f32[1,840]{1,0:T(1,128)S(1)}, f32[1,840]{1,0:T(1,128)S(1)}, u32[]{:S(2)}, u32[]{:S(2)}) collective-permute-start(f32[1,840]{1,0:T(1,128)S(1)} %reshape.623), channel_id=1, source_target_pairs={{0,24},{1,25},{2,26},{3,27},{4,28},{5,29},{6,30},{7,31},{8,0},{9,1... | collective-permute-start | bytes 10088 | tf_op jit(solution)/shard_map/ppermute | solution.py:468
  14.7 18.1 %collective-permute-start.2 = (bf16[2,96,384]{1,2,0:T(8,128)(2,1)S(1)}, bf16[2,96,384]{1,2,0:T(8,128)(2,1)S(1)}, u32[]{:S(2)}, u32[]{:S(2)}) collective-permute-start(bf16[2,96,384]{1,2,0:T(8,128)(2,1)S(1)} %pad_maximum_fusion.17), channel_id=1, source_target_pairs={{0,16},{1,17},{2,18},{3,19},{4,20},{5,21},{6,22},{7,23},{8,24},{9,... | collective-permute-start | bytes 442376 | tf_op jit(solution)/shard_map/ppermute | solution.py:468
  16.4 16.6 %collective-permute-start.1 = (bf16[2,96,384]{1,2,0:T(8,128)(2,1)S(1)}, bf16[2,96,384]{1,2,0:T(8,128)(2,1)S(1)}, u32[]{:S(2)}, u32[]{:S(2)}) collective-permute-start(bf16[2,96,384]{1,2,0:T(8,128)(2,1)S(1)} %pad_maximum_fusion.17), channel_id=1, source_target_pairs={{0,8},{1,9},{2,10},{3,11},{4,12},{5,13},{6,14},{7,15},{8,16},{9,17... | collective-permute-start | bytes 442376 | tf_op jit(solution)/shard_map/ppermute | solution.py:468
  33.2 22.4 %collective-permute-start.17 = (bf16[4,2,96,384]{3,2,1,0:T(8,128)(2,1)S(1)}, bf16[4,2,96,384]{3,2,1,0:T(8,128)(2,1)S(1)}, u32[]{:S(2)}, u32[]{:S(2)}) collective-permute-start(bf16[4,2,96,384]{3,2,1,0:T(8,128)(2,1)S(1)} %constant_dynamic-update-slice_fusion.4), channel_id=1, source_target_pairs={{0,4},{1,3},{2,6},{3,1},{4,0},{5,7},{6,2},{7,5},{8,12},{9,11},{10,... | collective-permute-start | bytes 1769480 | tf_op jit(solution)/shard_map/ppermute | solution.py:468
  34.8 8.5 %collective-permute-start.7 = (f32[4,1,840]{2,1,0:T(1,128)S(1)}, f32[4,1,840]{2,1,0:T(1,128)S(1)}, u32[]{:S(2)}, u32[]{:S(2)}) collective-permute-start(f32[4,1,840]{2,1,0:T(1,128)S(1)} %constant_dynamic-update-slice_fusion), channel_id=1, source_target_pairs={{0,4},{1,3},{2,6},{3,1},{4,0},{5,7},{6,2},{7,5},{8,12},{9,11},{10,... | collective-permute-start | bytes 40328 | tf_op jit(solution)/shard_map/ppermute | solution.py:468
  35.3 9.6 %collective-permute-start.10 = (bf16[24,768]{1,0:T(8,128)(2,1)S(1)}, bf16[24,768]{1,0:T(8,128)(2,1)S(1)}, u32[]{:S(2)}, u32[]{:S(2)}) collective-permute-start(bf16[24,768]{1,0:T(8,128)(2,1)S(1)} %dynamic-slice_bitcast_fusion.15), channel_id=1, source_target_pairs={{0,1},{1,0},{2,3},{3,2},{4,5},{5,4},{6,7},{7,6},{8,9},{9,8},{10,11... | collective-permute-start | bytes 110600 | tf_op jit(solution)/shard_map/ppermute | solution.py:468
  45.6 13.3 %collective-permute-start.12 = (bf16[2,24,768]{2,1,0:T(8,128)(2,1)}, bf16[2,24,768]{2,1,0:T(8,128)(2,1)}, u32[]{:S(2)}, u32[]{:S(2)}) collective-permute-start(bf16[2,24,768]{2,1,0:T(8,128)(2,1)} %pad_maximum_fusion.21), channel_id=1, source_target_pairs={{0,16},{1,17},{2,18},{3,19},{4,20},{5,21},{6,22},{7,23},{8,24},{9,... | collective-permute-start | bytes 221192 | tf_op jit(solution)/shard_map/ppermute | solution.py:468
  46.9 11.1 %collective-permute-start.11 = (bf16[2,24,768]{2,1,0:T(8,128)(2,1)}, bf16[2,24,768]{2,1,0:T(8,128)(2,1)}, u32[]{:S(2)}, u32[]{:S(2)}) collective-permute-start(bf16[2,24,768]{2,1,0:T(8,128)(2,1)} %pad_maximum_fusion.21), channel_id=1, source_target_pairs={{0,8},{1,9},{2,10},{3,11},{4,12},{5,13},{6,14},{7,15},{8,16},{9,17... | collective-permute-start | bytes 221192 | tf_op jit(solution)/shard_map/ppermute | solution.py:468
  46.9 12.9 %collective-permute-start.13 = (bf16[2,24,768]{2,1,0:T(8,128)(2,1)}, bf16[2,24,768]{2,1,0:T(8,128)(2,1)}, u32[]{:S(2)}, u32[]{:S(2)}) collective-permute-start(bf16[2,24,768]{2,1,0:T(8,128)(2,1)} %pad_maximum_fusion.21), channel_id=1, source_target_pairs={{0,24},{1,25},{2,26},{3,27},{4,28},{5,29},{6,30},{7,31},{8,0},{9,1... | collective-permute-start | bytes 221192 | tf_op jit(solution)/shard_map/ppermute | solution.py:468
  56.9 19.6 %collective-permute-start.18 = (bf16[2,4,2,96,384]{4,3,2,1,0:T(8,128)(2,1)}, bf16[2,4,2,96,384]{4,3,2,1,0:T(8,128)(2,1)S(1)}, u32[]{:S(2)}, u32[]{:S(2)}) collective-permute-start(bf16[2,4,2,96,384]{4,3,2,1,0:T(8,128)(2,1)} %pad_maximum_fusion.3), channel_id=1, source_target_pairs={{0,2},{1,5},{2,0},{3,7},{4,6},{5,1},{6,4},{7,3},{8,10},{9,13},{10,... | collective-permute-start | bytes 3538952 | tf_op jit(solution)/shard_map/ppermute | solution.py:468
  60.7 10.0 %collective-permute-start.14 = (bf16[4,2,24,768]{3,2,1,0:T(8,128)(2,1)S(1)}, bf16[4,2,24,768]{3,2,1,0:T(8,128)(2,1)}, u32[]{:S(2)}, u32[]{:S(2)}) collective-permute-start(bf16[4,2,24,768]{3,2,1,0:T(8,128)(2,1)S(1)} %bitcast_dynamic-update-slice_fusion), channel_id=1, source_target_pairs={{0,4},{1,3},{2,6},{3,1},{4,0},{5,7},{6,2},{7,5},{8,12},{9,11},{10,... | collective-permute-start | bytes 884744 | tf_op jit(solution)/shard_map/ppermute | solution.py:468
  71.8 11.0 %collective-permute-start.15 = (bf16[2,4,2,24,768]{4,3,2,1,0:T(8,128)(2,1)S(1)}, bf16[2,4,2,24,768]{4,3,2,1,0:T(8,128)(2,1)S(1)}, u32[]{:S(2)}, u32[]{:S(2)}) collective-permute-start(bf16[2,4,2,24,768]{4,3,2,1,0:T(8,128)(2,1)S(1)} %pad_maximum_fusion.7), channel_id=1, source_target_pairs={{0,2},{1,5},{2,0},{3,7},{4,6},{5,1},{6,4},{7,3},{8,10},{9,13},{10,... | collective-permute-start | bytes 1769480 | tf_op jit(solution)/shard_map/ppermute | solution.py:468
  77.6 21.4 %collective-permute-start.19 = (bf16[4,768,384]{2,1,0:T(8,128)(2,1)S(1)}, bf16[4,768,384]{2,1,0:T(8,128)(2,1)S(1)}, u32[]{:S(2)}, u32[]{:S(2)}) collective-permute-start(bf16[4,768,384]{2,1,0:T(8,128)(2,1)S(1)} %pad_maximum_fusion.w_ref.refs_2_.refs_4_), channel_id=1, source_target_pairs={{0,1},{1,0},{2,3},{3,2},{4,5},{5,4},{6,7},{7,6},{8,9},{9,8},{10,11... | collective-permute-start | bytes 7077896 | tf_op jit(solution)/shard_map/ppermute | solution.py:468
  84.1 13.1 %collective-permute-start.16 = (bf16[768,768]{1,0:T(8,128)(2,1)S(1)}, bf16[768,768]{1,0:T(8,128)(2,1)S(1)}, u32[]{:S(2)}, u32[]{:S(2)}) collective-permute-start(bf16[768,768]{1,0:T(8,128)(2,1)S(1)} %bitcast.442), channel_id=1, source_target_pairs={{0,1},{1,0},{2,3},{3,2},{4,5},{5,4},{6,7},{7,6},{8,9},{9,8},{10,11... | collective-permute-start | bytes 3538952 | tf_op jit(solution)/shard_map/ppermute | solution.py:468
  195.0 24.5 %collective-permute-start.26 = (bf16[4,768,384]{2,1,0:T(8,128)(2,1)}, bf16[4,768,384]{2,1,0:T(8,128)(2,1)}, u32[]{:S(2)}, u32[]{:S(2)}) collective-permute-start(bf16[4,768,384]{2,1,0:T(8,128)(2,1)} %get-tuple-element.74), channel_id=1, source_target_pairs={{0,1},{1,0},{2,3},{3,2},{4,5},{5,4},{6,7},{7,6},{8,9},{9,8},{10,11... | collective-permute-start | bytes 7077896 | tf_op jit(solution)/shard_map/ppermute | solution.py:468
  200.9 17.2 %collective-permute-start.27 = (bf16[2,4,2,2,24,384]{5,4,1,3,2,0:T(8,128)(2,1)}, bf16[2,4,2,2,24,384]{5,4,1,3,2,0:T(8,128)(2,1)}, u32[]{:S(2)}, u32[]{:S(2)}) collective-permute-start(bf16[2,4,2,2,24,384]{5,4,1,3,2,0:T(8,128)(2,1)} %bitcast.432), channel_id=1, source_target_pairs={{0,1},{1,0},{2,3},{3,2},{4,5},{5,4},{6,7},{7,6},{8,9},{9,8},{10,11... | collective-permute-start | bytes 1769480 | tf_op jit(solution)/shard_map/ppermute | solution.py:468
  221.5 13.1 %collective-permute-start.28 = (bf16[2,4,144,384]{3,2,1,0:T(8,128)(2,1)S(1)}, bf16[2,4,144,384]{3,2,1,0:T(8,128)(2,1)S(1)}, u32[]{:S(2)}, u32[]{:S(2)}) collective-permute-start(bf16[2,4,144,384]{3,2,1,0:T(8,128)(2,1)S(1)} %pad_maximum_fusion.4), channel_id=1, source_target_pairs={{0,2},{1,5},{2,0},{3,7},{4,6},{5,1},{6,4},{7,3},{8,10},{9,13},{10,... | collective-permute-start | bytes 2654216 | tf_op jit(solution)/shard_map/ppermute | solution.py:468
  234.9 8.4 %collective-permute-start.29 = (bf16[4,144,384]{2,1,0:T(8,128)(2,1)S(1)}, bf16[4,144,384]{2,1,0:T(8,128)(2,1)S(1)}, u32[]{:S(2)}, u32[]{:S(2)}) collective-permute-start(bf16[4,144,384]{2,1,0:T(8,128)(2,1)S(1)} %fusion.9), channel_id=1, source_target_pairs={{0,4},{1,3},{2,6},{3,1},{4,0},{5,7},{6,2},{7,5},{8,12},{9,11},{10,... | collective-permute-start | bytes 1327112 | tf_op jit(solution)/shard_map/ppermute | solution.py:468
  245.3 15.4 %collective-permute-start.31 = (bf16[144,384]{1,0:T(8,128)(2,1)S(1)}, bf16[144,384]{1,0:T(8,128)(2,1)S(1)}, u32[]{:S(2)}, u32[]{:S(2)}) collective-permute-start(bf16[144,384]{1,0:T(8,128)(2,1)S(1)} %get-tuple-element.259), channel_id=1, source_target_pairs={{0,8},{1,9},{2,10},{3,11},{4,12},{5,13},{6,14},{7,15},{8,16},{9,17... | collective-permute-start | bytes 331784 | tf_op jit(solution)/shard_map/ppermute | solution.py:468
  245.5 15.2 %collective-permute-start.33 = (bf16[144,384]{1,0:T(8,128)(2,1)S(1)}, bf16[144,384]{1,0:T(8,128)(2,1)S(1)}, u32[]{:S(2)}, u32[]{:S(2)}) collective-permute-start(bf16[144,384]{1,0:T(8,128)(2,1)S(1)} %get-tuple-element.260), channel_id=1, source_target_pairs={{0,24},{1,25},{2,26},{3,27},{4,28},{5,29},{6,30},{7,31},{8,0},{9,1... | collective-permute-start | bytes 331784 | tf_op jit(solution)/shard_map/ppermute | solution.py:468
  249.2 11.5 %collective-permute-start.32 = (bf16[144,384]{1,0:T(8,128)(2,1)S(1)}, bf16[144,384]{1,0:T(8,128)(2,1)S(1)}, u32[]{:S(2)}, u32[]{:S(2)}) collective-permute-start(bf16[144,384]{1,0:T(8,128)(2,1)S(1)} %get-tuple-element.261), channel_id=1, source_target_pairs={{0,16},{1,17},{2,18},{3,19},{4,20},{5,21},{6,22},{7,23},{8,24},{9,... | collective-permute-start | bytes 331784 | tf_op jit(solution)/shard_map/ppermute | solution.py:468
  249.2 11.6 %collective-permute-start.30 = (bf16[2,4,96,384]{3,2,1,0:T(8,128)(2,1)S(1)}, bf16[2,4,96,384]{3,2,1,0:T(8,128)(2,1)S(1)}, u32[]{:S(2)}, u32[]{:S(2)}) collective-permute-start(bf16[2,4,96,384]{3,2,1,0:T(8,128)(2,1)S(1)} %pad_maximum_fusion.12), channel_id=1, source_target_pairs={{0,2},{1,5},{2,0},{3,7},{4,6},{5,1},{6,4},{7,3},{8,10},{9,13},{10,... | collective-permute-start | bytes 1769480 | tf_op jit(solution)/shard_map/ppermute | solution.py:468
  269.3 9.0 %collective-permute-start.41 = (bf16[96,384]{1,0:T(8,128)(2,1)S(1)}, bf16[96,384]{1,0:T(8,128)(2,1)S(1)}, u32[]{:S(2)}, u32[]{:S(2)}) collective-permute-start(bf16[96,384]{1,0:T(8,128)(2,1)S(1)} %get-tuple-element.264), channel_id=1, source_target_pairs={{0,8},{1,9},{2,10},{3,11},{4,12},{5,13},{6,14},{7,15},{8,16},{9,17... | collective-permute-start | bytes 221192 | tf_op jit(solution)/shard_map/ppermute | solution.py:468
  269.9 10.4 %collective-permute-start.43 = (bf16[96,384]{1,0:T(8,128)(2,1)S(1)}, bf16[96,384]{1,0:T(8,128)(2,1)S(1)}, u32[]{:S(2)}, u32[]{:S(2)}) collective-permute-start(bf16[96,384]{1,0:T(8,128)(2,1)S(1)} %get-tuple-element.265), channel_id=1, source_target_pairs={{0,24},{1,25},{2,26},{3,27},{4,28},{5,29},{6,30},{7,31},{8,0},{9,1... | collective-permute-start | bytes 221192 | tf_op jit(solution)/shard_map/ppermute | solution.py:468
  (78 other events, 876.4 us)

commit v3 on v2

--- a/solution.py
+++ b/solution.py
@@ -65,7 +65,32 @@
     return jnp.concatenate([v[:, h * LEN : (h + 1) * LEN] for h in range(SUB)], axis=0)
 
 
-def attend_kernel(lens_ref, x_ref, w_ref, qkv_ref, p_ref, o_ref, rinv_ref, *, graphs):
+def attend_kernel(lens_ref, where_ref, x_ref, *refs, graphs, whole):
+    if whole:
+        w_ref, qkv_ref, p_ref, o_ref, rinv_ref = refs
+    else:
+        first_ref, third_ref, w_ref, qkv_ref, p_ref, o_ref, rinv_ref = refs
+        outs, rows = first_ref.shape[1], first_ref.shape[3]
+        far, head = pl.program_id(0) // 2, pl.program_id(0) % 2
+        outer, inner, gatherer = where_ref[0], where_ref[1], where_ref[2]
+        for i in range(2):
+            in_first = (far == 0) if i == 0 else (far == 0) & (gatherer == 0)
+            in_first = in_first | ((far == 1) & (gatherer == 1) & (i == 0))
+            at = jnp.where(in_first, jnp.where(far + i == 0, 0, 1), jnp.where(far + i == 2, 1, 0))
+
+            def place(source, at=at, i=i):
+                for o in range(outs):
+                    row = (lax.rem(outer + outs - o, outs) * 2 + (inner + i) % 2) * rows
+                    w_ref[0, pl.ds(pl.multiple_of(row, rows), rows), :] = source[at, o, head]
+
+            @pl.when(in_first)
+            def _(place=place):
+                place(first_ref)
+
+            @pl.when(jnp.logical_not(in_first))
+            def _(place=place):
+                place(third_ref)
+
     y = nn(x_ref[...], w_ref[0])
     qkv_ref[0, 0] = y[:, :128].astype(BF)
     qkv_ref[0, 1] = pltpu.roll(y, PACK - SW, 1)[:, :128].astype(BF)
@@ -89,30 +114,37 @@
         o_ref[0, rows, :] = jnp.where(col >= V_AT, both[:, :128] * rinv, 0.0).astype(BF)
 
 
-def attend(lens, x, w):
-    tokens, groups = x.shape[0], w.shape[0]
+def attend(lens, where, x, pieces):
+    tokens = x.shape[0]
+    groups = 4
+    whole = len(pieces) == 1
     block = lambda *tail: pl.BlockSpec((1,) + tail, lambda i: (i,) + (0,) * len(tail))
-    return pl.pallas_call(
-        functools.partial(attend_kernel, graphs=tokens // LEN),
+    full = lambda a: pl.BlockSpec(a.shape, lambda i: (0,) * a.ndim)
+    out_specs = [block(3, tokens, 128), block(tokens, 512), block(tokens, 128), block(tokens, 128)]
+    out_shape = [
+        jax.ShapeDtypeStruct((groups, 3, tokens, 128), BF),
+        jax.ShapeDtypeStruct((groups, tokens, 512), BF),
+        jax.ShapeDtypeStruct((groups, tokens, 128), BF),
+        jax.ShapeDtypeStruct((groups, tokens, 128), F32),
+    ]
+    if not whole:
+        out_specs = [block(D, PACK)] + out_specs
+        out_shape = [jax.ShapeDtypeStruct((groups, D, PACK), BF)] + out_shape
+    result = pl.pallas_call(
+        functools.partial(attend_kernel, graphs=tokens // LEN, whole=whole),
         grid=(groups,),
-        in_specs=[
-            pl.BlockSpec(memory_space=pltpu.SMEM),
-            pl.BlockSpec((tokens, D), lambda i: (0, 0)),
-            block(D, PACK),
-        ],
-        out_specs=[block(3, tokens, 128), block(tokens, 512), block(tokens, 128), block(tokens, 128)],
-        out_shape=[
-            jax.ShapeDtypeStruct((groups, 3, tokens, 128), BF),
-            jax.ShapeDtypeStruct((groups, tokens, 512), BF),
-            jax.ShapeDtypeStruct((groups, tokens, 128), BF),
-            jax.ShapeDtypeStruct((groups, tokens, 128), F32),
-        ],
+        in_specs=[pl.BlockSpec(memory_space=pltpu.SMEM)] * 2
+        + [full(x)]
+        + ([block(D, PACK)] if whole else [full(a) for a in pieces]),
+        out_specs=out_specs,
+        out_shape=out_shape,
         compiler_params=pltpu.CompilerParams(vmem_limit_bytes=VMEM_LIMIT),
         cost_estimate=pl.CostEstimate(
             flops=groups * 2_500_000_000, bytes_accessed=groups * 3_000_000, transcendentals=0
         ),
         name="attend",
-    )(lens, x, w)
+    )(lens, where, x, *pieces)
+    return (pieces[0], result) if whole else (result[0], result[1:])
 
 
 def attend_back_kernel(
@@ -451,6 +483,131 @@
     )(lens, middle, slope, d_out, d_hidden, gains, w_up)
 
 
+def loss_kernel(
+    where_ref, a1_ref, a3_ref, b1_ref, b3_ref, gain_ref, down_ref,
+    loss_ref, dout_ref, dhid_ref, dlow_ref, hid_ref, dgain_ref, xhat, stats, rows_ref
+):
+    outs, graphs = a1_ref.shape[1], a1_ref.shape[2]
+    outer, inner, far, core = (where_ref[i] for i in range(4))
+    count = outs * 2 * GRAPHS_DEV
+    place = lambda f, o, i, c: pl.multiple_of(
+        f * count + (o * 2 + i) * GRAPHS_DEV + c * graphs, graphs
+    )
+    for owner, refs in ((core, (a1_ref, a3_ref)), (1 - core, (b1_ref, b3_ref))):
+        for part, ref in enumerate(refs):
+            for at in range(2):
+                if part == at:
+                    f, i = part, part
+                else:
+                    f, i = (owner, 1 - owner) if part == 0 else (1 - owner, owner)
+                for o in range(outs):
+                    values = ref[at, o].astype(F32)
+                    row = place(
+                        lax.rem(far + f, 2), lax.rem(outer + outs - o, outs), lax.rem(inner + i, 2), owner
+                    )
+                    rows = pl.ds(row, graphs)
+                    xhat[rows, :] = values[:, 0:D] + values[:, D : 2 * D]
+                    rows_ref[rows, :] = values[:, 2 * D : 3 * D]
+                    stats[rows, :] = values[:, 3 * D :]
+    hid_ref[...] = rows_ref[...].astype(BF)
+    root = D**-0.5
+    left, right = xhat[0:count, :] * gain_ref[2:3, :], xhat[count:, :] * gain_ref[2:3, :]
+    exact = lambda a, b, dims: lax.dot_general(
+        a, b, (dims, ((), ())), precision=HIGHEST, preferred_element_type=F32
+    )
+    logits = exact(left, right, ((1,), (1,))) * root
+    row_top, col_top = jnp.max(logits, axis=1, keepdims=True), jnp.max(logits, axis=0, keepdims=True)
+    row_expo, col_expo = jnp.exp(logits - row_top), jnp.exp(logits - col_top)
+    row_sum, col_sum = jnp.sum(row_expo, axis=1, keepdims=True), jnp.sum(col_expo, axis=0, keepdims=True)
+    row_id = lax.broadcasted_iota(jnp.int32, (count, count), 0)
+    col_id = lax.broadcasted_iota(jnp.int32, (count, count), 1)
+    slot = stats[0:count, 4:5].astype(jnp.int32)
+    positive = jnp.where(col_id == (row_id & -GRAPHS_DEV) + slot, 1.0, 0.0)
+    loss = (
+        jnp.sum(row_top + jnp.log(row_sum), axis=0, keepdims=True)
+        + jnp.sum(col_top + jnp.log(col_sum), axis=1, keepdims=True)
+        - 2.0 * jnp.sum(jnp.sum(positive * logits, axis=1, keepdims=True), axis=0, keepdims=True)
+    )
+    loss_ref[...] = loss
+    d_logits = row_expo / row_sum + col_expo / col_sum - 2.0 * positive
+    rows_ref[0:count, :] = exact(d_logits, right, ((1,), (0,))) * root
+    rows_ref[count:, :] = exact(d_logits, left, ((0,), (0,))) * root
+    every = xhat[...]
+    d_summary = rows_ref[...]
+    dgain_ref[...] = jnp.sum(d_summary * every, axis=0, keepdims=True)
+    rstd, share = stats[:, 0:1] + stats[:, 1:2], stats[:, 2:3] + stats[:, 3:4]
+    d_rows = norm_back(d_summary, every, rstd, gain_ref[2:3, :]) * share
+    rows_ref[...] = d_rows
+    dlow_ref[...] = d_rows.astype(BF)
+    own = rows_ref[pl.ds(place(far, outer, inner, core), graphs), :]
+    dout_ref[...] = own
+    dhid_ref[...] = nn(own.astype(BF), down_ref[...])
+
+
+def contrast(where, pieces, gains, w_down):
+    outs, graphs = pieces[0].shape[1], pieces[0].shape[2]
+    total = outs * 4 * GRAPHS_DEV
+    return pl.pallas_call(
+        loss_kernel,
+        in_specs=[pl.BlockSpec(memory_space=pltpu.SMEM)]
+        + [pl.BlockSpec(memory_space=pltpu.VMEM)] * 6,
+        out_specs=[pl.BlockSpec(memory_space=pltpu.VMEM)] * 6,
+        out_shape=[
+            jax.ShapeDtypeStruct((1, 1), F32),
+            jax.ShapeDtypeStruct((graphs, D), F32),
+            jax.ShapeDtypeStruct((graphs, D), F32),
+            jax.ShapeDtypeStruct((total, D), BF),
+            jax.ShapeDtypeStruct((total, D), BF),
+            jax.ShapeDtypeStruct((1, D), F32),
+        ],
+        scratch_shapes=[
+            pltpu.VMEM((total, D), F32),
+            pltpu.VMEM((total, 128), F32),
+            pltpu.VMEM((total, D), F32),
+        ],
+        compiler_params=pltpu.CompilerParams(vmem_limit_bytes=24 * 2**20),
+        cost_estimate=pl.CostEstimate(
+            flops=3_000_000_000, bytes_accessed=4_000_000, transcendentals=0
+        ),
+        name="contrast",
+    )(where, *pieces, gains, w_down)
+
+
+def contrast_plain(everyone, gains, w_down, own_row, graphs):
+    n = everyone.shape[0]
+    stats = everyone[..., 3 * D :].astype(F32)
+    xhat = everyone[..., :D].astype(F32) + everyone[..., D : 2 * D].astype(F32)
+    hidden_sums = everyone[..., 2 * D : 3 * D].reshape(-1, D)
+    rstd_pool = (stats[..., 0:1] + stats[..., 1:2]).reshape(-1, 1)
+    share = (stats[..., 2:3] + stats[..., 3:4]).reshape(-1, 1)
+    summaries = xhat * gains[2]
+    left, right = summaries[:, 0].reshape(-1, D), summaries[:, 1].reshape(-1, D)
+    root_width = D**0.5
+    logits = jnp.dot(left, right.T, precision=HIGHEST) / root_width
+    row_totals, col_totals = log_total(logits, 1), log_total(logits, 0)
+    count = logits.shape[0]
+    group = jnp.arange(count, dtype=jnp.int32) // GRAPHS_DEV
+    partners = group * GRAPHS_DEV + stats[:, 0, :, 4].reshape(-1).astype(jnp.int32)
+    positive = (partners[:, None] == jnp.arange(count, dtype=jnp.int32)[None, :]).astype(F32)
+    total_loss = jnp.sum(row_totals) + jnp.sum(col_totals) - 2.0 * jnp.sum(positive * logits)
+    d_logits = (
+        jnp.exp(logits - row_totals[:, None])
+        + jnp.exp(logits - col_totals[None, :])
+        - 2.0 * positive
+    )
+    d_left = jnp.dot(d_logits, right, precision=HIGHEST) / root_width
+    d_right = jnp.dot(d_logits.T, left, precision=HIGHEST) / root_width
+    d_summary = jnp.stack(
+        [d_left.reshape(n, GRAPHS_DEV, D), d_right.reshape(n, GRAPHS_DEV, D)], axis=1
+    ).reshape(-1, D)
+    xhat = xhat.reshape(-1, D)
+    gain_three = jnp.sum(d_summary * xhat, axis=0, keepdims=True)
+    d_rows = norm_back(d_summary, xhat, rstd_pool, gains[2]) * share
+    d_out = lax.dynamic_slice_in_dim(d_rows, own_row, graphs, 0)
+    d_hidden = nn(d_out.astype(BF), w_down)
+    return total_loss, d_out, d_hidden, d_rows.astype(BF), hidden_sums, gain_three
+
+
 class Place:
     def __init__(self):
         self.n, self.heads = lax.axis_size("dp"), lax.axis_size("head")
@@ -490,12 +647,19 @@
             )
         return out
 
+    def outer_list(self, v):
+        return jnp.stack([v] + [self.to_outer(v, by) for by in range(1, self.outs)])
+
     def gather_pieces(self, v):
         return self.gather_near(self.gather_outer(v))
 
     def gather_near(self, own):
-        second = self.mixed(own, 0)
-        third = self.mixed(jnp.stack([own, second]), 1)
+        return self.gather_last(own, self.mixed(own, 0))
+
+    def gather_last(self, own, second):
+        return self.pieces_of(own, second, self.mixed(jnp.stack([own, second]), 1))
+
+    def pieces_of(self, own, second, third):
         return [
             [own, self.by_core(second, third[0])],
             [self.by_core(third[0], second), third[1]],
@@ -577,6 +741,18 @@
     ).astype(BF)
     found = jnp.einsum("glan,gnc->glac", picks, nodes, preferred_element_type=F32)
     return found.reshape(graphs * LEN, 2 * LAP).astype(BF)
+
+
+def stack_pieces(place, near, last):
+    pieces = place.pieces_of(near[0], near[1], last)
+    packs = []
+    for f in range(2):
+        for c in range(2):
+            rows = [
+                jnp.where(place.inner == i, pieces[f][0][:, c], pieces[f][1][:, c]) for i in range(2)
+            ]
+            packs.append(jnp.stack(rows, axis=1).reshape(D, PACK))
+    return jnp.stack(packs)
 
 
 def split_core(place, grad_up):
@@ -651,31 +827,19 @@
     )
     pick = lambda v, at: lax.dynamic_index_in_dim(v, at, 0, keepdims=False)
     near = jnp.stack([pick(shards, core), place.to_core(pick(shards, 1 - core))])
+    shard_rows = D // place.n
+    aligned = shard_rows % 16 == 0
     near, small = tie(near, small.reshape(1, -1))
-    near, small = tie(place.gather_outer(near), place.gather_outer(small))
-    pieces = place.gather_near(near)
-    small = place.both_cores(place.whole(place.gather_near(small)), 3)
+    near, small = tie((place.outer_list if aligned else place.gather_outer)(near), place.gather_outer(small))
+    near, small_near = jnp.stack([near, place.mixed(near, 0)]), place.mixed(small, 0)
+    near, small_near, ffn = tie(near, small_near, ffn_weight.astype(BF))
+    last = place.mixed(near, 1)
+    near_others = place.to_core(near)
+    small = place.both_cores(place.whole(place.gather_last(small, small_near)), 3)
     small = small.reshape(-1, small_rows, own_columns).transpose(1, 0, 2).reshape(small_rows, D)
     ident_full, gains = small[: 2 * LAP].astype(BF), small[2 * LAP :]
-    mine = jnp.stack(
-        [
-            jnp.stack(
-                [
-                    jnp.where(place.inner == i, pieces[f][0][:, c], pieces[f][1][:, c])
-                    for i in range(2)
-                ],
-                axis=1,
-            ).reshape(D, PACK)
-            for f in range(2)
-            for c in range(2)
-        ]
-    )
-    others = place.to_core(mine)
-    ffn, near = tie(ffn_weight.astype(BF), near)
     ffn_near = place.both_cores_of(pick(ffn, core), pick(ffn, 1 - core))
-    ffn_mine = place.whole(place.gather_pieces(ffn_near)).reshape(D, -1)
-    ffn_other = place.to_core(ffn_mine)
-    w_up, w_down = place.by_core(ffn_mine, ffn_other), place.by_core(ffn_other, ffn_mine)
+    ffn_pieces = place.gather_pieces(ffn_near)
 
     start_row = head * tokens
     lens = lax.dynamic_slice_in_dim(lengths.reshape(-1), head * graphs, graphs, 0)
@@ -689,46 +853,43 @@
     embedded = embedded + nn(ident_rows, ident_full)
     normed_one = (normalize(embedded)[0] * gains[0]).astype(BF)
 
-    saved_mine = attend(lens, normed_one, mine)
-    saved_others = attend(lens, normed_one, others)
     normed_turned = normed_one.T
+    last, normed_turned = tie(last, normed_turned)
+    last_others = place.to_core(last)
+    where = jnp.stack([place.outer, place.inner, core]).astype(jnp.int32)
+    where_others = jnp.stack([place.outer, place.inner, 1 - core]).astype(jnp.int32)
+    if aligned:
+        mine, saved_mine = attend(lens, where, normed_one, [near, last])
+    else:
+        packs = stack_pieces(place, near, last)
+        mine, saved_mine = attend(lens, where, normed_one, [packs])
+    ffn_pieces, heads_mine = tie(ffn_pieces, saved_mine[2])
+    if aligned:
+        others, saved_others = attend(lens, where_others, normed_one, [near_others, last_others])
+    else:
+        others, saved_others = attend(lens, where_others, normed_one, [place.to_core(packs)])
+    ffn_mine = place.whole(ffn_pieces).reshape(D, -1)
+    ffn_other = place.to_core(ffn_mine)
+    w_up, w_down = place.by_core(ffn_mine, ffn_other), place.by_core(ffn_other, ffn_mine)
     middle, slope, payload = forward_rest(
-        lens, partner, embedded, gains, w_up, w_down, [saved_mine[2], saved_others[2]], [mine, others]
-    )
-
-    everyone = place.gather_all(payload).reshape(place.n, 2, GRAPHS_DEV, -1)
-    stats = everyone[..., 3 * D :].astype(F32)
-    xhat = everyone[..., :D].astype(F32) + everyone[..., D : 2 * D].astype(F32)
-    hidden_sums = everyone[..., 2 * D : 3 * D].reshape(-1, D)
-    rstd_pool = (stats[..., 0:1] + stats[..., 1:2]).reshape(-1, 1)
-    share = (stats[..., 2:3] + stats[..., 3:4]).reshape(-1, 1)
-    summaries = xhat * gains[2]
-    left, right = summaries[:, 0].reshape(-1, D), summaries[:, 1].reshape(-1, D)
-    root_width = D**0.5
-    logits = jnp.dot(left, right.T, precision=HIGHEST) / root_width
-    row_totals, col_totals = log_total(logits, 1), log_total(logits, 0)
-    count = logits.shape[0]
-    group = jnp.arange(count, dtype=jnp.int32) // GRAPHS_DEV
-    partners = group * GRAPHS_DEV + stats[:, 0, :, 4].reshape(-1).astype(jnp.int32)
-    positive = (partners[:, None] == jnp.arange(count, dtype=jnp.int32)[None, :]).astype(F32)
-    total_loss = jnp.sum(row_totals) + jnp.sum(col_totals) - 2.0 * jnp.sum(positive * logits)
-    d_logits = (
-        jnp.exp(logits - row_totals[:, None])
-        + jnp.exp(logits - col_totals[None, :])
-        - 2.0 * positive
-    )
-    d_left = jnp.dot(d_logits, right, precision=HIGHEST) / root_width
-    d_right = jnp.dot(d_logits.T, left, precision=HIGHEST) / root_width
-    d_summary = jnp.stack(
-        [d_left.reshape(place.n, GRAPHS_DEV, D), d_right.reshape(place.n, GRAPHS_DEV, D)], axis=1
-    ).reshape(-1, D)
-    xhat = xhat.reshape(-1, D)
-    gain_three = jnp.sum(d_summary * xhat, axis=0)
-    d_rows = norm_back(d_summary, xhat, rstd_pool, gains[2]) * share
-    d_rows_low = d_rows.astype(BF)
+        lens, partner, embedded, gains, w_up, w_down, [heads_mine, saved_others[2]], [mine, others]
+    )
+
     own_row = (dp * heads + head) * graphs
-    d_out = lax.dynamic_slice_in_dim(d_rows, own_row, graphs, 0)
-    d_hidden = nn(d_out.astype(BF), w_down)
+    if place.n * GRAPHS_DEV <= 128:
+        first = place.outer_list(payload)
+        first = jnp.stack([first, place.mixed(first, 0)])
+        third = place.mixed(first, 1)
+        four = jnp.stack([place.outer, place.inner, place.far, core]).astype(jnp.int32)
+        total_loss, d_out, d_hidden, d_rows_low, hidden_sums, gain_three = contrast(
+            four, [first, third, place.to_core(first), place.to_core(third)], gains, w_down
+        )
+        total_loss = total_loss[0, 0]
+    else:
+        everyone = place.gather_all(payload).reshape(place.n, 2, GRAPHS_DEV, -1)
+        total_loss, d_out, d_hidden, d_rows_low, hidden_sums, gain_three = contrast_plain(
+            everyone, gains, w_down, own_row, graphs
+        )
 
     own_column = (dp * heads + head) * own_columns
     d_columns = lax.dynamic_slice_in_dim(d_rows_low, own_column, own_columns, 1)
@@ -784,10 +945,9 @@
     rows = place.fold_outer(rows_kept, place.mixed(rows_sent, 0), F32).reshape(own_columns, row_count).T
     grad_ident = rows[: 2 * LAP]
     grad_gains = jnp.concatenate(
-        [rows[2 * LAP :], lax.dynamic_slice_in_dim(gain_three, own_column, own_columns, 0)[None]],
+        [rows[2 * LAP :], lax.dynamic_slice_in_dim(gain_three, own_column, own_columns, 1)],
         axis=0,
     )
-    shard_rows = D // place.n
     own_half, other_half = even[:shard_rows], place.to_core(odd)
     halves = [place.by_core(own_half, other_half), place.by_core(other_half, own_half)]
     columns = lambda j: jnp.concatenate([v[:, j * SW : (j + 1) * SW] for v in halves], axis=1)

time: 321 us -> 299 us (0.931)
  other arithmetic: 34.4 us -> 20.5 us
  waiting for transfers between devices: 72.4 us -> 65.3 us
  Pallas kernels: 97.6 us -> 104 us
  between operations: 13.5 us -> 9.65 us
    pallas_call x2 -> x3, Pallas kernels: 19.2 us -> 27.1 us  [the longest x2 23.1 us: attend(): pl.pallas_call(functools.partial(attend_kernel, graphs=tokens // LEN, who...]
    ppermute x50 -> x52, waiting for transfers between devices: 72.4 us -> 65.3 us  [move(): return lax.ppermute(v, ('dp', 'head'), pairs)]
    unnamed x117 -> x122, local copies, waits for them, and re-layouts: 17.3 us -> 21.3 us
    reduce_sum x3 -> x0, other arithmetic: 3.92 us -> none  [the longest x1 2.6 us: per_device(): gain_three = jnp.sum(d_summary * xhat, axis=0)]
    ppermute x50 -> x52, starting transfers between devices: 61.5 us -> 64 us  [move(): return lax.ppermute(v, ('dp', 'head'), pairs)]
  transfers between devices with their start and end apart: 50 -> 52, of which waited for: 20 -> 23; matrix products, arithmetic and copies ran while one was open for 10% -> 7% of each run, Pallas kernels for 14% -> 12%
where the time goes in v3:
time: 299 us; the launch traced here: 295 us
  Pallas kernels  104 us (35%)
  waiting for transfers between devices  65.3 us (22%)
  starting transfers between devices  64 us (21%)
  local copies, waits for them, and re-layouts  28.8 us (10%)
  other arithmetic  20.5 us (7%)
  between operations  9.65 us (3%)
  matrix products  3.42 us (1%)
    ppermute x52, waiting for transfers between devices, move(): return lax.ppermute(v, ('dp', 'head'), pairs)  65.3 us
    ppermute x52, starting transfers between devices, move(): return lax.ppermute(v, ('dp', 'head'), pairs)  64 us
    pallas_call x4, Pallas kernels, attend_back(): pl.pallas_call(functools.partial(attend_back_kernel, graphs=tokens // LEN...  45.4 us
    pallas_call x2, Pallas kernels, attend(): pl.pallas_call(functools.partial(attend_kernel, graphs=tokens // LEN, who...  23.1 us
    unnamed x122, local copies, waits for them, and re-layouts  21.3 us
    pallas_call x1, Pallas kernels, forward_rest(): pl.pallas_call(functools.partial(forward_kernel, tile_graphs=tile_graphs,...  13.5 us
    pallas_call x1, Pallas kernels, first_back(): pl.pallas_call(functools.partial(first_back_kernel, parts=parts), grid=(t...  10.9 us
    pallas_call x1, Pallas kernels, ffn_back(): pl.pallas_call(functools.partial(ffn_back_kernel, tile_graphs=tile_graphs...  6.82 us
  transfers between devices with their start and end apart: 52, of which 23 were waited for; matrix products, arithmetic and copies ran while one was open for 7% of the time, Pallas kernels for 12%

profile of v3, /device:TPU:0, one launch (start us, length us, event | category | flops | bytes accessed | tf_op | source)
XLA Modules:
  0.0 295.3 jit_solution(6570594782443344607)
XLA Ops:
  4.6 5.0 %collective-permute-start.6 = (f32[1,840]{1,0:T(1,128)S(1)}, f32[1,840]{1,0:T(1,128)S(1)}, u32[]{:S(2)}, u32[]{:S(2)}) collective-permute-start(f32[1,840]{1,0:T(1,128)S(1)} %reshape.541), channel_id=1, source_target_pairs={{0,24},{1,25},{2,26},{3,27},{4,28},{5,29},{6,30},{7,31},{8,0},{9,1... | collective-permute-start | bytes 10088 | tf_op jit(solution)/shard_map/ppermute | solution.py:625
  17.8 9.4 %collective-permute-done.2 = bf16[2,96,384]{2,1,0:T(8,128)(2,1)S(1)} collective-permute-done((bf16[2,96,384]{2,1,0:T(8,128)(2,1)S(1)}, bf16[2,96,384]{2,1,0:T(8,128)(2,1)S(1)}, u32[]{:S(2)}, u32[]{:S(2)}) %collective-permute-start.2) | collective-permute-done | bytes 147488 | tf_op jit(solution)/shard_map/ppermute | solution.py:625
  30.6 6.6 %collective-permute-done.7 = bf16[4,2,96,384]{3,2,1,0:T(8,128)(2,1)S(1)} collective-permute-done((bf16[4,2,96,384]{3,2,1,0:T(8,128)(2,1)S(1)}, bf16[4,2,96,384]{3,2,1,0:T(8,128)(2,1)S(1)}, u32[]{:S(2)}, u32[]{:S(2)}) %collective-permute-start.7) | collective-permute-done | bytes 589856 | tf_op jit(solution)/shard_map/ppermute | solution.py:625
  44.3 4.0 %collective-permute-start.15 = (bf16[2,24,768]{2,1,0:T(8,128)(2,1)S(1)}, bf16[2,24,768]{2,1,0:T(8,128)(2,1)S(1)}, u32[]{:S(2)}, u32[]{:S(2)}) collective-permute-start(bf16[2,24,768]{2,1,0:T(8,128)(2,1)S(1)} %pad_maximum_fusion.15), channel_id=1, source_target_pairs={{0,24},{1,25},{2,26},{3,27},{4,28},{5,29},{6,30},{7,31},{8,0},{9,1... | collective-permute-start | bytes 221192 | tf_op jit(solution)/shard_map/ppermute | solution.py:625
  54.9 5.1 %collective-permute-done.16 = bf16[4,2,24,768]{3,2,1,0:T(8,128)(2,1)S(1)} collective-permute-done((bf16[4,2,24,768]{3,2,1,0:T(8,128)(2,1)S(1)}, bf16[4,2,24,768]{3,2,1,0:T(8,128)(2,1)S(1)}, u32[]{:S(2)}, u32[]{:S(2)}) %collective-permute-start.16) | collective-permute-done | bytes 294944 | tf_op jit(solution)/shard_map/ppermute | solution.py:625
  65.6 4.4 %collective-permute-done.17 = bf16[2,4,2,24,768]{4,3,2,1,0:T(8,128)(2,1)S(1)} collective-permute-done((bf16[2,4,2,24,768]{4,3,2,1,0:T(8,128)(2,1)S(1)}, bf16[2,4,2,24,768]{4,3,2,1,0:T(8,128)(2,1)S(1)}, u32[]{:S(2)}, u32[]{:S(2)}) %collective-permute-start.17) | collective-permute-done | bytes 589856 | tf_op jit(solution)/shard_map/ppermute | solution.py:625
  70.1 11.3 %attend.2 = (bf16[4,768,384]{2,1,0:T(8,128)(2,1)S(1)}, bf16[4,3,1024,128]{3,2,1,0:T(8,128)(2,1)}, bf16[4,1024,512]{2,1,0:T(8,128)(2,1)}, bf16[4,1024,128]{2,1,0:T(8,128)(2,1)S(1)}, f32[4,1024,128]{2,1,0:T(8,128)S(1)}) custom-call(s32[8]{0:T(128)S(1)} %dynamic_slice.152.lens_ref, s32[3]{0:T(128)S(1)} %pad_add_fusion.1.where_ref, ...), custom_call_target="tpu_custom_call" | custom-call | flops 10000000000 | bytes 12000000 | tf_op jit(solution)/shard_map/attend/pallas_call | solution.py:133
  91.2 11.8 %attend.3 = (bf16[4,768,384]{2,1,0:T(8,128)(2,1)S(1)}, bf16[4,3,1024,128]{3,2,1,0:T(8,128)(2,1)}, bf16[4,1024,512]{2,1,0:T(8,128)(2,1)}, bf16[4,1024,128]{2,1,0:T(8,128)(2,1)S(1)}, f32[4,1024,128]{2,1,0:T(8,128)S(1)}) custom-call(s32[8]{0:T(128)S(1)} %dynamic_slice.152.lens_ref, s32[3]{0:T(128)S(1)} %pad_add_fusion.3.where_ref, ...), custom_call_target="tpu_custom_call" | custom-call | flops 10000000000 | bytes 12000000 | tf_op jit(solution)/shard_map/attend/pallas_call | solution.py:133
  105.7 13.5 %forward_rest.1 = (f32[1024,768]{1,0:T(8,128)}, bf16[1024,768]{1,0:T(8,128)(2,1)S(1)}, bf16[8,2432]{1,0:T(8,128)(2,1)S(1)}) custom-call(s32[8]{0:T(128)S(1)} %dynamic_slice.152.lens_ref, s32[8]{0:T(128)S(1)} %dynamic_slice.153.partner_ref, f32[1024,768]{1,0:T(8,128)} %copy-done.30, f32[3,768]{1,0:T(4,128)S(1)} %slice.207.gain_ref, ...), custom_call_target="tpu_custom_call" | custom-call | flops 10000000000 | bytes 20000000 | tf_op jit(solution)/shard_map/forward_rest/pallas_call | solution.py:374
  124.3 3.4 %collective-permute-done.22 = bf16[8,2432]{1,0:T(8,128)(2,1)S(1)} collective-permute-done((bf16[8,2432]{1,0:T(8,128)(2,1)S(1)}, bf16[8,2432]{1,0:T(8,128)(2,1)S(1)}, u32[]{:S(2)}, u32[]{:S(2)}) %collective-permute-start.22) | collective-permute-done | bytes 38944 | tf_op jit(solution)/shard_map/ppermute | solution.py:625
  129.3 3.7 %collective-permute-done.24 = bf16[4,8,2432]{2,1,0:T(8,128)(2,1)S(1)} collective-permute-done((bf16[4,8,2432]{2,1,0:T(8,128)(2,1)S(1)}, bf16[4,8,2432]{2,1,0:T(8,128)(2,1)S(1)}, u32[]{:S(2)}, u32[]{:S(2)}) %collective-permute-start.24) | collective-permute-done | bytes 155680 | tf_op jit(solution)/shard_map/ppermute | solution.py:625
  134.7 5.4 %collective-permute-done.25.a3_ref = bf16[2,4,8,2432]{3,2,1,0:T(8,128)(2,1)S(1)} collective-permute-done((bf16[2,4,8,2432]{3,2,1,0:T(8,128)(2,1)S(1)}, bf16[2,4,8,2432]{3,2,1,0:T(8,128)(2,1)S(1)}, u32[]{:S(2)}, u32[]{:S(2)}) %collective-permute-start.25) | collective-permute-done | bytes 311328 | tf_op jit(solution)/shard_map/ppermute | solution.py:625
  144.2 4.1 %contrast.1 = (f32[1,1]{1,0:T(1,128)}, f32[8,768]{1,0:T(8,128)S(1)}, f32[8,768]{1,0:T(8,128)S(1)}, bf16[256,768]{1,0:T(8,128)(2,1)S(1)}, bf16[256,768]{1,0:T(8,128)(2,1)S(1)}, /*index=5*/f32[1,768]{1,0:T(1,128)S(1)}) custom-call(s32[4]{0:T(128)S(1)} %pad_add_fusion.4.where_ref, bf16[2,4,8,2432]{3,2,1,0:T(8,128)(2,1)S(1)} %pad_maximum_fusion.8.a1_ref, ...), custom_call_target="tpu_custom_call" | custom-call | flops 3000000000 | bytes 4000000 | tf_op jit(solution)/shard_map/contrast/pallas_call | solution.py:550
  149.0 6.8 %ffn_back.1 = (f32[1024,768]{1,0:T(8,128)S(1)}, bf16[1024,768]{1,0:T(8,128)(2,1)S(1)}, bf16[768,1024]{1,0:T(8,128)(2,1)S(1)}, bf16[2,768,384]{2,1,0:T(8,128)(2,1)S(1)}, f32[8,768]{1,0:T(8,128)S(1)}) custom-call(s32[8]{0:T(128)S(1)} %dynamic_slice.152.lens_ref, f32[1024,768]{1,0:T(8,128)} %get-tuple-element.94.mid_ref, bf16[1024,768]{1,0:T(8,128)(2,1)S(1)} %copy-done.25, ...), custom_call_target="tpu_custom_call" | custom-call | flops 10000000000 | bytes 15000000 | tf_op jit(solution)/shard_map/ffn_back/pallas_call | solution.py:458
  158.7 21.8 %attend_back.4 = (bf16[4,768,384]{2,1,0:T(8,128)(2,1)}, bf16[4,1024,384]{2,1,0:T(8,128)(2,1)}) custom-call(bf16[768,1024]{1,0:T(8,128)(2,1)S(1)} %copy.155.xt_ref, bf16[768,1024]{1,0:T(8,128)(2,1)S(1)} %get-tuple-element.99.dt_ref, bf16[1024,768]{1,0:T(8,128)(2,1)S(1)} %get-tuple-element.114.da_ref, bf16[4,768,384]{2,1,0:T(8,128)(2,1)} %copy-done.22, ...), custom_call_target="tpu_custom_call" | custom-call | flops 24000000000 | bytes 12000000 | tf_op jit(solution)/shard_map/attend_back/pallas_call | solution.py:206
  185.9 11.2 %attend_back.5 = (bf16[2,768,384]{2,1,0:T(8,128)(2,1)S(1)}, bf16[2,1024,384]{2,1,0:T(8,128)(2,1)S(1)}) custom-call(bf16[768,1024]{1,0:T(8,128)(2,1)S(1)} %copy.155.xt_ref, bf16[768,1024]{1,0:T(8,128)(2,1)S(1)} %copy-done.17, bf16[1024,768]{1,0:T(8,128)(2,1)S(1)} %copy-done.15, bf16[4,768,384]{2,1,0:T(8,128)(2,1)} %copy-done.9, ...), custom_call_target="tpu_custom_call" | custom-call | flops 12000000000 | bytes 6000000 | tf_op jit(solution)/shard_map/attend_back/pallas_call | solution.py:206
  202.4 6.1 %attend_back.6 = (bf16[1,768,384]{2,1,0:T(8,128)(2,1)S(1)}, bf16[1,1024,384]{2,1,0:T(8,128)(2,1)S(1)}) custom-call(bf16[768,1024]{1,0:T(8,128)(2,1)S(1)} %copy.155.xt_ref, bf16[768,1024]{1,0:T(8,128)(2,1)S(1)} %copy-done.17, bf16[1024,768]{1,0:T(8,128)(2,1)S(1)} %copy-done.15, bf16[4,768,384]{2,1,0:T(8,128)(2,1)} %copy-done.9, ...), custom_call_target="tpu_custom_call" | custom-call | flops 6000000000 | bytes 3000000 | tf_op jit(solution)/shard_map/attend_back/pallas_call | solution.py:206
  208.5 4.1 %collective-permute-done.30 = bf16[2,4,144,384]{3,2,1,0:T(8,128)(2,1)S(1)} collective-permute-done((bf16[2,4,144,384]{3,2,1,0:T(8,128)(2,1)S(1)}, bf16[2,4,144,384]{3,2,1,0:T(8,128)(2,1)S(1)}, u32[]{:S(2)}, u32[]{:S(2)}) %collective-permute-start.30) | collective-permute-done | bytes 884768 | tf_op jit(solution)/shard_map/ppermute | solution.py:625
  214.4 6.1 %attend_back.7 = (bf16[1,768,384]{2,1,0:T(8,128)(2,1)S(1)}, bf16[1,1024,384]{2,1,0:T(8,128)(2,1)S(1)}) custom-call(bf16[768,1024]{1,0:T(8,128)(2,1)S(1)} %copy.155.xt_ref, bf16[768,1024]{1,0:T(8,128)(2,1)S(1)} %copy-done.17, bf16[1024,768]{1,0:T(8,128)(2,1)S(1)} %copy-done.15, bf16[4,768,384]{2,1,0:T(8,128)(2,1)} %copy-done.9, ...), custom_call_target="tpu_custom_call" | custom-call | flops 6000000000 | bytes 3000000 | tf_op jit(solution)/shard_map/attend_back/pallas_call | solution.py:206
  223.3 3.8 %collective-permute-start.35 = (bf16[144,384]{1,0:T(8,128)(2,1)S(1)}, bf16[144,384]{1,0:T(8,128)(2,1)S(1)}, u32[]{:S(2)}, u32[]{:S(2)}) collective-permute-start(bf16[144,384]{1,0:T(8,128)(2,1)S(1)} %get-tuple-element.239), channel_id=1, source_target_pairs={{0,24},{1,25},{2,26},{3,27},{4,28},{5,29},{6,30},{7,31},{8,0},{9,1... | collective-permute-start | bytes 331784 | tf_op jit(solution)/shard_map/ppermute | solution.py:625
  228.7 10.9 %first_back.1 = f32[40,768]{1,0:T(8,128)S(1)} custom-call(f32[1024,768]{1,0:T(8,128)} %copy-done.30, f32[1024,768]{1,0:T(8,128)} %copy-done.21, bf16[1024,32]{1,0:T(8,128)(2,1)S(1)} %copy.160.ident_ref, f32[3,768]{1,0:T(4,128)S(1)} %slice.207.gain_ref, bf16[4,1024,384]{2,1,0:T(8,128)(2,1)} %get-tuple-element.122.refs_0_, ...), custom_call_target="tpu_custom_call" | custom-call | flops 8000000000 | bytes 15000000 | tf_op jit(solution)/shard_map/first_back/pallas_call | solution.py:266
  243.6 3.6 %collective-permute-done.37 = f32[2,4,816]{2,0,1:T(2,128)S(1)} collective-permute-done((f32[2,4,816]{2,0,1:T(2,128)S(1)}, f32[2,4,816]{2,0,1:T(2,128)S(1)}, u32[]{:S(2)}, u32[]{:S(2)}) %collective-permute-start.37) | collective-permute-done | bytes 26144 | tf_op jit(solution)/shard_map/ppermute | solution.py:625
  253.3 3.8 %collective-permute-start.41 = (f32[816]{0:T(1024)S(1)}, f32[816]{0:T(1024)S(1)}, u32[]{:S(2)}, u32[]{:S(2)}) collective-permute-start(f32[816]{0:T(1024)S(1)} %get-tuple-element.187), channel_id=1, source_target_pairs={{0,24},{1,25},{2,26},{3,27},{4,28},{5,29},{6,30},{7,31},{8,0},{9,1... | collective-permute-start | bytes 9800 | tf_op jit(solution)/shard_map/ppermute | solution.py:625
  283.1 3.5 %collective-permute-start.51 = (f32[]{:T(128)}, f32[]{:T(128)}, u32[]{:S(2)}, u32[]{:S(2)}) collective-permute-start(f32[]{:T(128)} %add.522), channel_id=1, source_target_pairs={{0,16},{1,17},{2,18},{3,19},{4,20},{5,21},{6,22},{7,23},{8,24},{9,... | collective-permute-start | bytes 20 | tf_op jit(solution)/shard_map/ppermute | solution.py:625
  (352 shorter events, 116.4 us)
Async XLA Ops:
  4.6 10.5 %collective-permute-start.6 = (f32[1,840]{1,0:T(1,128)S(1)}, f32[1,840]{1,0:T(1,128)S(1)}, u32[]{:S(2)}, u32[]{:S(2)}) collective-permute-start(f32[1,840]{1,0:T(1,128)S(1)} %reshape.541), channel_id=1, source_target_pairs={{0,24},{1,25},{2,26},{3,27},{4,28},{5,29},{6,30},{7,31},{8,0},{9,1... | collective-permute-start | bytes 10088 | tf_op jit(solution)/shard_map/ppermute | solution.py:625
  10.7 7.1 %collective-permute-start.3 = (bf16[2,96,384]{2,1,0:T(8,128)(2,1)S(1)}, bf16[2,96,384]{2,1,0:T(8,128)(2,1)S(1)}, u32[]{:S(2)}, u32[]{:S(2)}) collective-permute-start(bf16[2,96,384]{2,1,0:T(8,128)(2,1)S(1)} %pad_maximum_fusion.11), channel_id=1, source_target_pairs={{0,24},{1,25},{2,26},{3,27},{4,28},{5,29},{6,30},{7,31},{8,0},{9,1... | collective-permute-start | bytes 442376 | tf_op jit(solution)/shard_map/ppermute | solution.py:625
  13.5 13.7 %collective-permute-start.2 = (bf16[2,96,384]{2,1,0:T(8,128)(2,1)S(1)}, bf16[2,96,384]{2,1,0:T(8,128)(2,1)S(1)}, u32[]{:S(2)}, u32[]{:S(2)}) collective-permute-start(bf16[2,96,384]{2,1,0:T(8,128)(2,1)S(1)} %pad_maximum_fusion.11), channel_id=1, source_target_pairs={{0,16},{1,17},{2,18},{3,19},{4,20},{5,21},{6,22},{7,23},{8,24},{9,... | collective-permute-start | bytes 442376 | tf_op jit(solution)/shard_map/ppermute | solution.py:625
  15.1 12.0 %collective-permute-start.1 = (bf16[2,96,384]{2,1,0:T(8,128)(2,1)S(1)}, bf16[2,96,384]{2,1,0:T(8,128)(2,1)S(1)}, u32[]{:S(2)}, u32[]{:S(2)}) collective-permute-start(bf16[2,96,384]{2,1,0:T(8,128)(2,1)S(1)} %pad_maximum_fusion.11), channel_id=1, source_target_pairs={{0,8},{1,9},{2,10},{3,11},{4,12},{5,13},{6,14},{7,15},{8,16},{9,17... | collective-permute-start | bytes 442376 | tf_op jit(solution)/shard_map/ppermute | solution.py:625
  27.3 9.9 %collective-permute-start.7 = (bf16[4,2,96,384]{3,2,1,0:T(8,128)(2,1)S(1)}, bf16[4,2,96,384]{3,2,1,0:T(8,128)(2,1)S(1)}, u32[]{:S(2)}, u32[]{:S(2)}) collective-permute-start(bf16[4,2,96,384]{3,2,1,0:T(8,128)(2,1)S(1)} %pad_maximum_fusion.3), channel_id=1, source_target_pairs={{0,4},{1,3},{2,6},{3,1},{4,0},{5,7},{6,2},{7,5},{8,12},{9,11},{10,... | collective-permute-start | bytes 1769480 | tf_op jit(solution)/shard_map/ppermute | solution.py:625
  30.1 8.3 %collective-permute-start.8 = (f32[4,1,840]{2,1,0:T(1,128)S(1)}, f32[4,1,840]{2,1,0:T(1,128)S(1)}, u32[]{:S(2)}, u32[]{:S(2)}) collective-permute-start(f32[4,1,840]{2,1,0:T(1,128)S(1)} %constant_dynamic-update-slice_fusion), channel_id=1, source_target_pairs={{0,4},{1,3},{2,6},{3,1},{4,0},{5,7},{6,2},{7,5},{8,12},{9,11},{10,... | collective-permute-start | bytes 40328 | tf_op jit(solution)/shard_map/ppermute | solution.py:625
  40.0 30.1 %collective-permute-start.9 = (bf16[2,4,2,96,384]{4,3,2,1,0:T(8,128)(2,1)}, bf16[2,4,2,96,384]{4,3,2,1,0:T(8,128)(2,1)}, u32[]{:S(2)}, u32[]{:S(2)}) collective-permute-start(bf16[2,4,2,96,384]{4,3,2,1,0:T(8,128)(2,1)} %pad_maximum_fusion.refs_0_), channel_id=1, source_target_pairs={{0,2},{1,5},{2,0},{3,7},{4,6},{5,1},{6,4},{7,3},{8,10},{9,13},{10,... | collective-permute-start | bytes 3538952 | tf_op jit(solution)/shard_map/ppermute | solution.py:625
  42.8 10.4 %collective-permute-start.14 = (bf16[2,24,768]{2,1,0:T(8,128)(2,1)S(1)}, bf16[2,24,768]{2,1,0:T(8,128)(2,1)S(1)}, u32[]{:S(2)}, u32[]{:S(2)}) collective-permute-start(bf16[2,24,768]{2,1,0:T(8,128)(2,1)S(1)} %pad_maximum_fusion.15), channel_id=1, source_target_pairs={{0,16},{1,17},{2,18},{3,19},{4,20},{5,21},{6,22},{7,23},{8,24},{9,... | collective-permute-start | bytes 221192 | tf_op jit(solution)/shard_map/ppermute | solution.py:625
  44.3 8.8 %collective-permute-start.13 = (bf16[2,24,768]{2,1,0:T(8,128)(2,1)S(1)}, bf16[2,24,768]{2,1,0:T(8,128)(2,1)S(1)}, u32[]{:S(2)}, u32[]{:S(2)}) collective-permute-start(bf16[2,24,768]{2,1,0:T(8,128)(2,1)S(1)} %pad_maximum_fusion.15), channel_id=1, source_target_pairs={{0,8},{1,9},{2,10},{3,11},{4,12},{5,13},{6,14},{7,15},{8,16},{9,17... | collective-permute-start | bytes 221192 | tf_op jit(solution)/shard_map/ppermute | solution.py:625
  44.3 8.9 %collective-permute-start.15 = (bf16[2,24,768]{2,1,0:T(8,128)(2,1)S(1)}, bf16[2,24,768]{2,1,0:T(8,128)(2,1)S(1)}, u32[]{:S(2)}, u32[]{:S(2)}) collective-permute-start(bf16[2,24,768]{2,1,0:T(8,128)(2,1)S(1)} %pad_maximum_fusion.15), channel_id=1, source_target_pairs={{0,24},{1,25},{2,26},{3,27},{4,28},{5,29},{6,30},{7,31},{8,0},{9,1... | collective-permute-start | bytes 221192 | tf_op jit(solution)/shard_map/ppermute | solution.py:625
  60.0 9.9 %collective-permute-start.17 = (bf16[2,4,2,24,768]{4,3,2,1,0:T(8,128)(2,1)S(1)}, bf16[2,4,2,24,768]{4,3,2,1,0:T(8,128)(2,1)S(1)}, u32[]{:S(2)}, u32[]{:S(2)}) collective-permute-start(bf16[2,4,2,24,768]{4,3,2,1,0:T(8,128)(2,1)S(1)} %pad_maximum_fusion.4), channel_id=1, source_target_pairs={{0,2},{1,5},{2,0},{3,7},{4,6},{5,1},{6,4},{7,3},{8,10},{9,13},{10,... | collective-permute-start | bytes 1769480 | tf_op jit(solution)/shard_map/ppermute | solution.py:625
  134.7 7.3 %collective-permute-start.26 = (bf16[2,4,8,2432]{3,2,1,0:T(8,128)(2,1)S(1)}, bf16[2,4,8,2432]{3,2,1,0:T(8,128)(2,1)}, u32[]{:S(2)}, u32[]{:S(2)}) collective-permute-start(bf16[2,4,8,2432]{3,2,1,0:T(8,128)(2,1)S(1)} %pad_maximum_fusion.8.a1_ref), channel_id=1, source_target_pairs={{0,1},{1,0},{2,3},{3,2},{4,5},{5,4},{6,7},{7,6},{8,9},{9,8},{10,11... | collective-permute-start | bytes 933896 | tf_op jit(solution)/shard_map/ppermute | solution.py:625
  180.5 16.9 %collective-permute-start.28 = (bf16[4,768,384]{2,1,0:T(8,128)(2,1)}, bf16[4,768,384]{2,1,0:T(8,128)(2,1)}, u32[]{:S(2)}, u32[]{:S(2)}) collective-permute-start(bf16[4,768,384]{2,1,0:T(8,128)(2,1)} %get-tuple-element.104), channel_id=1, source_target_pairs={{0,1},{1,0},{2,3},{3,2},{4,5},{5,4},{6,7},{7,6},{8,9},{9,8},{10,11... | collective-permute-start | bytes 7077896 | tf_op jit(solution)/shard_map/ppermute | solution.py:625
  183.1 14.1 %collective-permute-start.29 = (bf16[2,4,2,2,24,384]{5,4,1,3,2,0:T(8,128)(2,1)S(1)}, bf16[2,4,2,2,24,384]{5,4,1,3,2,0:T(8,128)(2,1)S(1)}, u32[]{:S(2)}, u32[]{:S(2)}) collective-permute-start(bf16[2,4,2,2,24,384]{5,4,1,3,2,0:T(8,128)(2,1)S(1)} %bitcast.353), channel_id=1, source_target_pairs={{0,1},{1,0},{2,3},{3,2},{4,5},{5,4},{6,7},{7,6},{8,9},{9,8},{10,11... | collective-permute-start | bytes 1769480 | tf_op jit(solution)/shard_map/ppermute | solution.py:625
  199.5 13.1 %collective-permute-start.30 = (bf16[2,4,144,384]{3,2,1,0:T(8,128)(2,1)S(1)}, bf16[2,4,144,384]{3,2,1,0:T(8,128)(2,1)S(1)}, u32[]{:S(2)}, u32[]{:S(2)}) collective-permute-start(bf16[2,4,144,384]{3,2,1,0:T(8,128)(2,1)S(1)} %pad_maximum_fusion.2), channel_id=1, source_target_pairs={{0,2},{1,5},{2,0},{3,7},{4,6},{5,1},{6,4},{7,3},{8,10},{9,13},{10,... | collective-permute-start | bytes 2654216 | tf_op jit(solution)/shard_map/ppermute | solution.py:625
  212.9 8.4 %collective-permute-start.31 = (bf16[4,144,384]{2,1,0:T(8,128)(2,1)S(1)}, bf16[4,144,384]{2,1,0:T(8,128)(2,1)S(1)}, u32[]{:S(2)}, u32[]{:S(2)}) collective-permute-start(bf16[4,144,384]{2,1,0:T(8,128)(2,1)S(1)} %fusion.5), channel_id=1, source_target_pairs={{0,4},{1,3},{2,6},{3,1},{4,0},{5,7},{6,2},{7,5},{8,12},{9,11},{10,... | collective-permute-start | bytes 1327112 | tf_op jit(solution)/shard_map/ppermute | solution.py:625
  223.3 16.3 %collective-permute-start.33 = (bf16[144,384]{1,0:T(8,128)(2,1)S(1)}, bf16[144,384]{1,0:T(8,128)(2,1)S(1)}, u32[]{:S(2)}, u32[]{:S(2)}) collective-permute-start(bf16[144,384]{1,0:T(8,128)(2,1)S(1)} %get-tuple-element.238), channel_id=1, source_target_pairs={{0,8},{1,9},{2,10},{3,11},{4,12},{5,13},{6,14},{7,15},{8,16},{9,17... | collective-permute-start | bytes 331784 | tf_op jit(solution)/shard_map/ppermute | solution.py:625
  223.3 16.2 %collective-permute-start.35 = (bf16[144,384]{1,0:T(8,128)(2,1)S(1)}, bf16[144,384]{1,0:T(8,128)(2,1)S(1)}, u32[]{:S(2)}, u32[]{:S(2)}) collective-permute-start(bf16[144,384]{1,0:T(8,128)(2,1)S(1)} %get-tuple-element.239), channel_id=1, source_target_pairs={{0,24},{1,25},{2,26},{3,27},{4,28},{5,29},{6,30},{7,31},{8,0},{9,1... | collective-permute-start | bytes 331784 | tf_op jit(solution)/shard_map/ppermute | solution.py:625
  227.2 12.4 %collective-permute-start.34 = (bf16[144,384]{1,0:T(8,128)(2,1)S(1)}, bf16[144,384]{1,0:T(8,128)(2,1)S(1)}, u32[]{:S(2)}, u32[]{:S(2)}) collective-permute-start(bf16[144,384]{1,0:T(8,128)(2,1)S(1)} %get-tuple-element.240), channel_id=1, source_target_pairs={{0,16},{1,17},{2,18},{3,19},{4,20},{5,21},{6,22},{7,23},{8,24},{9,... | collective-permute-start | bytes 331784 | tf_op jit(solution)/shard_map/ppermute | solution.py:625
  227.2 12.5 %collective-permute-start.32 = (bf16[2,4,96,384]{3,2,1,0:T(8,128)(2,1)S(1)}, bf16[2,4,96,384]{3,2,1,0:T(8,128)(2,1)S(1)}, u32[]{:S(2)}, u32[]{:S(2)}) collective-permute-start(bf16[2,4,96,384]{3,2,1,0:T(8,128)(2,1)S(1)} %pad_maximum_fusion.5), channel_id=1, source_target_pairs={{0,2},{1,5},{2,0},{3,7},{4,6},{5,1},{6,4},{7,3},{8,10},{9,13},{10,... | collective-permute-start | bytes 1769480 | tf_op jit(solution)/shard_map/ppermute | solution.py:625
  240.6 7.3 %collective-permute-start.42 = (bf16[4,96,384]{2,1,0:T(8,128)(2,1)S(1)}, bf16[4,96,384]{2,1,0:T(8,128)(2,1)S(1)}, u32[]{:S(2)}, u32[]{:S(2)}) collective-permute-start(bf16[4,96,384]{2,1,0:T(8,128)(2,1)S(1)} %fusion.13), channel_id=1, source_target_pairs={{0,4},{1,3},{2,6},{3,1},{4,0},{5,7},{6,2},{7,5},{8,12},{9,11},{10,... | collective-permute-start | bytes 884744 | tf_op jit(solution)/shard_map/ppermute | solution.py:625
  248.1 8.9 %collective-permute-start.43 = (bf16[96,384]{1,0:T(8,128)(2,1)S(1)}, bf16[96,384]{1,0:T(8,128)(2,1)S(1)}, u32[]{:S(2)}, u32[]{:S(2)}) collective-permute-start(bf16[96,384]{1,0:T(8,128)(2,1)S(1)} %get-tuple-element.243), channel_id=1, source_target_pairs={{0,8},{1,9},{2,10},{3,11},{4,12},{5,13},{6,14},{7,15},{8,16},{9,17... | collective-permute-start | bytes 221192 | tf_op jit(solution)/shard_map/ppermute | solution.py:625
  248.8 10.4 %collective-permute-start.45 = (bf16[96,384]{1,0:T(8,128)(2,1)S(1)}, bf16[96,384]{1,0:T(8,128)(2,1)S(1)}, u32[]{:S(2)}, u32[]{:S(2)}) collective-permute-start(bf16[96,384]{1,0:T(8,128)(2,1)S(1)} %get-tuple-element.244), channel_id=1, source_target_pairs={{0,24},{1,25},{2,26},{3,27},{4,28},{5,29},{6,30},{7,31},{8,0},{9,1... | collective-permute-start | bytes 221192 | tf_op jit(solution)/shard_map/ppermute | solution.py:625
  252.0 7.2 %collective-permute-start.44 = (bf16[96,384]{1,0:T(8,128)(2,1)S(1)}, bf16[96,384]{1,0:T(8,128)(2,1)S(1)}, u32[]{:S(2)}, u32[]{:S(2)}) collective-permute-start(bf16[96,384]{1,0:T(8,128)(2,1)S(1)} %get-tuple-element.245), channel_id=1, source_target_pairs={{0,16},{1,17},{2,18},{3,19},{4,20},{5,21},{6,22},{7,23},{8,24},{9,... | collective-permute-start | bytes 221192 | tf_op jit(solution)/shard_map/ppermute | solution.py:625
  (84 other events, 934.7 us)
